TPU v7x, 32 devices: a whole 2x2x4 slice. The times are simulated.
32 devices in a mesh: dp: 16 (over z, y, core), stream: 2 (over x).
Axes of the slice: x: 2, y: 2, z: 4, core: 2. Of those that a mesh axis runs over, the one named last changes fastest.
Arguments:
- main_rows: bfloat16 [10240, 1024], P(('dp', 'stream')), may hold values from -6 to 6
- pred_rows: bfloat16 [20480, 1024], P(('dp', 'stream')), may hold values from -6 to 6
- enc_rows: bfloat16 [10240, 1024], P(('dp', 'stream')), may hold values from -6 to 6
- doc_lengths: int32 [16, 8], P('dp'), may hold values from 1 to 512, as said below
- main_cotangent: bfloat16 [10240, 1024], P(('dp', 'stream')), may hold values from -6 to 6
- pred_cotangent: bfloat16 [20480, 1024], P(('dp', 'stream')), may hold values from -6 to 6
- proj_master: float32 [1024, 12800], P(None, ('dp', 'stream'))
- proj_first: float32 [1024, 12800], P(None, ('dp', 'stream')), may hold values from -56 to 56
- proj_second: float32 [1024, 12800], P(None, ('dp', 'stream')), may hold values from 7.68 to 30.72
- bias_master: float32 [10752], P(('dp', 'stream')), may hold values from -0.6 to 0.6
- bias_first: float32 [10752], P(('dp', 'stream')), may hold values from -56 to 56
- bias_second: float32 [10752], P(('dp', 'stream')), may hold values from 7.68 to 30.72
- down_master: float32 [4096, 1024], P(('dp', 'stream')), may hold values from -0.09375 to 0.09375
- down_first: float32 [4096, 1024], P(('dp', 'stream')), may hold values from -56 to 56
- down_second: float32 [4096, 1024], P(('dp', 'stream')), may hold values from 7.68 to 30.72
- small_master: float32 [7, 1024], replicated
- small_first: float32 [7, 1024], replicated, may hold values from -56 to 56
- small_second: float32 [7, 1024], replicated, may hold values from 7.68 to 30.72
Outputs:
- main_out: bfloat16 [10240, 1024], P(('dp', 'stream'))
- pred_out: bfloat16 [20480, 1024], P(('dp', 'stream'))
- main_grad: bfloat16 [10240, 1024], P(('dp', 'stream'))
- pred_grad: bfloat16 [20480, 1024], P(('dp', 'stream'))
- enc_grad: bfloat16 [10240, 1024], P(('dp', 'stream'))
- proj_new: float32 [1024, 12800], P(None, ('dp', 'stream'))
- proj_first_new: float32 [1024, 12800], P(None, ('dp', 'stream'))
- proj_second_new: float32 [1024, 12800], P(None, ('dp', 'stream'))
- bias_new: float32 [10752], P(('dp', 'stream'))
- bias_first_new: float32 [10752], P(('dp', 'stream'))
- bias_second_new: float32 [10752], P(('dp', 'stream'))
- down_new: float32 [4096, 1024], P(('dp', 'stream'))
- down_first_new: float32 [4096, 1024], P(('dp', 'stream'))
- down_second_new: float32 [4096, 1024], P(('dp', 'stream'))
- small_new: float32 [7, 1024], replicated
- small_first_new: float32 [7, 1024], replicated
- small_second_new: float32 [7, 1024], replicated
Inputs may be any that keep to these rules, and one draw needn't show every extreme that they name: `doc_lengths`: each row's 8 lengths sum to 640; the second length of every row is 512.
All inputs are finite; a program needn't handle non-finite values.
Results may differ from a plain program's by a relative error of at most 0.023.
Values may be sent and summed in bfloat16 or wider, within the bound.
A program may use at most 384 MiB of HBM per device.

v0:
```python
from functools import partial
import math

import jax
import jax.numpy as jnp
from jax import lax
from jax.sharding import PartitionSpec as P

D = 1024
HEADS = 16
BUCKETS = 32
STEP = 10
HEAD_DIM = 64


NORM_EPS = 1e-05
BETA_FIRST = 0.9
BETA_SECOND = 0.999
ADAM_EPS = 1e-08
RATE_MATRIX = 0.04
RATE_VECTOR = 0.15
RATE_SMALL = 0.5
WEIGHT_DECAY = 0.01
MASKED = -1e30
HEAD_GROUP = 4


def bucket_edges():
    return [int(math.ceil(16.0 * 8.0 ** (step_index / 16.0))) for step_index in range(1, 16)]


def bucket_of(distance):
    counted = jnp.zeros_like(distance)
    for threshold in bucket_edges():
        counted = counted + (distance >= threshold).astype(jnp.int32)
    return jnp.where(distance < 16, distance, 16 + counted)


def doc_ids(lengths, length_total):
    doc_ends = jnp.cumsum(lengths)
    places = jnp.arange(length_total, dtype=jnp.int32)
    return jnp.sum((places[:, None] >= doc_ends[None, :]).astype(jnp.int32), axis=1)


def layer_norm(hidden, gain_row, shift_row):
    centre = hidden - jnp.mean(hidden, axis=-1, keepdims=True)
    spread = jnp.mean(centre * centre, axis=-1, keepdims=True)
    return centre * lax.rsqrt(spread + NORM_EPS) * gain_row + shift_row


def matmul(left_side, right_side):
    return jnp.dot(left_side, right_side, preferred_element_type=jnp.float32)


def outer_sum(left_side, right_side):
    return lax.dot_general(
        left_side, right_side, (((0,), (0,)), ((), ())), preferred_element_type=jnp.float32
    )


def times_transpose(left_side, right_side):
    return lax.dot_general(
        left_side, right_side, (((1,), (1,)), ((), ())), preferred_element_type=jnp.float32
    )


def split_heads(matrix):
    row_count = matrix.shape[0]
    return matrix.reshape(row_count, HEADS // HEAD_GROUP, HEAD_GROUP, HEAD_DIM).transpose(
        1, 2, 0, 3
    )


def join_heads(stacked):
    row_count = stacked.shape[2]
    return stacked.transpose(2, 0, 1, 3).reshape(row_count, HEADS * HEAD_DIM)


def split_table(table):
    row_count = table.shape[0]
    return table.reshape(row_count, BUCKETS, HEADS // HEAD_GROUP, HEAD_GROUP).transpose(2, 3, 0, 1)


def join_table(stacked):
    row_count = stacked.shape[2]
    return stacked.transpose(2, 3, 0, 1).reshape(row_count, BUCKETS * HEADS)


def bucket_bias(table_heads, buckets):
    total = jnp.zeros(table_heads.shape[:2] + buckets.shape[1:], jnp.float32)
    for column in range(BUCKETS):
        total = total + jnp.where(
            buckets[None] == column, table_heads[:, :, column][:, :, None], 0.0
        )
    return total


def self_scores(query_heads, key_heads, table_heads, own_keys, buckets, allowed, main_flag):
    score_scale = HEAD_DIM ** (-0.5)
    raw_scores = (
        jnp.einsum("hqd,hkd->hqk", query_heads, key_heads, preferred_element_type=jnp.float32)
        * score_scale
    )
    scores = raw_scores + bucket_bias(table_heads, buckets)
    own_score = (
        jnp.sum(query_heads.astype(jnp.float32) * own_keys.astype(jnp.float32), axis=2)
        * score_scale
    )
    own_score = own_score + table_heads[:, :, 0]
    scores = jnp.where(allowed[None], scores, MASKED)
    own_score = jnp.where(main_flag[None], MASKED, own_score)
    return (scores, own_score)


def self_forward(pieces, buckets, allowed, main_flag):
    query_heads, key_heads, value_heads, table_heads, own_keys, own_values = pieces
    scores, own_score = self_scores(
        query_heads, key_heads, table_heads, own_keys, buckets, allowed, main_flag
    )
    row_top = jnp.maximum(jnp.max(scores, axis=2), own_score)
    weights = jnp.exp(scores - row_top[:, :, None])
    own_weight = jnp.exp(own_score - row_top)
    row_total = jnp.sum(weights, axis=2) + own_weight
    probabilities = (weights / row_total[:, :, None]).astype(jnp.bfloat16)
    own_prob = (own_weight / row_total).astype(jnp.bfloat16)
    context = jnp.einsum(
        "hqk,hkd->hqd", probabilities, value_heads, preferred_element_type=jnp.float32
    )
    context = context + own_prob.astype(jnp.float32)[:, :, None] * own_values.astype(jnp.float32)
    return (context, row_top + jnp.log(row_total))


def self_backward(pieces, buckets, allowed, main_flag, one_hot):
    (
        query_heads,
        key_heads,
        value_heads,
        table_heads,
        own_keys,
        own_values,
        log_total,
        context_grad,
    ) = pieces
    score_scale = HEAD_DIM ** (-0.5)
    scores, own_score = self_scores(
        query_heads, key_heads, table_heads, own_keys, buckets, allowed, main_flag
    )
    probs_full = jnp.exp(scores - log_total[:, :, None])
    own_full = jnp.exp(own_score - log_total)
    prob_grad = jnp.einsum(
        "hqd,hkd->hqk", context_grad, value_heads, preferred_element_type=jnp.float32
    )
    context_wide = context_grad.astype(jnp.float32)
    own_prob_grad = jnp.sum(context_wide * own_values.astype(jnp.float32), axis=2)
    row_dot = jnp.sum(probs_full * prob_grad, axis=2) + own_full * own_prob_grad
    score_grad = (probs_full * (prob_grad - row_dot[:, :, None])).astype(jnp.bfloat16)
    own_grad = (own_full * (own_prob_grad - row_dot)).astype(jnp.bfloat16)
    own_wide = own_grad.astype(jnp.float32)[:, :, None]
    query_grad = jnp.einsum(
        "hqk,hkd->hqd", score_grad, key_heads, preferred_element_type=jnp.float32
    )
    query_grad = (query_grad + own_wide * own_keys.astype(jnp.float32)) * score_scale
    key_grad = (
        jnp.einsum("hqk,hqd->hkd", score_grad, query_heads, preferred_element_type=jnp.float32)
        * score_scale
    )
    own_key_grad = own_wide * query_heads.astype(jnp.float32) * score_scale
    value_grad = jnp.einsum(
        "hqk,hqd->hkd",
        probs_full.astype(jnp.bfloat16),
        context_grad,
        preferred_element_type=jnp.float32,
    )
    own_value_grad = own_full.astype(jnp.bfloat16).astype(jnp.float32)[:, :, None] * context_wide
    table_grad = jnp.einsum("hqk,qkb->hqb", score_grad, one_hot, preferred_element_type=jnp.float32)
    table_grad = table_grad.at[:, :, 0].add(own_grad.astype(jnp.float32))
    return (query_grad, key_grad, value_grad, own_key_grad, own_value_grad, table_grad)


def cross_scores(query_heads, key_heads, same_doc):
    score_scale = HEAD_DIM ** (-0.5)
    raw_scores = (
        jnp.einsum("hqd,hkd->hqk", query_heads, key_heads, preferred_element_type=jnp.float32)
        * score_scale
    )
    return jnp.where(same_doc[None], raw_scores, MASKED)


def cross_forward(pieces, same_doc):
    query_heads, key_heads, value_heads = pieces
    scores = cross_scores(query_heads, key_heads, same_doc)
    row_top = jnp.max(scores, axis=2)
    weights = jnp.exp(scores - row_top[:, :, None])
    row_total = jnp.sum(weights, axis=2)
    probabilities = (weights / row_total[:, :, None]).astype(jnp.bfloat16)
    context = jnp.einsum(
        "hqk,hkd->hqd", probabilities, value_heads, preferred_element_type=jnp.float32
    )
    return (context, row_top + jnp.log(row_total))


def cross_backward(pieces, same_doc):
    query_heads, key_heads, value_heads, log_total, context_grad = pieces
    score_scale = HEAD_DIM ** (-0.5)
    scores = cross_scores(query_heads, key_heads, same_doc)
    probs_full = jnp.exp(scores - log_total[:, :, None])
    prob_grad = jnp.einsum(
        "hqd,hkd->hqk", context_grad, value_heads, preferred_element_type=jnp.float32
    )
    row_dot = jnp.sum(probs_full * prob_grad, axis=2)
    score_grad = (probs_full * (prob_grad - row_dot[:, :, None])).astype(jnp.bfloat16)
    query_grad = (
        jnp.einsum("hqk,hkd->hqd", score_grad, key_heads, preferred_element_type=jnp.float32)
        * score_scale
    )
    key_grad = (
        jnp.einsum("hqk,hqd->hkd", score_grad, query_heads, preferred_element_type=jnp.float32)
        * score_scale
    )
    value_grad = jnp.einsum(
        "hqk,hqd->hkd",
        probs_full.astype(jnp.bfloat16),
        context_grad,
        preferred_element_type=jnp.float32,
    )
    return (query_grad, key_grad, value_grad)


def adam_step(master, first_moment, second_moment, gradient, step_rate, step_decay):
    first_new = BETA_FIRST * first_moment + (1.0 - BETA_FIRST) * gradient
    second_new = BETA_SECOND * second_moment + (1.0 - BETA_SECOND) * gradient * gradient
    first_hat = first_new / (1.0 - BETA_FIRST**STEP)
    second_hat = second_new / (1.0 - BETA_SECOND**STEP)
    master_new = master - step_rate * (
        first_hat / (jnp.sqrt(second_hat) + ADAM_EPS) + step_decay * master
    )
    return (master_new, first_new, second_new)


def local(
    main_rows,
    pred_rows,
    enc_rows,
    doc_lengths,
    main_cotangent,
    pred_cotangent,
    proj_master,
    proj_first,
    proj_second,
    bias_master,
    bias_first,
    bias_second,
    down_master,
    down_first,
    down_second,
    small_master,
    small_first,
    small_second,
):
    proj_low = proj_master.astype(jnp.bfloat16)
    bias_low = bias_master.astype(jnp.bfloat16)
    down_low = down_master.astype(jnp.bfloat16)
    proj_weight, bias_weight, down_weight = (
        lax.all_gather(proj_low, ("dp", "stream"), axis=1, tiled=True),
        lax.all_gather(bias_low, ("dp", "stream"), axis=0, tiled=True),
        lax.all_gather(down_low, ("dp", "stream"), axis=0, tiled=True),
    )
    rel_width = BUCKETS * HEADS
    cross_start = 4 * D + rel_width
    self_weight = proj_weight[:, 0 : 3 * D]
    out_weight = proj_weight[:, 3 * D : 4 * D]
    table_weight = proj_weight[:, 4 * D : cross_start]
    cross_weight = proj_weight[:, cross_start : cross_start + D]
    pair_weight = proj_weight[:, cross_start + D : cross_start + 3 * D]
    back_weight = proj_weight[:, cross_start + 3 * D : cross_start + 4 * D]
    up_weight = proj_weight[:, cross_start + 4 * D :]
    bias_wide = bias_weight.astype(jnp.float32)
    query_bias = bias_wide[0:D]
    value_bias = bias_wide[D : 2 * D]
    out_bias = bias_wide[2 * D : 3 * D]
    table_bias = bias_wide[3 * D : 3 * D + rel_width]
    cross_bias = bias_wide[3 * D + rel_width : 4 * D + rel_width]
    pair_bias = bias_wide[4 * D + rel_width : 5 * D + rel_width]
    back_bias = bias_wide[5 * D + rel_width : 6 * D + rel_width]
    up_bias = bias_wide[6 * D + rel_width :]
    zero_bias = jnp.zeros((D,), jnp.float32)
    half_rows = main_rows.shape[0]
    group_rows = pred_rows.shape[0]
    main_start = lax.axis_index("stream") * half_rows
    places = jnp.arange(group_rows, dtype=jnp.int32)
    group_docs = doc_ids(doc_lengths[0], group_rows)
    query_docs = jnp.concatenate(
        [lax.dynamic_slice_in_dim(group_docs, main_start, half_rows), group_docs]
    )
    query_places = jnp.concatenate([main_start + jnp.arange(half_rows, dtype=jnp.int32), places])
    main_flag = jnp.arange(half_rows + group_rows, dtype=jnp.int32) < half_rows
    same_doc = query_docs[:, None] == group_docs[None, :]
    distance = query_places[:, None] - places[None, :]
    allowed = same_doc & ((distance > 0) | (distance == 0) & main_flag[:, None])
    buckets = bucket_of(jnp.maximum(distance, 0))
    inputs = jnp.concatenate([main_rows, pred_rows], axis=0)
    input_values = inputs.astype(jnp.float32)
    self_low = (
        matmul(inputs, self_weight) + jnp.concatenate([query_bias, zero_bias, value_bias])
    ).astype(jnp.bfloat16)
    query_rows = self_low[:, 0:D]
    key_rows = self_low[:, D : 2 * D]
    value_rows = self_low[:, 2 * D :]
    table = matmul(inputs, table_weight) + table_bias
    key_main, value_main = (
        lax.all_gather(key_rows[:half_rows], "stream", axis=0, tiled=True),
        lax.all_gather(value_rows[:half_rows], "stream", axis=0, tiled=True),
    )
    pair_low = (matmul(enc_rows, pair_weight) + jnp.concatenate([zero_bias, pair_bias])).astype(
        jnp.bfloat16
    )
    cross_keys, cross_values = (
        lax.all_gather(pair_low[:, 0:D], "stream", axis=0, tiled=True),
        lax.all_gather(pair_low[:, D:], "stream", axis=0, tiled=True),
    )
    self_pieces = (
        split_heads(query_rows),
        split_heads(key_main),
        split_heads(value_main),
        split_table(table),
        split_heads(key_rows),
        split_heads(value_rows),
    )
    context_stack, self_log = lax.map(
        partial(self_forward, buckets=buckets, allowed=allowed, main_flag=main_flag), self_pieces
    )
    context_low = join_heads(context_stack).astype(jnp.bfloat16)
    attn_out = matmul(context_low, out_weight) + out_bias
    norm_one_in = input_values + attn_out
    hidden_one = layer_norm(norm_one_in, small_master[1], small_master[4])
    one_low = hidden_one.astype(jnp.bfloat16)
    cross_query = (matmul(one_low, cross_weight) + cross_bias).astype(jnp.bfloat16)
    cross_pieces = (split_heads(cross_query), split_heads(cross_keys), split_heads(cross_values))
    cross_stack, cross_log = lax.map(partial(cross_forward, same_doc=same_doc), cross_pieces)
    cross_context_low = join_heads(cross_stack).astype(jnp.bfloat16)
    cross_out = matmul(cross_context_low, back_weight) + back_bias
    norm_two_in = hidden_one + cross_out
    hidden_two = layer_norm(norm_two_in, small_master[2], small_master[5])
    two_low = hidden_two.astype(jnp.bfloat16)
    pre_act = matmul(two_low, up_weight) + up_bias
    activated = jax.nn.gelu(pre_act, approximate=False).astype(jnp.bfloat16)
    ffn_out = matmul(activated, down_weight) + small_master[0]
    norm_three_in = hidden_two + ffn_out
    final_rows = layer_norm(norm_three_in, small_master[3], small_master[6])
    cotangent = jnp.concatenate([main_cotangent, pred_cotangent], axis=0).astype(jnp.float32)
    unused, norm_three = jax.vjp(layer_norm, norm_three_in, small_master[3], small_master[6])
    sum_three, gain_three, shift_three = norm_three(cotangent)
    ffn_grad = sum_three.astype(jnp.bfloat16)
    down_grad = outer_sum(activated, ffn_grad)
    act_grad = times_transpose(ffn_grad, down_weight)
    unused, gelu_back = jax.vjp(partial(jax.nn.gelu, approximate=False), pre_act)
    pre_grad = gelu_back(act_grad)[0].astype(jnp.bfloat16)
    up_grad = outer_sum(two_low, pre_grad)
    two_grad = sum_three + times_transpose(pre_grad, up_weight)
    unused, norm_two = jax.vjp(layer_norm, norm_two_in, small_master[2], small_master[5])
    sum_two, gain_two, shift_two = norm_two(two_grad)
    branch_grad = sum_two.astype(jnp.bfloat16)
    back_grad = outer_sum(cross_context_low, branch_grad)
    cross_context_grad = times_transpose(branch_grad, back_weight).astype(jnp.bfloat16)
    cquery_stack, ckey_stack, cvalue_stack = lax.map(
        partial(cross_backward, same_doc=same_doc),
        (
            split_heads(cross_query),
            split_heads(cross_keys),
            split_heads(cross_values),
            cross_log,
            split_heads(cross_context_grad),
        ),
    )
    ckey_grad, cvalue_grad = (
        lax.psum_scatter(
            join_heads(ckey_stack).astype(jnp.bfloat16), "stream", scatter_dimension=0, tiled=True
        ).astype(jnp.float32),
        lax.psum_scatter(
            join_heads(cvalue_stack).astype(jnp.bfloat16), "stream", scatter_dimension=0, tiled=True
        ).astype(jnp.float32),
    )
    pair_grad = jnp.concatenate([ckey_grad, cvalue_grad], axis=1).astype(jnp.bfloat16)
    pair_weight_grad = outer_sum(enc_rows, pair_grad)
    enc_grad = times_transpose(pair_grad, pair_weight).astype(jnp.bfloat16)
    cquery_grad = join_heads(cquery_stack).astype(jnp.bfloat16)
    cross_weight_grad = outer_sum(one_low, cquery_grad)
    one_grad = sum_two + times_transpose(cquery_grad, cross_weight)
    unused, norm_one = jax.vjp(layer_norm, norm_one_in, small_master[1], small_master[4])
    sum_one, gain_one, shift_one = norm_one(one_grad)
    attn_grad = sum_one.astype(jnp.bfloat16)
    out_grad = outer_sum(context_low, attn_grad)
    context_grad = times_transpose(attn_grad, out_weight).astype(jnp.bfloat16)
    one_hot = (buckets[:, :, None] == jnp.arange(BUCKETS, dtype=jnp.int32)[None, None, :]).astype(
        jnp.bfloat16
    )
    back_pieces = (
        split_heads(query_rows),
        split_heads(key_main),
        split_heads(value_main),
        split_table(table),
        split_heads(key_rows),
        split_heads(value_rows),
        self_log,
        split_heads(context_grad),
    )
    query_stack, key_stack, value_stack, own_key_stack, own_value_stack, table_stack = lax.map(
        partial(
            self_backward, buckets=buckets, allowed=allowed, main_flag=main_flag, one_hot=one_hot
        ),
        back_pieces,
    )
    key_main_grad, value_main_grad = (
        lax.psum_scatter(
            join_heads(key_stack).astype(jnp.bfloat16), "stream", scatter_dimension=0, tiled=True
        ).astype(jnp.float32),
        lax.psum_scatter(
            join_heads(value_stack).astype(jnp.bfloat16), "stream", scatter_dimension=0, tiled=True
        ).astype(jnp.float32),
    )
    key_grad = jnp.concatenate([key_main_grad, join_heads(own_key_stack)[half_rows:]], axis=0)
    value_grad = jnp.concatenate([value_main_grad, join_heads(own_value_stack)[half_rows:]], axis=0)
    self_grad = jnp.concatenate([join_heads(query_stack), key_grad, value_grad], axis=1).astype(
        jnp.bfloat16
    )
    table_grad = join_table(table_stack).astype(jnp.bfloat16)
    self_weight_grad = outer_sum(inputs, self_grad)
    table_weight_grad = outer_sum(inputs, table_grad)
    input_grad = (
        sum_one
        + times_transpose(self_grad, self_weight)
        + times_transpose(table_grad, table_weight)
    )
    self_sums = jnp.sum(self_grad, axis=0, dtype=jnp.float32)
    proj_grad_full = jnp.concatenate(
        [
            self_weight_grad,
            out_grad,
            table_weight_grad,
            cross_weight_grad,
            pair_weight_grad,
            back_grad,
            up_grad,
        ],
        axis=1,
    )
    bias_grad_full = jnp.concatenate(
        [
            self_sums[0:D],
            self_sums[2 * D :],
            jnp.sum(attn_grad, axis=0, dtype=jnp.float32),
            jnp.sum(table_grad, axis=0, dtype=jnp.float32),
            jnp.sum(cquery_grad, axis=0, dtype=jnp.float32),
            jnp.sum(pair_grad[:, D:], axis=0, dtype=jnp.float32),
            jnp.sum(branch_grad, axis=0, dtype=jnp.float32),
            jnp.sum(pre_grad, axis=0, dtype=jnp.float32),
        ]
    )
    small_stack = jnp.stack(
        [
            jnp.sum(ffn_grad, axis=0, dtype=jnp.float32),
            gain_one,
            gain_two,
            gain_three,
            shift_one,
            shift_two,
            shift_three,
        ]
    )
    proj_grad, bias_grad, down_shard_grad = (
        lax.psum_scatter(proj_grad_full, ("dp", "stream"), scatter_dimension=1, tiled=True),
        lax.psum_scatter(bias_grad_full, ("dp", "stream"), scatter_dimension=0, tiled=True),
        lax.psum_scatter(down_grad, ("dp", "stream"), scatter_dimension=0, tiled=True),
    )
    small_grad = lax.psum(small_stack, ("dp", "stream"))
    proj_new, proj_first_new, proj_second_new = adam_step(
        proj_master, proj_first, proj_second, proj_grad, RATE_MATRIX, WEIGHT_DECAY
    )
    bias_new, bias_first_new, bias_second_new = adam_step(
        bias_master, bias_first, bias_second, bias_grad, RATE_VECTOR, 0.0
    )
    down_new, down_first_new, down_second_new = adam_step(
        down_master, down_first, down_second, down_shard_grad, RATE_MATRIX, WEIGHT_DECAY
    )
    small_new, small_first_new, small_second_new = adam_step(
        small_master, small_first, small_second, small_grad, RATE_SMALL, 0.0
    )
    return (
        final_rows[:half_rows].astype(jnp.bfloat16),
        final_rows[half_rows:].astype(jnp.bfloat16),
        input_grad[:half_rows].astype(jnp.bfloat16),
        input_grad[half_rows:].astype(jnp.bfloat16),
        enc_grad,
        proj_new,
        proj_first_new,
        proj_second_new,
        bias_new,
        bias_first_new,
        bias_second_new,
        down_new,
        down_first_new,
        down_second_new,
        small_new,
        small_first_new,
        small_second_new,
    )


def solution(mesh):
    placed = (
        P(("dp", "stream"), None),
        P(("dp", "stream"), None),
        P(("dp", "stream"), None),
        P("dp", None),
        P(("dp", "stream"), None),
        P(("dp", "stream"), None),
        P(None, ("dp", "stream")),
        P(None, ("dp", "stream")),
        P(None, ("dp", "stream")),
        P(("dp", "stream")),
        P(("dp", "stream")),
        P(("dp", "stream")),
        P(("dp", "stream"), None),
        P(("dp", "stream"), None),
        P(("dp", "stream"), None),
        P(),
        P(),
        P(),
    )
    return jax.shard_map(
        local,
        mesh=mesh,
        in_specs=placed,
        out_specs=(
            P(("dp", "stream"), None),
            P(("dp", "stream"), None),
            P(("dp", "stream"), None),
            P(("dp", "stream"), None),
            P(("dp", "stream"), None),
            P(None, ("dp", "stream")),
            P(None, ("dp", "stream")),
            P(None, ("dp", "stream")),
            P(("dp", "stream")),
            P(("dp", "stream")),
            P(("dp", "stream")),
            P(("dp", "stream"), None),
            P(("dp", "stream"), None),
            P(("dp", "stream"), None),
            P(),
            P(),
            P(),
        ),
        check_vma=False,
    )
```

profile of v0, /device:TPU:11, one launch (start us, length us, event | category | flops | bytes accessed | tf_op | source)
XLA Modules:
  0.0 3099.2 jit_solution(14651663903076168027)
XLA Ops:
  10.8 41.5 %all-reduce.1 = bf16[10752]{0:T(1024)(128)(2,1)S(1)} all-reduce(bf16[10752]{0:T(1024)(128)(2,1)S(1)} %dynamic-update-slice.7), channel_id=1, replica_groups=mesh['dp'=16,'stream'=2] {'dp','stream'}, use_global_device_ids=true, to_apply=%add.1 | all-reduce | flops 10752 | bytes 43008
  56.1 115.8 %all-gather.7.cloned.1.call-done = bf16[1024,12800]{0,1:T(8,128)(2,1)} async-done(((bf16[1024,400]{0,1:T(8,128)(2,1)}), bf16[1024,12800]{0,1:T(8,128)(2,1)}) %all-gather.7.cloned.1.call-update) | async-done | bytes 26214416 | tf_op jit(solution)/shard_map/all_gather | solution.py:264
  171.9 9.0 add_convert_fusion.1
  238.5 304.3 %while.71 = (s32[]{:T(128)}, bf16[4,4,960,64]{2,3,1,0:T(8,128)(2,1)}, f32[4,4,960]{2,1,0:T(4,128)S(1)}, bf16[4,4,960,64]{2,3,1,0:T(8,128)(2,1)S(1)}, bf16[4,4,64...) while((s32[]{:T(128)}, ...), condition=%wide.region_6.7_spmd.clone.clone.clone, body=%wide.region_2.6_spmd.clone.clone.clone.sunk | while | flops 861320640 | bytes 92358680 | solution.py:329
  241.0 17.2 fusion.439
  258.3 49.3 %fusion.440 = (f32[4,960]{1,0:T(4,128)S(1)}, f32[4,960,640]{2,1,0:T(8,128)S(1)}) fusion(f32[4,960]{1,0:T(4,128)S(1)} %get-tuple-element.1780, pred[960,640]{1,0:T(8,128)(4,1)} %get-tuple-element.1781, f32[4,960]{1,0:T(4,128)S(1)} %get-tuple-element.1782, pred[960,640]{1,0:T(8,128)(4,1)} %get-tuple-element.1783, ...), kind=kOutput, calls=%fused_computation.513.clone.3 | convolution fusion | flops 479228160 | bytes 31498240 | tf_op jit(solution)/shard_map/while/body/eval_jaxpr/hqd,hkd->hqk/dot_general | solution.py:101
  317.0 17.2 fusion.439
  334.2 49.3 %fusion.440 = (f32[4,960]{1,0:T(4,128)S(1)}, f32[4,960,640]{2,1,0:T(8,128)S(1)}) fusion(f32[4,960]{1,0:T(4,128)S(1)} %get-tuple-element.1780, pred[960,640]{1,0:T(8,128)(4,1)} %get-tuple-element.1781, f32[4,960]{1,0:T(4,128)S(1)} %get-tuple-element.1782, pred[960,640]{1,0:T(8,128)(4,1)} %get-tuple-element.1783, ...), kind=kOutput, calls=%fused_computation.513.clone.3 | convolution fusion | flops 479228160 | bytes 31498240 | tf_op jit(solution)/shard_map/while/body/eval_jaxpr/hqd,hkd->hqk/dot_general | solution.py:101
  393.0 17.2 fusion.439
  410.2 49.3 %fusion.440 = (f32[4,960]{1,0:T(4,128)S(1)}, f32[4,960,640]{2,1,0:T(8,128)S(1)}) fusion(f32[4,960]{1,0:T(4,128)S(1)} %get-tuple-element.1780, pred[960,640]{1,0:T(8,128)(4,1)} %get-tuple-element.1781, f32[4,960]{1,0:T(4,128)S(1)} %get-tuple-element.1782, pred[960,640]{1,0:T(8,128)(4,1)} %get-tuple-element.1783, ...), kind=kOutput, calls=%fused_computation.513.clone.3 | convolution fusion | flops 479228160 | bytes 31498240 | tf_op jit(solution)/shard_map/while/body/eval_jaxpr/hqd,hkd->hqk/dot_general | solution.py:101
  469.0 17.2 fusion.439
  486.2 49.3 %fusion.440 = (f32[4,960]{1,0:T(4,128)S(1)}, f32[4,960,640]{2,1,0:T(8,128)S(1)}) fusion(f32[4,960]{1,0:T(4,128)S(1)} %get-tuple-element.1780, pred[960,640]{1,0:T(8,128)(4,1)} %get-tuple-element.1781, f32[4,960]{1,0:T(4,128)S(1)} %get-tuple-element.1782, pred[960,640]{1,0:T(8,128)(4,1)} %get-tuple-element.1783, ...), kind=kOutput, calls=%fused_computation.513.clone.3 | convolution fusion | flops 479228160 | bytes 31498240 | tf_op jit(solution)/shard_map/while/body/eval_jaxpr/hqd,hkd->hqk/dot_general | solution.py:101
  565.5 51.2 %while.68 = (s32[]{:T(128)}, bf16[4,4,960,64]{2,3,1,0:T(8,128)(2,1)}, f32[4,4,960]{2,1,0:T(4,128)S(1)}, bf16[4,4,960,64]{2,3,1,0:T(8,128)(2,1)S(1)}, bf16[4,4,64...) while((s32[]{:T(128)}, ...), condition=%wide.region_12.13_spmd.clone, body=%wide.region_9.12_spmd.clone.sunk | while | flops 659247360 | bytes 50042272 | solution.py:339
  616.7 7.5 fusion.327
  626.2 48.2 %multiply_convert_fusion.2 = (bf16[960,4096]{1,0:T(8,128)(2,1)}, f32[960,4096]{1,0:T(8,128)}, f32[960,4096]{1,0:T(8,128)}) fusion(f32[4096]{0:T(1024)S(1)} %copy-done.90, bf16[1024,12800]{0,1:T(8,128)(2,1)} %all-gather.7.cloned.1.call-done, f32[960,1024]{1,0:T(8,128)S(1)} %get-tuple-element.1233, f32[1024]{0:T(1024)S(1)} %bitcast.675, ...), kind=kOutput, calls=%fused_computation.348 | convolution fusion | flops 8317501440 | bytes 51674624 | tf_op jit(solution)/shard_map/dot_general | solution.py:52
  674.4 14.4 fusion.328
  700.2 23.6 convert_reduce_fusion
  723.8 17.0 multiply_reduce_fusion.2
  758.5 83.2 %while.69 = (s32[]{:T(128)}, bf16[4,4,960,64]{2,3,1,0:T(8,128)(2,1)}, bf16[4,4,640,64]{2,3,1,0:T(8,128)(2,1)}, bf16[4,4,640,64]{2,3,1,0:T(8,128)(2,1)}, bf16[4,4...) while((s32[]{:T(128)}, ...), condition=%wide.region_23.24_spmd.clone, body=%wide.region_21.23_spmd.clone.sunk | while | flops 1610748160 | bytes 126310992 | solution.py:365
  844.5 8.0 multiply_reduce_fusion.3
  872.2 531.5 %while.70 = (s32[]{:T(128)}, bf16[4,4,960,64]{2,3,1,0:T(8,128)(2,1)}, bf16[4,4,640,64]{2,3,1,0:T(8,128)(2,1)}, bf16[4,4,640,64]{2,3,1,0:T(8,128)(2,1)}, bf16[4,4...) while((s32[]{:T(128)}, ...), condition=%wide.region_30.31_spmd.clone.clone, body=%wide.region_26.30_spmd.clone.clone.sunk | while | flops 2006722304 | bytes 195811552 | solution.py:407
  882.1 19.4 fusion.431
  901.5 53.4 %multiply_reduce_fusion.12 = (f32[4,960]{1,0:T(4,128)S(1)}, f32[4,960,640]{2,1,0:T(8,128)S(1)}) fusion(f32[4,960,640]{2,1,0:T(8,128)S(1)} %fusion.429, f32[4,960]{1,0:T(4,128)} %dynamic-slice_bitcast_fusion.9, f32[4,960]{1,0:T(4,128)S(1)} %get-tuple-element.1695, pred[960,640]{1,0:T(8,128)(4,1)} %get-tuple-element.1696, ...), kind=kOutput, calls=%fused_computation.74.clone.3 | convolution fusion | flops 484143360 | bytes 41331712 | tf_op jit(solution)/shard_map/while/body/eval_jaxpr/hqd,hkd->hqk/dot_general | solution.py:101
  962.5 13.4 fusion.433
  984.0 16.2 scatter-add.8
  1014.9 19.4 fusion.431
  1034.3 53.4 %multiply_reduce_fusion.12 = (f32[4,960]{1,0:T(4,128)S(1)}, f32[4,960,640]{2,1,0:T(8,128)S(1)}) fusion(f32[4,960,640]{2,1,0:T(8,128)S(1)} %fusion.429, f32[4,960]{1,0:T(4,128)} %dynamic-slice_bitcast_fusion.9, f32[4,960]{1,0:T(4,128)S(1)} %get-tuple-element.1695, pred[960,640]{1,0:T(8,128)(4,1)} %get-tuple-element.1696, ...), kind=kOutput, calls=%fused_computation.74.clone.3 | convolution fusion | flops 484143360 | bytes 41331712 | tf_op jit(solution)/shard_map/while/body/eval_jaxpr/hqd,hkd->hqk/dot_general | solution.py:101
  1095.3 13.4 fusion.433
  1116.8 16.2 scatter-add.8
  1147.6 19.4 fusion.431
  1167.0 53.4 %multiply_reduce_fusion.12 = (f32[4,960]{1,0:T(4,128)S(1)}, f32[4,960,640]{2,1,0:T(8,128)S(1)}) fusion(f32[4,960,640]{2,1,0:T(8,128)S(1)} %fusion.429, f32[4,960]{1,0:T(4,128)} %dynamic-slice_bitcast_fusion.9, f32[4,960]{1,0:T(4,128)S(1)} %get-tuple-element.1695, pred[960,640]{1,0:T(8,128)(4,1)} %get-tuple-element.1696, ...), kind=kOutput, calls=%fused_computation.74.clone.3 | convolution fusion | flops 484143360 | bytes 41331712 | tf_op jit(solution)/shard_map/while/body/eval_jaxpr/hqd,hkd->hqk/dot_general | solution.py:101
  1228.0 13.4 fusion.433
  1249.5 16.2 scatter-add.8
  1280.3 19.4 fusion.431
  1299.7 53.4 %multiply_reduce_fusion.12 = (f32[4,960]{1,0:T(4,128)S(1)}, f32[4,960,640]{2,1,0:T(8,128)S(1)}) fusion(f32[4,960,640]{2,1,0:T(8,128)S(1)} %fusion.429, f32[4,960]{1,0:T(4,128)} %dynamic-slice_bitcast_fusion.9, f32[4,960]{1,0:T(4,128)S(1)} %get-tuple-element.1695, pred[960,640]{1,0:T(8,128)(4,1)} %get-tuple-element.1696, ...), kind=kOutput, calls=%fused_computation.74.clone.3 | convolution fusion | flops 484143360 | bytes 41331712 | tf_op jit(solution)/shard_map/while/body/eval_jaxpr/hqd,hkd->hqk/dot_general | solution.py:101
  1360.7 13.4 fusion.433
  1382.2 16.2 scatter-add.8
  1432.0 23.8 reduce-scatter.21.cloned.1.call-done
  1458.0 14.4 convert_reduce_fusion.1
  1481.0 15.4 fusion.329
  1496.5 7.1 copy.323
  1514.9 9.2 copy.328
  1524.1 18.6 convolution_dynamic-update-slice_fusion.1
  1565.9 12.7 convolution_dynamic-update-slice_fusion
  1578.6 51.7 %copy.349 = f32[1024,12800]{0,1:T(8,128)} copy(f32[1024,12800]{1,0:T(8,128)} %convolution_dynamic-update-slice_fusion) | data formatting | bytes 104857600
  1642.6 10.6 fusion.241
  1665.6 307.0 %reduce-scatter.17.cloned.1.call-done = f32[128,1024]{1,0:T(8,128)} async-done(((f32[4096,1024]{1,0:T(8,128)}), f32[128,1024]{1,0:T(8,128)}) %reduce-scatter.17.cloned.1.call-update) | async-done | bytes 524304 | tf_op jit(solution)/shard_map/reduce_scatter | solution.py:473
  1975.6 1100.0 %reduce-scatter.27.cloned.1.call-done = f32[400,1024]{1,0:T(8,128)} async-done(((f32[12800,1024]{1,0:T(8,128)}), f32[400,1024]{1,0:T(8,128)}) %reduce-scatter.27.cloned.1.call-update) | async-done | bytes 1638416
  (668 shorter events, 550.0 us)
Async XLA Ops:
  7.2 178.3 %copy-start = (bf16[320,1024]{1,0:T(8,128)(2,1)S(1)}, bf16[320,1024]{1,0:T(8,128)(2,1)}, u32[]{:S(2)}) copy-start(bf16[320,1024]{1,0:T(8,128)(2,1)} %param.30) | copy-start | bytes 1966084
  7.2 47.8 %copy-start.58 = (bf16[640,1024]{1,0:T(8,128)(2,1)S(1)}, bf16[640,1024]{1,0:T(8,128)(2,1)}, u32[]{:S(2)}) copy-start(bf16[640,1024]{1,0:T(8,128)(2,1)} %param.29) | copy-start | bytes 3932164
  7.2 164.7 %all-gather.7.cloned.1.call-start = ((), (), s32[]{:S(2)}) async-start(), calls=%async_computation.6 | async-start | bytes 27033600 | tf_op jit(solution)/shard_map/all_gather | solution.py:264
  9.9 215.6 %all-gather.11.cloned.1.call-start = ((), (), s32[]{:S(2)}) async-start(), calls=%async_computation.8 | async-start | bytes 1966080 | tf_op jit(solution)/shard_map/all_gather | solution.py:312
  184.7 49.8 %all-gather.9.cloned.1.call-start = ((), (), s32[]{:S(2)}) async-start(), calls=%async_computation.7 | async-start | bytes 1966080 | tf_op jit(solution)/shard_map/all_gather | solution.py:311
  185.4 373.5 %all-gather.15.cloned.1.call-start = ((), (), s32[]{:S(2)}) async-start(), calls=%async_computation.10 | async-start | bytes 1966080 | tf_op jit(solution)/shard_map/all_gather | solution.py:319
  190.5 370.9 %all-gather.13.cloned.1.call-start = ((), (), s32[]{:S(2)}) async-start(), calls=%async_computation.9 | async-start | bytes 1966080 | tf_op jit(solution)/shard_map/all_gather | solution.py:318
  191.0 483.4 %all-gather.17.cloned.1.call-start = ((), (), s32[]{:S(2)}) async-start(), calls=%async_computation.11 | async-start | bytes 8650752 | tf_op jit(solution)/shard_map/all_gather | solution.py:266
  191.9 1230.5 %reduce-scatter.25.cloned.1.call-start = ((), (), s32[]{:S(2)}) async-start(), calls=%async_computation.16 | async-start | bytes 1966080
  238.5 304.4 %copy-start.104 = (f32[1024]{0:T(1024)S(1)}, f32[1024]{0:T(1024)}, u32[]{:S(2)}) copy-start(f32[1024]{0:T(1024)} %get-tuple-element.1229) | copy-start | bytes 12292
  549.0 67.7 %copy-start.67 = (f32[960]{0:T(1024)}, f32[960]{0:T(1024)S(1)}, u32[]{:S(2)}) copy-start(f32[960]{0:T(1024)S(1)} %broadcast_multiply_fusion.2) | copy-start | bytes 11524
  549.5 67.1 %copy-start.84 = (f32[960]{0:T(1024)}, f32[960]{0:T(1024)S(1)}, u32[]{:S(2)}) copy-start(f32[960]{0:T(1024)S(1)} %fusion.299) | copy-start | bytes 11524
  565.5 51.2 %copy-start.102 = (f32[1024]{0:T(1024)S(1)}, f32[1024]{0:T(1024)}, u32[]{:S(2)}) copy-start(f32[1024]{0:T(1024)} %get-tuple-element.1226) | copy-start | bytes 12292
  624.3 116.6 %copy-start.70 = (f32[960]{0:T(1024)}, f32[960]{0:T(1024)S(1)}, u32[]{:S(2)}) copy-start(f32[960]{0:T(1024)S(1)} %broadcast_multiply_fusion.1) | copy-start | bytes 11524
  625.4 115.4 %copy-start.87 = (f32[960]{0:T(1024)}, f32[960]{0:T(1024)S(1)}, u32[]{:S(2)}) copy-start(f32[960]{0:T(1024)S(1)} %fusion.300) | copy-start | bytes 11524
  626.2 48.3 %copy-start.101 = (f32[1,1024]{1,0:T(1,128)S(1)}, f32[1,1024]{1,0:T(1,128)}, u32[]{:S(2)}) copy-start(f32[1,1024]{1,0:T(1,128)} %get-tuple-element.1218) | copy-start | bytes 12292
  700.2 23.7 copy-start.53
  723.8 17.0 copy-start.77
  723.8 17.0 copy-start.14
  844.4 585.3 %reduce-scatter.19.cloned.1.call-start = ((), (), s32[]{:S(2)}) async-start(), calls=%async_computation.13 | async-start | bytes 1966080
  872.4 9.7 copy-start.2
  1005.2 9.7 copy-start.2
  1137.9 9.7 copy-start.2
  1270.7 9.7 copy-start.2
  1406.3 49.4 %reduce-scatter.21.cloned.1.call-start = ((), (), s32[]{:S(2)}) async-start(), calls=%async_computation.14 | async-start | bytes 1966080
  1409.0 96.9 %reduce-scatter.23.cloned.1.call-start = ((), (), s32[]{:S(2)}) async-start(), calls=%async_computation.15 | async-start | bytes 1966080
  1411.5 251.2 %all-reduce.6.cloned.1.call-start = ((), (), s32[]{:S(2)}) async-start(), calls=%async_computation.18 | async-start | bytes 155648
  1412.0 9.7 copy-start.93
  1412.0 9.7 copy-start.94
  1412.0 9.7 copy-start.95
  1412.0 9.7 copy-start.105
  1412.0 9.7 copy-start.106
  1412.0 9.7 copy-start.107
  1412.0 9.7 copy-start.108
  1418.4 39.6 %copy-start.20 = (bf16[4,4,960,64]{2,3,1,0:T(8,128)(2,1)S(1)}, bf16[4,4,960,64]{2,3,1,0:T(8,128)(2,1)}, u32[]{:S(2)}) copy-start(bf16[4,4,960,64]{2,3,1,0:T(8,128)(2,1)} %get-tuple-element.430) | copy-start | bytes 5898244
  1432.0 41.6 %copy-start.92 = (f32[1024]{0:T(1024)S(1)}, f32[1024]{0:T(1024)}, u32[]{:S(2)}) copy-start(f32[1024]{0:T(1024)} %get-tuple-element.1054) | copy-start | bytes 12292
  1458.0 20.3 copy-start.91
  1458.0 21.6 copy-start.89
  1480.9 491.7 %reduce-scatter.17.cloned.1.call-start = ((), (), s32[]{:S(2)}) async-start(), calls=%async_computation.12 | async-start | bytes 17301504 | tf_op jit(solution)/shard_map/reduce_scatter | solution.py:473
  1496.4 1579.2 %reduce-scatter.27.cloned.1.call-start = ((), (), s32[]{:S(2)}) async-start(), calls=%async_computation.17 | async-start | bytes 54067200
  1524.1 18.6 copy-start.45
  1524.1 18.6 copy-start.55
  1547.2 9.3 slice-start
  1551.7 14.1 slice-start.2
  1556.5 9.3 slice-start.3
  1642.6 10.6 copy-start.8
  1642.6 10.6 copy-start.38
  1642.6 10.6 copy-start.73
  (132 other events, 467.4 us)
Sparse Core Ops, SparseCore 0:
  11.5 160.3 all-gather.6
  184.8 23.1 all-gather.10
  210.1 24.3 all-gather.8
  236.4 24.2 all-gather.14
  262.7 24.2 all-gather.12
  290.4 78.5 all-gather.16
  844.5 23.1 reduce-scatter.24
  1406.4 23.1 reduce-scatter.18
  1432.5 23.1 reduce-scatter.20
  1458.5 23.1 reduce-scatter.22
  1488.5 119.6 all-reduce.5
  1610.4 362.1 reduce-scatter.16
  1974.9 1100.6 reduce-scatter.26
where the time goes:
time: 3110 us; the launch traced here: 3100 us
  waiting for transfers between devices  1560 us (50%)
  matrix products  866 us (28%)
  local copies, waits for them, and re-layouts  339 us (11%)
  other arithmetic  273 us (9%)
  blocking collectives  41.5 us (1%)
    unnamed x19, waiting for transfers between devices  1130 us
    dot_general x8, matrix products, self_scores(): jnp.einsum('hqd,hkd->hqk', query_heads, key_heads, preferred_element_type...  411 us
    reduce_scatter x1, waiting for transfers between devices, local(): lax.psum_scatter(down_grad, ('dp', 'stream'), scatter_dimension=0, tiled=...  307 us
    and x8, other arithmetic, local(): allowed = same_doc & ((distance > 0) | (distance == 0) & main_flag[:, None])  146 us
    unnamed x226, local copies, waits for them, and re-layouts  116 us
    all_gather x1, waiting for transfers between devices, local(): lax.all_gather(proj_low, ('dp', 'stream'), axis=1, tiled=True)  116 us
    dot_general x8, matrix products, matmul(): return jnp.dot(left_side, right_side, preferred_element_type=jnp.float32)  98.5 us
    dot_general x8, matrix products, times_transpose(): lax.dot_general(left_side, right_side, (((1,), (1,)), ((), ())), preferre...  76.8 us
  transfers between devices with their start and end apart: 13, of which 6 were waited for; matrix products, arithmetic and copies ran while one was open for 41% of the time, Pallas kernels for 0%

commit v1 on v0

--- a/solution.py
+++ b/solution.py
@@ -237,7 +237,86 @@
     return (master_new, first_new, second_new)
 
 
+def column_sums(left_side, right_side):
+    return outer_sum(left_side, right_side).astype(jnp.bfloat16)
+
+
+def inner_levels(dp_count):
+    levels = [("dp", 1, 2), ("stream", 1, 2)]
+    if dp_count == 64:
+        return levels + [("dp", 2, 2), ("dp", 4, 4)]
+    return levels + [("dp", 2, 2)]
+
+
+def rotation(level, shift, dp_count):
+    axis, stride, size = level
+    total = 2 if axis == "stream" else dp_count
+    pairs = []
+    for source in range(total):
+        place = (source // stride) % size
+        target = source + ((place + shift) % size - place) * stride
+        pairs.append((source, target))
+    return pairs
+
+
+def place_on(level):
+    axis, stride, size = level
+    return (lax.axis_index(axis) // stride) % size
+
+
+def pick(stacked, index, dim):
+    return lax.dynamic_index_in_dim(stacked, index, dim, keepdims=False)
+
+
+def scatter_level(stacked, dim, level, dp_count, final_type):
+    axis, stride, size = level
+    mine = place_on(level)
+    total = pick(stacked, mine, dim).astype(jnp.float32)
+    for shift in range(1, size):
+        sent = pick(stacked, (mine + shift) % size, dim)
+        came = lax.ppermute(sent, axis, rotation(level, shift, dp_count))
+        total = total + came.astype(jnp.float32)
+    return total.astype(final_type)
+
+
+def scatter_rows(rows, outer_range, dp_count):
+    levels = inner_levels(dp_count)
+    inner = levels[2:]
+    sizes = [size for axis, stride, size in reversed(inner)]
+    outer_count = len(outer_range)
+    width = rows.shape[1]
+    block = rows.shape[0] // (outer_count * math.prod(sizes) * 4)
+    stacked = rows.reshape([outer_count] + sizes + [2, 2, block, width])
+    core_dim = 1 + len(sizes)
+    stacked = scatter_level(stacked, core_dim, levels[0], dp_count, jnp.bfloat16)
+    outer_level = ("dp", dp_count // 4, 4)
+    zi = place_on(outer_level)
+    results = []
+    for part in range(2):
+        cut = (block // 2 + 15) // 16 * 16
+        piece = stacked[..., :cut, :] if part == 0 else stacked[..., cut:, :]
+        names = list(reversed(inner)) + [levels[1]]
+        order = [levels[1]] + inner if part == 0 else [inner[0], levels[1]] + inner[1:]
+        for level in order:
+            dim = 1 + names.index(level)
+            names.remove(level)
+            piece = scatter_level(piece, dim, level, dp_count, jnp.bfloat16)
+        first = outer_range[0]
+        total = pick(piece, jnp.clip(zi - first, 0, outer_count - 1), 0).astype(jnp.float32)
+        for shift in range(1, 4):
+            pairs = [
+                pair
+                for pair in rotation(outer_level, shift, dp_count)
+                if pair[1] // outer_level[1] in outer_range
+            ]
+            target = jnp.clip((zi + shift) % 4 - first, 0, outer_count - 1)
+            total = total + lax.ppermute(pick(piece, target, 0), "dp", pairs).astype(jnp.float32)
+        results.append(total)
+    return jnp.concatenate(results)
+
+
 def local(
+    dp_count,
     main_rows,
     pred_rows,
     enc_rows,
@@ -257,14 +336,15 @@
     small_first,
     small_second,
 ):
-    proj_low = proj_master.astype(jnp.bfloat16)
+    proj_low = proj_master.astype(jnp.bfloat16).T
     bias_low = bias_master.astype(jnp.bfloat16)
     down_low = down_master.astype(jnp.bfloat16)
-    proj_weight, bias_weight, down_weight = (
-        lax.all_gather(proj_low, ("dp", "stream"), axis=1, tiled=True),
+    proj_rows, bias_weight, down_weight = (
+        lax.all_gather(proj_low, ("dp", "stream"), axis=0, tiled=True),
         lax.all_gather(bias_low, ("dp", "stream"), axis=0, tiled=True),
         lax.all_gather(down_low, ("dp", "stream"), axis=0, tiled=True),
     )
+    proj_weight = proj_rows.T
     rel_width = BUCKETS * HEADS
     cross_start = 4 * D + rel_width
     self_weight = proj_weight[:, 0 : 3 * D]
@@ -287,6 +367,7 @@
     half_rows = main_rows.shape[0]
     group_rows = pred_rows.shape[0]
     main_start = lax.axis_index("stream") * half_rows
+    zi = place_on(("dp", dp_count // 4, 4))
     places = jnp.arange(group_rows, dtype=jnp.int32)
     group_docs = doc_ids(doc_lengths[0], group_rows)
     query_docs = jnp.concatenate(
@@ -351,16 +432,15 @@
     unused, norm_three = jax.vjp(layer_norm, norm_three_in, small_master[3], small_master[6])
     sum_three, gain_three, shift_three = norm_three(cotangent)
     ffn_grad = sum_three.astype(jnp.bfloat16)
-    down_grad = outer_sum(activated, ffn_grad)
+    down_shard_grad = scatter_rows(column_sums(activated, ffn_grad), range(4), dp_count)
     act_grad = times_transpose(ffn_grad, down_weight)
     unused, gelu_back = jax.vjp(partial(jax.nn.gelu, approximate=False), pre_act)
     pre_grad = gelu_back(act_grad)[0].astype(jnp.bfloat16)
-    up_grad = outer_sum(two_low, pre_grad)
+    up_rows = column_sums(pre_grad, two_low)
     two_grad = sum_three + times_transpose(pre_grad, up_weight)
     unused, norm_two = jax.vjp(layer_norm, norm_two_in, small_master[2], small_master[5])
     sum_two, gain_two, shift_two = norm_two(two_grad)
     branch_grad = sum_two.astype(jnp.bfloat16)
-    back_grad = outer_sum(cross_context_low, branch_grad)
     cross_context_grad = times_transpose(branch_grad, back_weight).astype(jnp.bfloat16)
     cquery_stack, ckey_stack, cvalue_stack = lax.map(
         partial(cross_backward, same_doc=same_doc),
@@ -381,15 +461,18 @@
         ).astype(jnp.float32),
     )
     pair_grad = jnp.concatenate([ckey_grad, cvalue_grad], axis=1).astype(jnp.bfloat16)
-    pair_weight_grad = outer_sum(enc_rows, pair_grad)
+    pair_rows = column_sums(pair_grad, enc_rows)
+    half_cols = proj_rows.shape[0] // 2
+    early_rows = jnp.concatenate(
+        [pair_rows[half_cols - cross_start - D :], column_sums(branch_grad, cross_context_low), up_rows]
+    )
+    proj_early = scatter_rows(early_rows, range(2, 4), dp_count)
     enc_grad = times_transpose(pair_grad, pair_weight).astype(jnp.bfloat16)
     cquery_grad = join_heads(cquery_stack).astype(jnp.bfloat16)
-    cross_weight_grad = outer_sum(one_low, cquery_grad)
     one_grad = sum_two + times_transpose(cquery_grad, cross_weight)
     unused, norm_one = jax.vjp(layer_norm, norm_one_in, small_master[1], small_master[4])
     sum_one, gain_one, shift_one = norm_one(one_grad)
     attn_grad = sum_one.astype(jnp.bfloat16)
-    out_grad = outer_sum(context_low, attn_grad)
     context_grad = times_transpose(attn_grad, out_weight).astype(jnp.bfloat16)
     one_hot = (buckets[:, :, None] == jnp.arange(BUCKETS, dtype=jnp.int32)[None, None, :]).astype(
         jnp.bfloat16
@@ -424,26 +507,23 @@
         jnp.bfloat16
     )
     table_grad = join_table(table_stack).astype(jnp.bfloat16)
-    self_weight_grad = outer_sum(inputs, self_grad)
-    table_weight_grad = outer_sum(inputs, table_grad)
     input_grad = (
         sum_one
         + times_transpose(self_grad, self_weight)
         + times_transpose(table_grad, table_weight)
     )
     self_sums = jnp.sum(self_grad, axis=0, dtype=jnp.float32)
-    proj_grad_full = jnp.concatenate(
+    late_rows = jnp.concatenate(
         [
-            self_weight_grad,
-            out_grad,
-            table_weight_grad,
-            cross_weight_grad,
-            pair_weight_grad,
-            back_grad,
-            up_grad,
-        ],
-        axis=1,
-    )
+            column_sums(self_grad, inputs),
+            column_sums(attn_grad, context_low),
+            column_sums(table_grad, inputs),
+            column_sums(cquery_grad, one_low),
+            pair_rows[: half_cols - cross_start - D],
+        ]
+    )
+    proj_late = scatter_rows(late_rows, range(0, 2), dp_count)
+    proj_grad = jnp.where(zi < 2, proj_late, proj_early).T
     bias_grad_full = jnp.concatenate(
         [
             self_sums[0:D],
@@ -467,12 +547,23 @@
             shift_three,
         ]
     )
-    proj_grad, bias_grad, down_shard_grad = (
-        lax.psum_scatter(proj_grad_full, ("dp", "stream"), scatter_dimension=1, tiled=True),
-        lax.psum_scatter(bias_grad_full, ("dp", "stream"), scatter_dimension=0, tiled=True),
-        lax.psum_scatter(down_grad, ("dp", "stream"), scatter_dimension=0, tiled=True),
-    )
-    small_grad = lax.psum(small_stack, ("dp", "stream"))
+    count = 2 * dp_count
+    vector_parts = jnp.concatenate(
+        [bias_grad_full.reshape(count, -1), small_stack.reshape(count, -1)], axis=1
+    )
+    vector_sum = jnp.sum(
+        lax.all_to_all(vector_parts, ("dp", "stream"), 0, 0, tiled=True), axis=0
+    )
+    bias_len = bias_master.shape[0]
+    bias_grad = vector_sum[:bias_len]
+    small_part = vector_sum[bias_len:]
+    small_grad = lax.all_to_all(
+        jnp.broadcast_to(small_part[None], (count, small_part.shape[0])),
+        ("dp", "stream"),
+        0,
+        0,
+        tiled=True,
+    ).reshape(small_master.shape)
     proj_new, proj_first_new, proj_second_new = adam_step(
         proj_master, proj_first, proj_second, proj_grad, RATE_MATRIX, WEIGHT_DECAY
     )
@@ -528,7 +619,7 @@
         P(),
     )
     return jax.shard_map(
-        local,
+        partial(local, mesh.shape["dp"]),
         mesh=mesh,
         in_specs=placed,
         out_specs=(

time: 3110 us -> 1930 us (0.62)
  waiting for transfers between devices: 1560 us -> 261 us
  starting transfers between devices: 1 us -> 74 us
  other arithmetic: 273 us -> 325 us
  local copies, waits for them, and re-layouts: 339 us -> 297 us
    unnamed x19 -> x14, waiting for transfers between devices: 1130 us -> 1.39 us
    reduce_scatter x1 -> x0, waiting for transfers between devices: 307 us -> none  [local(): lax.psum_scatter(down_grad, ('dp', 'stream'), scatter_dimension=0, tiled=...]
    ppermute x0 -> x33, waiting for transfers between devices: none -> 129 us  [the longest x15 93.8 us: scatter_level(): came = lax.ppermute(sent, axis, rotation(level, shift, dp_count))]
    unnamed x226 -> x245, local copies, waits for them, and re-layouts: 116 us -> 44.5 us
    ppermute x0 -> x33, starting transfers between devices: none -> 61.4 us  [the longest x18 52.3 us: scatter_rows(): lax.ppermute(pick(piece, target, 0), 'dp', pairs).astype(jnp.float32)]
    convert_element_type x1 -> x15, other arithmetic: 2.58 us -> 34.7 us  [scatter_level(): return total.astype(final_type)]
  transfers between devices with their start and end apart: 13 -> 45, of which waited for: 6 -> 13; matrix products, arithmetic and copies ran while one was open for 41% -> 39% of each run, Pallas kernels for 0% -> 0%
where the time goes in v1:
time: 1930 us; the launch traced here: 1910 us
  matrix products  892 us (46%)
  other arithmetic  325 us (17%)
  local copies, waits for them, and re-layouts  297 us (15%)
  waiting for transfers between devices  261 us (14%)
  starting transfers between devices  74 us (4%)
  blocking collectives  41.5 us (2%)
    dot_general x8, matrix products, self_scores(): jnp.einsum('hqd,hkd->hqk', query_heads, key_heads, preferred_element_type...  411 us
    and x8, other arithmetic, local(): allowed = same_doc & ((distance > 0) | (distance == 0) & main_flag[:, None])  146 us
    all_gather x1, waiting for transfers between devices, local(): lax.all_gather(proj_low, ('dp', 'stream'), axis=0, tiled=True)  116 us
    dot_general x8, matrix products, matmul(): return jnp.dot(left_side, right_side, preferred_element_type=jnp.float32)  98.8 us
    ppermute x15, waiting for transfers between devices, scatter_level(): came = lax.ppermute(sent, axis, rotation(level, shift, dp_count))  93.8 us
    dot_general x8, matrix products, outer_sum(): lax.dot_general(left_side, right_side, (((0,), (0,)), ((), ())), preferre...  78.5 us
    dot_general x8, matrix products, times_transpose(): lax.dot_general(left_side, right_side, (((1,), (1,)), ((), ())), preferre...  76.7 us
    scatter-add x4, local copies, waits for them, and re-layouts, self_backward(): table_grad = table_grad.at[:, :, 0].add(own_grad.astype(jnp.float32))  65 us
  transfers between devices with their start and end apart: 45, of which 13 were waited for; matrix products, arithmetic and copies ran while one was open for 39% of the time, Pallas kernels for 0%

profile of v1, /device:TPU:11, one launch (start us, length us, event | category | flops | bytes accessed | tf_op | source)
XLA Modules:
  0.0 1910.7 jit_solution(14871969966051882996)
XLA Ops:
  10.8 41.5 %all-reduce.1 = bf16[10752]{0:T(1024)(128)(2,1)S(1)} all-reduce(bf16[10752]{0:T(1024)(128)(2,1)S(1)} %dynamic-update-slice.7), channel_id=1, replica_groups=mesh['dp'=16,'stream'=2] {'dp','stream'}, use_global_device_ids=true, to_apply=%add.1 | all-reduce | flops 10752 | bytes 43008
  56.1 115.8 %all-gather.7.cloned.1.call-done = bf16[12800,1024]{1,0:T(8,128)(2,1)} async-done(((bf16[400,1024]{1,0:T(8,128)(2,1)}), bf16[12800,1024]{1,0:T(8,128)(2,1)}) %all-gather.7.cloned.1.call-update) | async-done | bytes 26214416 | tf_op jit(solution)/shard_map/all_gather | solution.py:343
  238.4 301.9 %while.71 = (s32[]{:T(128)}, bf16[4,4,960,64]{2,3,1,0:T(8,128)(2,1)}, f32[4,4,960]{2,1,0:T(4,128)S(1)}, bf16[4,4,960,64]{2,3,1,0:T(8,128)(2,1)S(1)}, bf16[4,4,64...) while((s32[]{:T(128)}, ...), condition=%wide.region_6.7_spmd.clone.clone.clone, body=%wide.region_2.6_spmd.clone.clone.clone.sunk | while | flops 861320640 | bytes 76626888 | solution.py:410
  239.0 17.2 fusion.468
  257.3 49.3 %fusion.469 = (f32[4,960]{1,0:T(4,128)S(1)}, f32[4,960,640]{2,1,0:T(8,128)S(1)}) fusion(f32[4,960]{1,0:T(4,128)S(1)} %get-tuple-element.1721, pred[960,640]{1,0:T(8,128)(4,1)} %get-tuple-element.1722, f32[4,960]{1,0:T(4,128)S(1)} %get-tuple-element.1723, pred[960,640]{1,0:T(8,128)(4,1)} %get-tuple-element.1724, ...), kind=kOutput, calls=%fused_computation.611.clone.3 | convolution fusion | flops 479228160 | bytes 31498240 | tf_op jit(solution)/shard_map/while/body/eval_jaxpr/hqd,hkd->hqk/dot_general | solution.py:101
  314.3 17.1 fusion.468
  332.6 49.3 %fusion.469 = (f32[4,960]{1,0:T(4,128)S(1)}, f32[4,960,640]{2,1,0:T(8,128)S(1)}) fusion(f32[4,960]{1,0:T(4,128)S(1)} %get-tuple-element.1721, pred[960,640]{1,0:T(8,128)(4,1)} %get-tuple-element.1722, f32[4,960]{1,0:T(4,128)S(1)} %get-tuple-element.1723, pred[960,640]{1,0:T(8,128)(4,1)} %get-tuple-element.1724, ...), kind=kOutput, calls=%fused_computation.611.clone.3 | convolution fusion | flops 479228160 | bytes 31498240 | tf_op jit(solution)/shard_map/while/body/eval_jaxpr/hqd,hkd->hqk/dot_general | solution.py:101
  389.6 17.1 fusion.468
  407.9 49.3 %fusion.469 = (f32[4,960]{1,0:T(4,128)S(1)}, f32[4,960,640]{2,1,0:T(8,128)S(1)}) fusion(f32[4,960]{1,0:T(4,128)S(1)} %get-tuple-element.1721, pred[960,640]{1,0:T(8,128)(4,1)} %get-tuple-element.1722, f32[4,960]{1,0:T(4,128)S(1)} %get-tuple-element.1723, pred[960,640]{1,0:T(8,128)(4,1)} %get-tuple-element.1724, ...), kind=kOutput, calls=%fused_computation.611.clone.3 | convolution fusion | flops 479228160 | bytes 31498240 | tf_op jit(solution)/shard_map/while/body/eval_jaxpr/hqd,hkd->hqk/dot_general | solution.py:101
  464.9 17.1 fusion.468
  483.2 49.3 %fusion.469 = (f32[4,960]{1,0:T(4,128)S(1)}, f32[4,960,640]{2,1,0:T(8,128)S(1)}) fusion(f32[4,960]{1,0:T(4,128)S(1)} %get-tuple-element.1721, pred[960,640]{1,0:T(8,128)(4,1)} %get-tuple-element.1722, f32[4,960]{1,0:T(4,128)S(1)} %get-tuple-element.1723, pred[960,640]{1,0:T(8,128)(4,1)} %get-tuple-element.1724, ...), kind=kOutput, calls=%fused_computation.611.clone.3 | convolution fusion | flops 479228160 | bytes 31498240 | tf_op jit(solution)/shard_map/while/body/eval_jaxpr/hqd,hkd->hqk/dot_general | solution.py:101
  562.9 48.5 %while.68 = (s32[]{:T(128)}, bf16[4,4,960,64]{2,3,1,0:T(8,128)(2,1)}, f32[4,4,960]{2,1,0:T(4,128)S(1)}, bf16[4,4,960,64]{2,3,1,0:T(8,128)(2,1)S(1)}, bf16[4,4,64...) while((s32[]{:T(128)}, ...), condition=%wide.region_12.13_spmd.clone, body=%wide.region_9.12_spmd.clone.sunk | while | flops 659247360 | bytes 34311520 | solution.py:420
  620.8 48.6 %multiply_convert_fusion.2 = (bf16[960,4096]{1,0:T(8,128)(2,1)}, f32[960,4096]{1,0:T(8,128)}, f32[960,4096]{1,0:T(8,128)}) fusion(f32[4096]{0:T(1024)S(1)} %copy-done.106, bf16[1024,12800]{0,1:T(8,128)(2,1)} %bitcast.812, f32[960,1024]{1,0:T(8,128)S(1)} %get-tuple-element.1172, f32[1024]{0:T(1024)S(1)} %bitcast.840, f32[1024]{0:T(1024)S(1)} %bitcast.829, ...), kind=kOutput, calls=%fused_computation.348 | convolution fusion | flops 8317501440 | bytes 51674624 | tf_op jit(solution)/shard_map/dot_general | solution.py:52
  669.4 14.4 fusion.358
  695.2 23.6 %convert_reduce_fusion = (f32[4096]{0:T(1024)}, bf16[960,4096]{1,0:T(8,128)(2,1)}) fusion(f32[960,4096]{1,0:T(8,128)} %get-tuple-element.979, f32[960,4096]{1,0:T(8,128)} %get-tuple-element.1173, f32[4096]{0:T(1024)S(1)} %copy-done.106, bf16[960,1024]{1,0:T(8,128)(2,1)S(1)} %get-tuple-element.968, bf16[4096,1024]{1,0:T(8,128)(2,1)} %all-gather.17.cloned.1.call-done), kind=kOutput, calls=%fused_computation.346 | convolution fusion | flops 8119906304 | bytes 49709056 | tf_op jit(solution)/shard_map/dot_general | solution.py:62
  718.8 16.7 multiply_reduce_fusion.2
  753.2 83.3 %while.69 = (s32[]{:T(128)}, bf16[4,4,960,64]{2,3,1,0:T(8,128)(2,1)}, bf16[4,4,640,64]{2,3,1,0:T(8,128)(2,1)}, bf16[4,4,640,64]{2,3,1,0:T(8,128)(2,1)}, bf16[4,4...) while((s32[]{:T(128)}, ...), condition=%wide.region_23.24_spmd.clone, body=%wide.region_21.23_spmd.clone.sunk | while | flops 1610748160 | bytes 100096464 | solution.py:445
  865.0 546.3 %while.70 = (s32[]{:T(128)}, bf16[4,4,960,64]{2,3,1,0:T(8,128)(2,1)}, bf16[4,4,640,64]{2,3,1,0:T(8,128)(2,1)}, bf16[4,4,640,64]{2,3,1,0:T(8,128)(2,1)}, bf16[4,4...) while((s32[]{:T(128)}, ...), condition=%wide.region_30.31_spmd.clone.clone, body=%wide.region_26.30_spmd.clone.clone.sunk | while | flops 2006722304 | bytes 274161600 | solution.py:490
  869.5 19.3 %fusion.460 = (pred[960,640]{1,0:T(8,128)(4,1)S(1)}, pred[960,640]{1,0:T(8,128)(4,1)S(1)}, pred[960,640]{1,0:T(8,128)(4,1)S(1)}, pred[960,640]{1,0:T(8,128)(4,1)...) fusion(s32[960]{0:T(1024)S(1)} %get-tuple-element.1958, ...), kind=kLoop, calls=%fused_computation.100.clone.1 | loop fusion | flops 53452800 | bytes 20286400 | tf_op jit(solution)/shard_map/and | solution.py:380
  892.0 53.5 %multiply_reduce_fusion.12 = (f32[4,960]{1,0:T(4,128)S(1)}, f32[4,960,640]{2,1,0:T(8,128)S(1)}) fusion(f32[4,960,640]{2,1,0:T(8,128)S(1)} %fusion.458, f32[4,960]{1,0:T(4,128)S(1)} %dynamic-slice_bitcast_fusion.39, f32[4,960]{1,0:T(4,128)S(1)} %get-tuple-element.1636, pred[960,640]{1,0:T(8,128)(4,1)} %get-tuple-element.1637, ...), kind=kOutput, calls=%fused_computation.74.clone.3 | convolution fusion | flops 484143360 | bytes 41334784 | tf_op jit(solution)/shard_map/while/body/eval_jaxpr/hqd,hkd->hqk/dot_general | solution.py:101
  949.3 14.9 fusion.462
  967.4 16.2 scatter-add.8
  1005.9 19.3 %fusion.460 = (pred[960,640]{1,0:T(8,128)(4,1)S(1)}, pred[960,640]{1,0:T(8,128)(4,1)S(1)}, pred[960,640]{1,0:T(8,128)(4,1)S(1)}, pred[960,640]{1,0:T(8,128)(4,1)...) fusion(s32[960]{0:T(1024)S(1)} %get-tuple-element.1958, ...), kind=kLoop, calls=%fused_computation.100.clone.1 | loop fusion | flops 53452800 | bytes 20286400 | tf_op jit(solution)/shard_map/and | solution.py:380
  1028.5 53.5 %multiply_reduce_fusion.12 = (f32[4,960]{1,0:T(4,128)S(1)}, f32[4,960,640]{2,1,0:T(8,128)S(1)}) fusion(f32[4,960,640]{2,1,0:T(8,128)S(1)} %fusion.458, f32[4,960]{1,0:T(4,128)S(1)} %dynamic-slice_bitcast_fusion.39, f32[4,960]{1,0:T(4,128)S(1)} %get-tuple-element.1636, pred[960,640]{1,0:T(8,128)(4,1)} %get-tuple-element.1637, ...), kind=kOutput, calls=%fused_computation.74.clone.3 | convolution fusion | flops 484143360 | bytes 41334784 | tf_op jit(solution)/shard_map/while/body/eval_jaxpr/hqd,hkd->hqk/dot_general | solution.py:101
  1085.8 14.9 fusion.462
  1103.8 16.2 scatter-add.8
  1142.3 19.3 %fusion.460 = (pred[960,640]{1,0:T(8,128)(4,1)S(1)}, pred[960,640]{1,0:T(8,128)(4,1)S(1)}, pred[960,640]{1,0:T(8,128)(4,1)S(1)}, pred[960,640]{1,0:T(8,128)(4,1)...) fusion(s32[960]{0:T(1024)S(1)} %get-tuple-element.1958, ...), kind=kLoop, calls=%fused_computation.100.clone.1 | loop fusion | flops 53452800 | bytes 20286400 | tf_op jit(solution)/shard_map/and | solution.py:380
  1164.9 53.5 %multiply_reduce_fusion.12 = (f32[4,960]{1,0:T(4,128)S(1)}, f32[4,960,640]{2,1,0:T(8,128)S(1)}) fusion(f32[4,960,640]{2,1,0:T(8,128)S(1)} %fusion.458, f32[4,960]{1,0:T(4,128)S(1)} %dynamic-slice_bitcast_fusion.39, f32[4,960]{1,0:T(4,128)S(1)} %get-tuple-element.1636, pred[960,640]{1,0:T(8,128)(4,1)} %get-tuple-element.1637, ...), kind=kOutput, calls=%fused_computation.74.clone.3 | convolution fusion | flops 484143360 | bytes 41334784 | tf_op jit(solution)/shard_map/while/body/eval_jaxpr/hqd,hkd->hqk/dot_general | solution.py:101
  1222.2 14.9 fusion.462
  1240.3 16.2 scatter-add.8
  1278.7 19.3 %fusion.460 = (pred[960,640]{1,0:T(8,128)(4,1)S(1)}, pred[960,640]{1,0:T(8,128)(4,1)S(1)}, pred[960,640]{1,0:T(8,128)(4,1)S(1)}, pred[960,640]{1,0:T(8,128)(4,1)...) fusion(s32[960]{0:T(1024)S(1)} %get-tuple-element.1958, ...), kind=kLoop, calls=%fused_computation.100.clone.1 | loop fusion | flops 53452800 | bytes 20286400 | tf_op jit(solution)/shard_map/and | solution.py:380
  1301.3 53.5 %multiply_reduce_fusion.12 = (f32[4,960]{1,0:T(4,128)S(1)}, f32[4,960,640]{2,1,0:T(8,128)S(1)}) fusion(f32[4,960,640]{2,1,0:T(8,128)S(1)} %fusion.458, f32[4,960]{1,0:T(4,128)S(1)} %dynamic-slice_bitcast_fusion.39, f32[4,960]{1,0:T(4,128)S(1)} %get-tuple-element.1636, pred[960,640]{1,0:T(8,128)(4,1)} %get-tuple-element.1637, ...), kind=kOutput, calls=%fused_computation.74.clone.3 | convolution fusion | flops 484143360 | bytes 41334784 | tf_op jit(solution)/shard_map/while/body/eval_jaxpr/hqd,hkd->hqk/dot_general | solution.py:101
  1358.6 14.9 fusion.462
  1376.7 16.2 scatter-add.8
  1418.7 11.9 convolution_convert_fusion
  1464.4 14.8 convolution_convert_fusion.1
  1483.4 16.4 convert_reduce_fusion.1
  1499.9 28.4 %convert_dynamic-update-slice_fusion = bf16[6400,1024]{1,0:T(8,128)(2,1)} fusion(bf16[960,1024]{1,0:T(8,128)(2,1)} %constant_dynamic-update-slice_fusion.1, bf16[640,1024]{0,1:T(8,128)(2,1)S(1)} %bitcast.804, bf16[320,1024]{0,1:T(8,128)(2,1)S(1)} %copy-done.50, bf16[640,1024]{0,1:T(8,128)(2,1)S(1)} %bitcast.801, bf16[320,1024]{0,1:T(8,128)(2,1)S(1)} %copy.308, ...), kind=kOutput, calls=%fused_computation.384 | convolution fusion | flops 6072434688 | bytes 14155776 | tf_op jit(solution)/shard_map/dot_general | solution.py:56
  1562.2 25.3 %pad_maximum_fusion = bf16[6400,1024]{1,0:T(8,128)(2,1)S(1)} fusion(bf16[4096,1024]{1,0:T(8,128)(2,1)} %convolution_convert_fusion.1, bf16[1024,1024]{1,0:T(8,128)(2,1)S(1)} %copy-done.53, bf16[1280,1024]{1,0:T(8,128)(2,1)S(1)} %slice.780), kind=kLoop, calls=%fused_computation.362 | loop fusion | flops 39321600 | bytes 26214400 | tf_op jit(solution)/shard_map/concatenate | solution.py:466
  1587.5 12.3 constant_dynamic-slice_fusion.3
  1685.1 11.1 fusion.238
  1736.6 32.6 %collective-permute-done.17 = bf16[2,2,192,1024]{3,2,0,1:T(8,128)(2,1)S(1)} collective-permute-done((bf16[2,2,192,1024]{3,2,0,1:T(8,128)(2,1)S(1)}, bf16[2,2,192,1024]{3,2,0,1:T(8,128)(2,1)S(1)}, u32[]{:S(2)}, u32[]{:S(2)}) %collective-permute-start.17) | collective-permute-done | bytes 1572896 | tf_op jit(solution)/shard_map/ppermute | solution.py:277
  1772.4 22.8 %collective-permute-done.12 = bf16[2,2,208,1024]{3,2,0,1:T(8,128)(2,1)S(1)} collective-permute-done((bf16[2,2,208,1024]{3,2,0,1:T(8,128)(2,1)S(1)}, bf16[2,2,208,1024]{3,2,0,1:T(8,128)(2,1)S(1)}, u32[]{:S(2)}, u32[]{:S(2)}) %collective-permute-start.12) | collective-permute-done | bytes 1703968 | tf_op jit(solution)/shard_map/ppermute | solution.py:277
  1796.8 15.2 collective-permute-done.7
  1815.7 13.2 collective-permute-done.18
  1841.1 22.5 %collective-permute-start.5 = (bf16[208,1024]{1,0:T(8,128)(2,1)S(1)}, bf16[208,1024]{1,0:T(8,128)(2,1)S(1)}, u32[]{:S(2)}, u32[]{:S(2)}) collective-permute-start(bf16[208,1024]{1,0:T(8,128)(2,1)S(1)} %get-tuple-element.1139), channel_id=1, source_target_pairs={{8,0},{10,2},{12,4},{14,6},{16,8},{18,10},{20,12},{22,14},{9,1},{1... | collective-permute-start | bytes 1277960 | tf_op jit(solution)/shard_map/ppermute | solution.py:313
  1870.8 16.4 collective-permute-done.5
  1887.5 12.4 collective-permute-done.15
  (811 shorter events, 692.8 us)
Async XLA Ops:
  7.2 178.2 %copy-start = (bf16[320,1024]{1,0:T(8,128)(2,1)S(1)}, bf16[320,1024]{1,0:T(8,128)(2,1)}, u32[]{:S(2)}) copy-start(bf16[320,1024]{1,0:T(8,128)(2,1)} %param.30) | copy-start | bytes 1966084
  7.2 164.7 %all-gather.7.cloned.1.call-start = ((), (), s32[]{:S(2)}) async-start(), calls=%async_computation.6 | async-start | bytes 27033600 | tf_op jit(solution)/shard_map/all_gather | solution.py:343
  9.9 217.3 %all-gather.11.cloned.1.call-start = ((), (), s32[]{:S(2)}) async-start(), calls=%async_computation.8 | async-start | bytes 1966080 | tf_op jit(solution)/shard_map/all_gather | solution.py:393
  184.6 49.8 %all-gather.9.cloned.1.call-start = ((), (), s32[]{:S(2)}) async-start(), calls=%async_computation.7 | async-start | bytes 1966080 | tf_op jit(solution)/shard_map/all_gather | solution.py:392
  185.4 371.1 %all-gather.13.cloned.1.call-start = ((), (), s32[]{:S(2)}) async-start(), calls=%async_computation.9 | async-start | bytes 1966080 | tf_op jit(solution)/shard_map/all_gather | solution.py:399
  190.4 368.5 %all-gather.15.cloned.1.call-start = ((), (), s32[]{:S(2)}) async-start(), calls=%async_computation.10 | async-start | bytes 1966080 | tf_op jit(solution)/shard_map/all_gather | solution.py:400
  191.0 478.4 %all-gather.17.cloned.1.call-start = ((), (), s32[]{:S(2)}) async-start(), calls=%async_computation.11 | async-start | bytes 8650752 | tf_op jit(solution)/shard_map/all_gather | solution.py:345
  191.8 1287.5 %reduce-scatter.13.cloned.1.call-start = ((), (), s32[]{:S(2)}) async-start(), calls=%async_computation.12 | async-start | bytes 1966080
  238.4 302.0 %copy-start.118 = (f32[1024]{0:T(1024)S(1)}, f32[1024]{0:T(1024)}, u32[]{:S(2)}) copy-start(f32[1024]{0:T(1024)} %get-tuple-element.1168) | copy-start | bytes 12292
  619.0 116.5 %copy-start.85 = (f32[960]{0:T(1024)}, f32[960]{0:T(1024)S(1)}, u32[]{:S(2)}) copy-start(f32[960]{0:T(1024)S(1)} %broadcast_multiply_fusion.1) | copy-start | bytes 11524
  1413.9 67.0 %reduce-scatter.15.cloned.1.call-start = ((), (), s32[]{:S(2)}) async-start(), calls=%async_computation.13 | async-start | bytes 1966080
  1418.6 110.3 %reduce-scatter.19.cloned.1.call-start = ((), (), s32[]{:S(2)}) async-start(), calls=%async_computation.15 | async-start | bytes 1966080
  1436.8 190.6 %collective-permute-start.22 = (bf16[4,2,2,128,1024]{4,3,0,2,1:T(8,128)(2,1)}, bf16[4,2,2,128,1024]{4,3,0,2,1:T(8,128)(2,1)}, u32[]{:S(2)}, u32[]{:S(2)}) collective-permute-start(bf16[4,2,2,128,1024]{4,3,0,2,1:T(8,128)(2,1)} %bitcast.639), channel_id=1, source_target_pairs={{0,2},{2,0},{4,6},{6,4},{8,10},{10,8},{12,14},{14,12},{16,18},{18,... | collective-permute-start | bytes 12582920 | tf_op jit(solution)/shard_map/ppermute | solution.py:277
  1458.0 96.3 %reduce-scatter.17.cloned.1.call-start = ((), (), s32[]{:S(2)}) async-start(), calls=%async_computation.14 | async-start | bytes 1966080
  1603.2 81.9 %collective-permute-start = (bf16[2,2,2,400,1024]{4,3,0,2,1:T(8,128)(2,1)}, bf16[2,2,2,400,1024]{4,3,0,2,1:T(8,128)(2,1)}, u32[]{:S(2)}, u32[]{:S(2)}) collective-permute-start(bf16[2,2,2,400,1024]{4,3,0,2,1:T(8,128)(2,1)} %bitcast.795), channel_id=1, source_target_pairs={{0,2},{2,0},{4,6},{6,4},{8,10},{10,8},{12,14},{14,12},{16,18},{18,... | collective-permute-start | bytes 19660808 | tf_op jit(solution)/shard_map/ppermute | solution.py:277
  1604.0 43.3 %all-to-all-start = ((f32[32,1,560]{2,1,0:T(1,128)}), f32[32,1,560]{2,1,0:T(1,128)}, u32[]{:S(2)}, u32[]{:S(2)}) async-start(f32[32,1,560]{2,1,0:T(1,128)} %all_to_all.10), calls=%async_computation | async-start | bytes 163840 | tf_op jit(solution)/shard_map/all_to_all | solution.py:555
  1617.3 85.3 %collective-permute-start.11 = (bf16[2,2,2,400,1024]{4,3,0,2,1:T(8,128)(2,1)}, bf16[2,2,2,400,1024]{4,3,0,2,1:T(8,128)(2,1)}, u32[]{:S(2)}, u32[]{:S(2)}) collective-permute-start(bf16[2,2,2,400,1024]{4,3,0,2,1:T(8,128)(2,1)} %bitcast.637), channel_id=1, source_target_pairs={{0,2},{2,0},{4,6},{6,4},{8,10},{10,8},{12,14},{14,12},{16,18},{18,... | collective-permute-start | bytes 19660808 | tf_op jit(solution)/shard_map/ppermute | solution.py:277
  1633.2 31.9 %collective-permute-start.23 = (bf16[4,2,64,1024]{3,2,0,1:T(8,128)(2,1)}, bf16[4,2,64,1024]{3,2,0,1:T(8,128)(2,1)}, u32[]{:S(2)}, u32[]{:S(2)}) collective-permute-start(bf16[4,2,64,1024]{3,2,0,1:T(8,128)(2,1)} %dynamic-slice_bitcast_fusion.9), channel_id=1, source_target_pairs={{0,1},{1,0},{2,3},{3,2},{4,5},{5,4},{6,7},{7,6},{8,9},{9,8},{10,11... | collective-permute-start | bytes 3145736 | tf_op jit(solution)/shard_map/ppermute | solution.py:277
  1639.1 29.3 %collective-permute-start.28 = (bf16[4,2,64,1024]{3,2,0,1:T(8,128)(2,1)}, bf16[4,2,64,1024]{3,2,0,1:T(8,128)(2,1)}, u32[]{:S(2)}, u32[]{:S(2)}) collective-permute-start(bf16[4,2,64,1024]{3,2,0,1:T(8,128)(2,1)} %dynamic-slice_bitcast_fusion.8), channel_id=1, source_target_pairs={{0,4},{2,6},{4,0},{6,2},{8,12},{10,14},{12,8},{14,10},{16,20},{18,... | collective-permute-start | bytes 3145736 | tf_op jit(solution)/shard_map/ppermute | solution.py:277
  1649.0 15.9 all-to-all-start.1
  1667.1 13.2 collective-permute-start.24
  1670.1 13.6 collective-permute-start.29
  1681.3 38.0 %collective-permute-start.25 = (bf16[64,1024]{1,0:T(8,128)(2,1)}, bf16[64,1024]{1,0:T(8,128)(2,1)S(1)}, u32[]{:S(2)}, u32[]{:S(2)}) collective-permute-start(bf16[64,1024]{1,0:T(8,128)(2,1)} %get-tuple-element.1150), channel_id=1, source_target_pairs={{0,8},{2,10},{4,12},{6,14},{8,16},{10,18},{12,20},{14,22},{16,24},... | collective-permute-start | bytes 393224 | tf_op jit(solution)/shard_map/ppermute | solution.py:313
  1682.5 37.2 %collective-permute-start.26 = (bf16[64,1024]{1,0:T(8,128)(2,1)}, bf16[64,1024]{1,0:T(8,128)(2,1)S(1)}, u32[]{:S(2)}, u32[]{:S(2)}) collective-permute-start(bf16[64,1024]{1,0:T(8,128)(2,1)} %get-tuple-element.1152), channel_id=1, source_target_pairs={{0,16},{2,18},{4,20},{6,22},{8,24},{10,26},{12,28},{14,30},{16,0},... | collective-permute-start | bytes 393224 | tf_op jit(solution)/shard_map/ppermute | solution.py:313
  1683.7 39.3 %collective-permute-start.27 = (bf16[64,1024]{1,0:T(8,128)(2,1)}, bf16[64,1024]{1,0:T(8,128)(2,1)}, u32[]{:S(2)}, u32[]{:S(2)}) collective-permute-start(bf16[64,1024]{1,0:T(8,128)(2,1)} %get-tuple-element.1151), channel_id=1, source_target_pairs={{0,24},{2,26},{4,28},{6,30},{8,0},{10,2},{12,4},{14,6},{16,8},{18,... | collective-permute-start | bytes 393224 | tf_op jit(solution)/shard_map/ppermute | solution.py:313
  1701.5 34.0 %collective-permute-start.6 = (bf16[2,2,192,1024]{3,2,0,1:T(8,128)(2,1)}, bf16[2,2,192,1024]{3,2,0,1:T(8,128)(2,1)S(1)}, u32[]{:S(2)}, u32[]{:S(2)}) collective-permute-start(bf16[2,2,192,1024]{3,2,0,1:T(8,128)(2,1)} %dynamic-slice_bitcast_fusion.7), channel_id=1, source_target_pairs={{0,4},{2,6},{4,0},{6,2},{8,12},{10,14},{12,8},{14,10},{16,20},{18,... | collective-permute-start | bytes 4718600 | tf_op jit(solution)/shard_map/ppermute | solution.py:277
  1716.2 53.0 %collective-permute-start.17 = (bf16[2,2,192,1024]{3,2,0,1:T(8,128)(2,1)S(1)}, bf16[2,2,192,1024]{3,2,0,1:T(8,128)(2,1)S(1)}, u32[]{:S(2)}, u32[]{:S(2)}) collective-permute-start(bf16[2,2,192,1024]{3,2,0,1:T(8,128)(2,1)S(1)} %dynamic-slice_bitcast_fusion.6), channel_id=1, source_target_pairs={{0,4},{2,6},{4,0},{6,2},{8,12},{10,14},{12,8},{14,10},{16,20},{18,... | collective-permute-start | bytes 4718600 | tf_op jit(solution)/shard_map/ppermute | solution.py:277
  1719.3 5.3 collective-permute-start.30
  1719.7 9.9 collective-permute-start.31
  1722.9 47.4 %collective-permute-start.1 = (bf16[2,2,208,1024]{3,2,0,1:T(8,128)(2,1)S(1)}, bf16[2,2,208,1024]{3,2,0,1:T(8,128)(2,1)S(1)}, u32[]{:S(2)}, u32[]{:S(2)}) collective-permute-start(bf16[2,2,208,1024]{3,2,0,1:T(8,128)(2,1)S(1)} %dynamic-slice_bitcast_fusion.5), channel_id=1, source_target_pairs={{0,1},{1,0},{2,3},{3,2},{4,5},{5,4},{6,7},{7,6},{8,9},{9,8},{10,11... | collective-permute-start | bytes 5111816 | tf_op jit(solution)/shard_map/ppermute | solution.py:277
  1724.6 8.6 collective-permute-start.32
  1729.6 65.6 %collective-permute-start.12 = (bf16[2,2,208,1024]{3,2,0,1:T(8,128)(2,1)S(1)}, bf16[2,2,208,1024]{3,2,0,1:T(8,128)(2,1)S(1)}, u32[]{:S(2)}, u32[]{:S(2)}) collective-permute-start(bf16[2,2,208,1024]{3,2,0,1:T(8,128)(2,1)S(1)} %dynamic-slice_bitcast_fusion.4), channel_id=1, source_target_pairs={{0,1},{1,0},{2,3},{3,2},{4,5},{5,4},{6,7},{7,6},{8,9},{9,8},{10,11... | collective-permute-start | bytes 5111816 | tf_op jit(solution)/shard_map/ppermute | solution.py:277
  1736.3 75.8 %collective-permute-start.7 = (bf16[2,192,1024]{2,1,0:T(8,128)(2,1)S(1)}, bf16[2,192,1024]{2,1,0:T(8,128)(2,1)S(1)}, u32[]{:S(2)}, u32[]{:S(2)}) collective-permute-start(bf16[2,192,1024]{2,1,0:T(8,128)(2,1)S(1)} %dynamic-slice_bitcast_fusion.13), channel_id=1, source_target_pairs={{0,1},{1,0},{2,3},{3,2},{4,5},{5,4},{6,7},{7,6},{8,9},{9,8},{10,11... | collective-permute-start | bytes 2359304 | tf_op jit(solution)/shard_map/ppermute | solution.py:277
  1770.0 58.9 %collective-permute-start.18 = (bf16[2,192,1024]{2,1,0:T(8,128)(2,1)S(1)}, bf16[2,192,1024]{2,1,0:T(8,128)(2,1)S(1)}, u32[]{:S(2)}, u32[]{:S(2)}) collective-permute-start(bf16[2,192,1024]{2,1,0:T(8,128)(2,1)S(1)} %dynamic-slice_bitcast_fusion.12), channel_id=1, source_target_pairs={{0,1},{1,0},{2,3},{3,2},{4,5},{5,4},{6,7},{7,6},{8,9},{9,8},{10,11... | collective-permute-start | bytes 2359304 | tf_op jit(solution)/shard_map/ppermute | solution.py:277
  1771.2 59.4 %collective-permute-start.2 = (bf16[2,208,1024]{2,1,0:T(8,128)(2,1)S(1)}, bf16[2,208,1024]{2,1,0:T(8,128)(2,1)S(1)}, u32[]{:S(2)}, u32[]{:S(2)}) collective-permute-start(bf16[2,208,1024]{2,1,0:T(8,128)(2,1)S(1)} %dynamic-slice_bitcast_fusion.11), channel_id=1, source_target_pairs={{0,4},{2,6},{4,0},{6,2},{8,12},{10,14},{12,8},{14,10},{16,20},{18,... | collective-permute-start | bytes 2555912 | tf_op jit(solution)/shard_map/ppermute | solution.py:277
  1796.1 37.1 %collective-permute-start.13 = (bf16[2,208,1024]{2,1,0:T(8,128)(2,1)S(1)}, bf16[2,208,1024]{2,1,0:T(8,128)(2,1)S(1)}, u32[]{:S(2)}, u32[]{:S(2)}) collective-permute-start(bf16[2,208,1024]{2,1,0:T(8,128)(2,1)S(1)} %dynamic-slice_bitcast_fusion.10), channel_id=1, source_target_pairs={{0,4},{2,6},{4,0},{6,2},{8,12},{10,14},{12,8},{14,10},{16,20},{18,... | collective-permute-start | bytes 2555912 | tf_op jit(solution)/shard_map/ppermute | solution.py:277
  1812.5 22.4 %collective-permute-start.10 = (bf16[192,1024]{1,0:T(8,128)(2,1)S(1)}, bf16[192,1024]{1,0:T(8,128)(2,1)S(1)}, u32[]{:S(2)}, u32[]{:S(2)}) collective-permute-start(bf16[192,1024]{1,0:T(8,128)(2,1)S(1)} %get-tuple-element.1145), channel_id=1, source_target_pairs={{8,0},{10,2},{12,4},{14,6},{16,8},{18,10},{20,12},{22,14},{9,1},{1... | collective-permute-start | bytes 1179656 | tf_op jit(solution)/shard_map/ppermute | solution.py:313
  1814.4 24.6 %collective-permute-start.8 = (bf16[192,1024]{1,0:T(8,128)(2,1)S(1)}, bf16[192,1024]{1,0:T(8,128)(2,1)S(1)}, u32[]{:S(2)}, u32[]{:S(2)}) collective-permute-start(bf16[192,1024]{1,0:T(8,128)(2,1)S(1)} %get-tuple-element.1144), channel_id=1, source_target_pairs={{0,8},{2,10},{4,12},{6,14},{24,0},{26,2},{28,4},{30,6},{1,9},{3,11... | collective-permute-start | bytes 1179656 | tf_op jit(solution)/shard_map/ppermute | solution.py:313
  1828.9 10.9 collective-permute-start.9
  1830.6 10.5 collective-permute-start.19
  1833.2 36.6 %collective-permute-start.3 = (bf16[208,1024]{1,0:T(8,128)(2,1)S(1)}, bf16[208,1024]{1,0:T(8,128)(2,1)S(1)}, u32[]{:S(2)}, u32[]{:S(2)}) collective-permute-start(bf16[208,1024]{1,0:T(8,128)(2,1)S(1)} %get-tuple-element.1138), channel_id=1, source_target_pairs={{0,8},{2,10},{4,12},{6,14},{24,0},{26,2},{28,4},{30,6},{1,9},{3,11... | collective-permute-start | bytes 1277960 | tf_op jit(solution)/shard_map/ppermute | solution.py:313
  1834.8 29.1 %collective-permute-start.20 = (bf16[192,1024]{1,0:T(8,128)(2,1)S(1)}, bf16[192,1024]{1,0:T(8,128)(2,1)S(1)}, u32[]{:S(2)}, u32[]{:S(2)}) collective-permute-start(bf16[192,1024]{1,0:T(8,128)(2,1)S(1)} %get-tuple-element.1149), channel_id=1, source_target_pairs={{0,16},{2,18},{4,20},{6,22},{8,24},{10,26},{12,28},{14,30},{1,17},... | collective-permute-start | bytes 1179656 | tf_op jit(solution)/shard_map/ppermute | solution.py:313
  1839.0 28.4 %collective-permute-start.21 = (bf16[192,1024]{1,0:T(8,128)(2,1)S(1)}, bf16[192,1024]{1,0:T(8,128)(2,1)S(1)}, u32[]{:S(2)}, u32[]{:S(2)}) collective-permute-start(bf16[192,1024]{1,0:T(8,128)(2,1)S(1)} %get-tuple-element.1148), channel_id=1, source_target_pairs={{0,24},{2,26},{4,28},{6,30},{24,16},{26,18},{28,20},{30,22},{1,25}... | collective-permute-start | bytes 1179656 | tf_op jit(solution)/shard_map/ppermute | solution.py:313
  1839.8 31.0 %collective-permute-start.4 = (bf16[208,1024]{1,0:T(8,128)(2,1)S(1)}, bf16[208,1024]{1,0:T(8,128)(2,1)S(1)}, u32[]{:S(2)}, u32[]{:S(2)}) collective-permute-start(bf16[208,1024]{1,0:T(8,128)(2,1)S(1)} %get-tuple-element.1140), channel_id=1, source_target_pairs={{16,0},{18,2},{20,4},{22,6},{24,8},{26,10},{28,12},{30,14},{17,1},... | collective-permute-start | bytes 1277960 | tf_op jit(solution)/shard_map/ppermute | solution.py:313
  1841.1 46.1 %collective-permute-start.5 = (bf16[208,1024]{1,0:T(8,128)(2,1)S(1)}, bf16[208,1024]{1,0:T(8,128)(2,1)S(1)}, u32[]{:S(2)}, u32[]{:S(2)}) collective-permute-start(bf16[208,1024]{1,0:T(8,128)(2,1)S(1)} %get-tuple-element.1139), channel_id=1, source_target_pairs={{8,0},{10,2},{12,4},{14,6},{16,8},{18,10},{20,12},{22,14},{9,1},{1... | collective-permute-start | bytes 1277960 | tf_op jit(solution)/shard_map/ppermute | solution.py:313
  1863.9 23.6 %collective-permute-start.14 = (bf16[208,1024]{1,0:T(8,128)(2,1)S(1)}, bf16[208,1024]{1,0:T(8,128)(2,1)S(1)}, u32[]{:S(2)}, u32[]{:S(2)}) collective-permute-start(bf16[208,1024]{1,0:T(8,128)(2,1)S(1)} %get-tuple-element.1141), channel_id=1, source_target_pairs={{8,16},{10,18},{12,20},{14,22},{16,24},{18,26},{20,28},{22,30},{9,... | collective-permute-start | bytes 1277960 | tf_op jit(solution)/shard_map/ppermute | solution.py:313
  1867.3 32.5 %collective-permute-start.15 = (bf16[208,1024]{1,0:T(8,128)(2,1)S(1)}, bf16[208,1024]{1,0:T(8,128)(2,1)S(1)}, u32[]{:S(2)}, u32[]{:S(2)}) collective-permute-start(bf16[208,1024]{1,0:T(8,128)(2,1)S(1)} %get-tuple-element.1143), channel_id=1, source_target_pairs={{0,16},{2,18},{4,20},{6,22},{8,24},{10,26},{12,28},{14,30},{1,17},... | collective-permute-start | bytes 1277960 | tf_op jit(solution)/shard_map/ppermute | solution.py:313
  1869.8 30.1 %collective-permute-start.16 = (bf16[208,1024]{1,0:T(8,128)(2,1)S(1)}, bf16[208,1024]{1,0:T(8,128)(2,1)S(1)}, u32[]{:S(2)}, u32[]{:S(2)}) collective-permute-start(bf16[208,1024]{1,0:T(8,128)(2,1)S(1)} %get-tuple-element.1142), channel_id=1, source_target_pairs={{0,24},{2,26},{4,28},{6,30},{24,16},{26,18},{28,20},{30,22},{1,25}... | collective-permute-start | bytes 1277960 | tf_op jit(solution)/shard_map/ppermute | solution.py:313
  (178 other events, 1838.3 us)
Sparse Core Ops, SparseCore 0:
  11.5 160.3 all-gather.6
  184.7 23.1 all-gather.10
  210.1 24.2 all-gather.8
  236.4 24.2 all-gather.12
  262.6 24.2 all-gather.14
  290.3 78.5 all-gather.16
  1414.0 23.1 reduce-scatter.12
  1440.2 23.1 reduce-scatter.14
  1465.7 23.1 reduce-scatter.18
  1491.6 23.1 reduce-scatter.16

commit v2 on v0

v2 whole, which is shorter than its diff:
```python
from functools import partial
import math

import jax
import jax.numpy as jnp
from jax import lax
from jax.experimental import pallas as pl
from jax.experimental.pallas import tpu as pltpu
from jax.sharding import PartitionSpec as P

D = 1024
HEADS = 16
BUCKETS = 32
STEP = 10
HEAD_DIM = 64
LANES = 128
CHUNK = 128
SCORE_SCALE = HEAD_DIM**-0.5

NORM_EPS = 1e-05
BETA_FIRST = 0.9
BETA_SECOND = 0.999
ADAM_EPS = 1e-08
RATE_MATRIX = 0.04
RATE_VECTOR = 0.15
RATE_SMALL = 0.5
WEIGHT_DECAY = 0.01
MASKED = -1e30


def bucket_edges():
    return [int(math.ceil(16.0 * 8.0 ** (step_index / 16.0))) for step_index in range(1, 16)]


def bucket_of(distance):
    counted = jnp.zeros_like(distance)
    for threshold in bucket_edges():
        counted = counted + (distance >= threshold).astype(jnp.int32)
    return jnp.where(distance < 16, distance, 16 + counted)


def doc_ids(lengths, length_total):
    doc_ends = jnp.cumsum(lengths)
    places = jnp.arange(length_total, dtype=jnp.int32)
    return jnp.sum((places[:, None] >= doc_ends[None, :]).astype(jnp.int32), axis=1)


def matmul(left_side, right_side):
    return jnp.dot(left_side, right_side, preferred_element_type=jnp.float32)


def outer_sum(left_side, right_side):
    return lax.dot_general(
        left_side, right_side, (((0,), (0,)), ((), ())), preferred_element_type=jnp.float32
    )


def times_transpose(left_side, right_side):
    return lax.dot_general(
        left_side, right_side, (((1,), (1,)), ((), ())), preferred_element_type=jnp.float32
    )


def norm_stats(hidden):
    mean = jnp.mean(hidden, axis=-1, keepdims=True)
    centre = hidden - mean
    spread = jnp.mean(centre * centre, axis=-1, keepdims=True)
    return mean, lax.rsqrt(spread + NORM_EPS)


def norm_back(hidden, stats, gain_row, grad):
    mean, inverse = stats
    normed = (hidden - mean) * inverse
    scaled = grad * gain_row
    first = jnp.mean(scaled, axis=-1, keepdims=True)
    second = jnp.mean(scaled * normed, axis=-1, keepdims=True)
    hidden_grad = (scaled - first - normed * second) * inverse
    return hidden_grad, jnp.sum(grad * normed, axis=0), jnp.sum(grad, axis=0)


def gelu_and_slope(values):
    size = jnp.abs(values) * (0.5**0.5)
    place = 1.0 / (1.0 + 0.5 * size)
    fit = 0.17087277
    for coefficient in (
        -0.82215223,
        1.48851587,
        -1.13520398,
        0.27886807,
        -0.18628806,
        0.09678418,
        0.37409196,
        1.00002368,
        -1.26551223,
    ):
        fit = fit * place + coefficient
    bell = jnp.exp(-size * size)
    tail = 0.5 * place * bell * jnp.exp(fit)
    below = jnp.where(values >= 0.0, 1.0 - tail, tail)
    return values * below, below + values * bell * (1.0 / math.sqrt(2.0 * math.pi))


def dot_rows(left_side, right_side):
    return lax.dot_general(
        left_side, right_side, (((1,), (1,)), ((), ())), preferred_element_type=jnp.float32
    )


def lookup(table, index):
    return jnp.take_along_axis(table, index, axis=1, mode="promise_in_bounds")


def wide(column):
    return jnp.broadcast_to(column, (column.shape[0], LANES))


def tiled(block, key_count):
    return jnp.concatenate([block] * (key_count // LANES), axis=1)


def row_blocks(main_count, key_count, size):
    blocks = [(at, min(size, main_count - at), key_count) for at in range(0, main_count, size)]
    step = min(size, LANES)
    for at in range(0, key_count, step):
        seen = min(key_count, (at + step + LANES - 1) // LANES * LANES)
        blocks.append((main_count + at, min(step, key_count - at), seen))
    return blocks


def bias_of(near_bias, far_bias, edge, row_count, key_count):
    lane = lax.broadcasted_iota(jnp.int32, (row_count, LANES), 1)
    return jnp.concatenate(
        [
            jnp.where(lane + at > edge, near_bias, far_bias)
            for at in range(0, key_count, LANES)
        ],
        axis=1,
    )


def both_halves(block, head):
    lane = lax.broadcasted_iota(jnp.int32, block.shape, 1)
    turned = pltpu.roll(block, HEAD_DIM, 1)
    return jnp.where((lane < HEAD_DIM) == (head == 0), block, turned)


def self_forward_kernel(
    query_ref,
    key_ref,
    value_ref,
    own_key_ref,
    own_value_ref,
    table_ref,
    spread_ref,
    edge_ref,
    mask_ref,
    context_ref,
    log_ref,
    score_ref,
    prob_ref,
    near_ref,
    far_ref,
):
    rows, key_count = mask_ref.shape
    main_count = rows - key_count
    parity = lax.rem(pl.program_id(0), 2)
    groups = row_blocks(main_count, key_count, 512)
    chunks = row_blocks(main_count, key_count, CHUNK)
    for head in range(2):
        at = head * HEAD_DIM
        head_lanes = slice(at, at + HEAD_DIM)
        first = (parity * 2 + head) * BUCKETS
        query = query_ref[:, head_lanes] * jnp.bfloat16(SCORE_SCALE)
        keys = key_ref[:, head_lanes]
        values = value_ref[:, head_lanes]
        own_keys = own_key_ref[:, head_lanes].astype(jnp.float32)
        own_values = own_value_ref[:, head_lanes].astype(jnp.float32)
        near_ref[head] = lookup(table_ref[...], spread_ref[...] + first)
        far_ref[head] = lookup(
            table_ref[...], jnp.full((rows, LANES), first + BUCKETS - 1, jnp.int32)
        )
        own_score = wide(
            jnp.sum(query[main_count:].astype(jnp.float32) * own_keys, axis=1, keepdims=True)
        ) + lookup(table_ref[main_count:, :], jnp.full((key_count, LANES), first, jnp.int32))
        for row, count, seen in groups:
            score_ref[head, row : row + count, 0:seen] = dot_rows(
                query[row : row + count], keys[0:seen]
            )
        tops = []
        for row, count, seen in chunks:
            part = slice(row, row + count)
            scores = (
                score_ref[head, part, 0:seen]
                + bias_of(near_ref[head, part], far_ref[head, part], edge_ref[part], count, seen)
                + mask_ref[part, 0:seen]
            )
            score_ref[head, part, 0:seen] = scores
            tops.append(wide(jnp.max(scores, axis=1, keepdims=True)))
        top = jnp.concatenate(tops, axis=0)
        top = jnp.concatenate(
            [top[:main_count], jnp.maximum(top[main_count:], own_score)], axis=0
        )
        own_weight = jnp.exp(own_score - top[main_count:])
        totals = []
        for row, count, seen in chunks:
            part = slice(row, row + count)
            weights = jnp.exp(score_ref[head, part, 0:seen] - tiled(top[part], seen))
            score_ref[head, part, 0:seen] = weights
            totals.append(wide(jnp.sum(weights, axis=1, keepdims=True)))
        total = jnp.concatenate(totals, axis=0)
        total = jnp.concatenate([total[:main_count], total[main_count:] + own_weight], axis=0)
        inverse = 1.0 / total
        log_ref[:, head_lanes] = (top + jnp.log(total))[:, 0:HEAD_DIM]
        own_prob = (own_weight * inverse[main_count:]).astype(jnp.bfloat16).astype(jnp.float32)
        for row, count, seen in chunks:
            part = slice(row, row + count)
            prob_ref[head, part, 0:seen] = (
                score_ref[head, part, 0:seen] * tiled(inverse[part], seen)
            ).astype(jnp.bfloat16)
        for row, count, seen in groups:
            part = slice(row, row + count)
            context = matmul(prob_ref[head, part, 0:seen], values[0:seen])
            if row >= main_count:
                own = slice(row - main_count, row - main_count + count)
                context = context + own_prob[own, 0:HEAD_DIM] * own_values[own]
            context_ref[part, head_lanes] = context.astype(jnp.bfloat16)


def self_backward_kernel(
    query_ref,
    key_ref,
    value_ref,
    own_key_ref,
    own_value_ref,
    table_ref,
    spread_ref,
    edge_ref,
    turn_ref,
    mask_ref,
    log_ref,
    context_ref,
    query_grad_ref,
    key_grad_ref,
    value_grad_ref,
    table_grad_ref,
    score_ref,
    prob_grad_ref,
    prob_ref,
    score_grad_ref,
    near_ref,
    far_ref,
    close_ref,
    rest_ref,
):
    rows, key_count = mask_ref.shape
    main_count = rows - key_count
    parity = lax.rem(pl.program_id(0), 2)
    groups = row_blocks(main_count, key_count, 512)
    chunks = row_blocks(main_count, key_count, CHUNK)
    bucket = bucket_of(lax.broadcasted_iota(jnp.int32, (LANES, LANES), 0))
    bucket_lane = lax.broadcasted_iota(jnp.int32, (LANES, LANES), 1)
    row_lane = lax.broadcasted_iota(jnp.int32, (rows, LANES), 1)
    table_total = jnp.zeros((rows, LANES), jnp.float32)
    own_total = jnp.zeros((key_count, LANES), jnp.float32)
    for head in range(2):
        at = head * HEAD_DIM
        head_lanes = slice(at, at + HEAD_DIM)
        first = (parity * 2 + head) * BUCKETS
        query = query_ref[:, head_lanes] * jnp.bfloat16(SCORE_SCALE)
        keys = key_ref[:, head_lanes]
        values = value_ref[:, head_lanes]
        context = context_ref[:, head_lanes]
        own_keys = own_key_ref[:, head_lanes].astype(jnp.float32)
        own_values = own_value_ref[:, head_lanes].astype(jnp.float32)
        own_query = query[main_count:].astype(jnp.float32)
        own_context = context[main_count:].astype(jnp.float32)
        near_ref[head] = lookup(table_ref[...], spread_ref[...] + first)
        far_ref[head] = lookup(
            table_ref[...], jnp.full((rows, LANES), first + BUCKETS - 1, jnp.int32)
        )
        own_score = wide(jnp.sum(own_query * own_keys, axis=1, keepdims=True)) + lookup(
            table_ref[main_count:, :], jnp.full((key_count, LANES), first, jnp.int32)
        )
        log_total = both_halves(log_ref[...], head)
        own_prob = jnp.exp(own_score - log_total[main_count:])
        own_prob_grad = wide(jnp.sum(own_context * own_values, axis=1, keepdims=True))
        value_grad_ref[key_count:, head_lanes] = (
            own_prob[:, 0:HEAD_DIM].astype(jnp.bfloat16).astype(jnp.float32) * own_context
        ).astype(jnp.bfloat16)
        for row, count, seen in groups:
            part = slice(row, row + count)
            score_ref[head, part, 0:seen] = dot_rows(query[part], keys[0:seen])
            prob_grad_ref[head, part, 0:seen] = dot_rows(context[part], values[0:seen])
        row_dots = []
        for row, count, seen in chunks:
            part = slice(row, row + count)
            edge = edge_ref[part]
            bias = bias_of(near_ref[head, part], far_ref[head, part], edge, count, seen)
            probs = jnp.exp(
                score_ref[head, part, 0:seen]
                + bias
                + (mask_ref[part, 0:seen] - tiled(log_total[part], seen))
            )
            prob_grad = prob_grad_ref[head, part, 0:seen]
            row_dot = wide(jnp.sum(probs * prob_grad, axis=1, keepdims=True))
            if row >= main_count:
                own = slice(row - main_count, row - main_count + count)
                row_dot = row_dot + own_prob[own] * own_prob_grad[own]
                row_dots.append(row_dot)
            score_grad = (probs * (prob_grad - tiled(row_dot, seen))).astype(jnp.bfloat16)
            prob_ref[head, part, 0:seen] = probs.astype(jnp.bfloat16)
            score_grad_ref[head, part, 0:seen] = score_grad
            score_wide = score_grad.astype(jnp.float32)
            lane = lax.broadcasted_iota(jnp.int32, (count, LANES), 1)
            close = jnp.zeros((count, LANES), jnp.float32)
            whole = jnp.zeros((count, LANES), jnp.float32)
            for at_key in range(0, seen, LANES):
                block = score_wide[:, at_key : at_key + LANES]
                whole = whole + block
                close = close + jnp.where(lane + at_key > edge, block, 0.0)
            close_ref[head, part] = close
            rest_ref[head, part] = whole - close
        own_grad = (
            (own_prob * (own_prob_grad - jnp.concatenate(row_dots, axis=0)))
            .astype(jnp.bfloat16)
            .astype(jnp.float32)
        )
        key_grad_ref[key_count:, head_lanes] = (own_grad[:, 0:HEAD_DIM] * own_query).astype(
            jnp.bfloat16
        )
        turned = lookup(close_ref[head], turn_ref[...]).astype(jnp.bfloat16)
        table_total = table_total + matmul(
            turned, (bucket_lane == bucket + first).astype(jnp.bfloat16)
        )
        table_total = table_total + jnp.where(
            row_lane == first + BUCKETS - 1, jnp.sum(rest_ref[head], axis=1, keepdims=True), 0.0
        )
        own_total = own_total + jnp.where(row_lane[main_count:] == first, own_grad, 0.0)
        for row, count, seen in groups:
            part = slice(row, row + count)
            query_grad = matmul(score_grad_ref[head, part, 0:seen], keys[0:seen])
            if row >= main_count:
                own = slice(row - main_count, row - main_count + count)
                query_grad = query_grad + own_grad[own, 0:HEAD_DIM] * own_keys[own]
            query_grad_ref[part, head_lanes] = (query_grad * SCORE_SCALE).astype(jnp.bfloat16)
        for at_key in range(0, key_count, LANES):
            block = slice(at_key, at_key + LANES)
            later = slice(main_count + at_key, rows)
            key_grad_ref[block, head_lanes] = (
                outer_sum(score_grad_ref[head, 0:main_count, block], query[0:main_count])
                + outer_sum(score_grad_ref[head, later, block], query[later])
            ).astype(jnp.bfloat16)
            value_grad_ref[block, head_lanes] = (
                outer_sum(prob_ref[head, 0:main_count, block], context[0:main_count])
                + outer_sum(prob_ref[head, later, block], context[later])
            ).astype(jnp.bfloat16)
    table_total = jnp.concatenate(
        [table_total[:main_count], table_total[main_count:] + own_total], axis=0
    )

    @pl.when(parity == 0)
    def first_pair():
        table_grad_ref[...] = table_total

    @pl.when(parity == 1)
    def second_pair():
        table_grad_ref[...] += table_total


def cross_forward_kernel(
    query_ref, key_ref, value_ref, mask_ref, context_ref, log_ref, score_ref, prob_ref
):
    rows = mask_ref.shape[0]
    for head in range(2):
        at = head * HEAD_DIM
        head_lanes = slice(at, at + HEAD_DIM)
        query = query_ref[:, head_lanes] * jnp.bfloat16(SCORE_SCALE)
        score_ref[head] = dot_rows(query, key_ref[:, head_lanes])
        for row in range(0, rows, CHUNK):
            part = slice(row, min(row + CHUNK, rows))
            scores = score_ref[head, part] + mask_ref[part]
            top = jnp.max(scores, axis=1, keepdims=True)
            weights = jnp.exp(scores - top)
            total = jnp.sum(weights, axis=1, keepdims=True)
            prob_ref[head, part] = (weights * (1.0 / total)).astype(jnp.bfloat16)
            log_ref[part, head_lanes] = jnp.broadcast_to(
                top + jnp.log(total), (scores.shape[0], HEAD_DIM)
            )
        context_ref[:, head_lanes] = matmul(prob_ref[head], value_ref[:, head_lanes]).astype(
            jnp.bfloat16
        )


def cross_backward_kernel(
    query_ref,
    key_ref,
    value_ref,
    mask_ref,
    log_ref,
    context_ref,
    query_grad_ref,
    key_grad_ref,
    value_grad_ref,
    score_ref,
    prob_grad_ref,
    prob_ref,
    score_grad_ref,
):
    rows = mask_ref.shape[0]
    for head in range(2):
        at = head * HEAD_DIM
        head_lanes = slice(at, at + HEAD_DIM)
        query = query_ref[:, head_lanes] * jnp.bfloat16(SCORE_SCALE)
        keys = key_ref[:, head_lanes]
        context = context_ref[:, head_lanes]
        score_ref[head] = dot_rows(query, keys)
        prob_grad_ref[head] = dot_rows(context, value_ref[:, head_lanes])
        for row in range(0, rows, CHUNK):
            part = slice(row, min(row + CHUNK, rows))
            probs = jnp.exp(
                score_ref[head, part] + (mask_ref[part] - log_ref[part, at : at + 1])
            )
            prob_grad = prob_grad_ref[head, part]
            row_dot = jnp.sum(probs * prob_grad, axis=1, keepdims=True)
            prob_ref[head, part] = probs.astype(jnp.bfloat16)
            score_grad_ref[head, part] = (probs * (prob_grad - row_dot)).astype(jnp.bfloat16)
        query_grad_ref[:, head_lanes] = (matmul(score_grad_ref[head], keys) * SCORE_SCALE).astype(
            jnp.bfloat16
        )
        key_grad_ref[:, head_lanes] = outer_sum(score_grad_ref[head], query).astype(jnp.bfloat16)
        value_grad_ref[:, head_lanes] = outer_sum(prob_ref[head], context).astype(jnp.bfloat16)


def pair_block(row_count, row_block=0, first_pair=0):
    return pl.BlockSpec((row_count, LANES), lambda pair: (row_block, first_pair + pair))


def whole_block(shape):
    return pl.BlockSpec(shape, lambda pair: (0, 0))


def attention_call(kernel, name, in_specs, out_specs, out_shape, scratch, arrays, flops, passes):
    moved = sum(array.size * array.dtype.itemsize for array in arrays)
    moved += sum(math.prod(shape.shape) * shape.dtype.itemsize for shape in out_shape)
    return pl.pallas_call(
        kernel,
        grid=(HEADS // 2,),
        in_specs=in_specs,
        out_specs=out_specs,
        out_shape=out_shape,
        scratch_shapes=scratch,
        compiler_params=pltpu.CompilerParams(vmem_limit_bytes=56 * 2**20),
        cost_estimate=pl.CostEstimate(flops=flops, bytes_accessed=moved, transcendentals=passes),
        name=name,
    )(*arrays)


def low_array(row_count):
    return jax.ShapeDtypeStruct((row_count, D), jnp.bfloat16)


def self_forward(query, pairs, table, spread, edge, mask):
    rows, keys = mask.shape
    width = D // LANES
    square = pltpu.VMEM((2, rows, keys), jnp.float32)
    narrow = pltpu.VMEM((2, rows, LANES), jnp.float32)
    return attention_call(
        self_forward_kernel,
        "self_forward",
        [
            pair_block(rows),
            pair_block(keys),
            pair_block(keys, 0, width),
            pair_block(keys, 1),
            pair_block(keys, 1, width),
            pl.BlockSpec((rows, LANES), lambda pair: (0, pair // 2)),
            whole_block((rows, LANES)),
            whole_block((rows, LANES)),
            whole_block((rows, keys)),
        ],
        [pair_block(rows), pair_block(rows)],
        [low_array(rows), jax.ShapeDtypeStruct((rows, D), jnp.float32)],
        [square, pltpu.VMEM((2, rows, keys), jnp.bfloat16), narrow, narrow],
        (query, pairs, pairs, pairs, pairs, table, spread, edge, mask),
        4 * rows * keys * D,
        rows * keys * HEADS,
    )


def self_backward(query, pairs, table, spread, edge, turn, mask, log_total, context_grad):
    rows, keys = mask.shape
    width = D // LANES
    square = pltpu.VMEM((2, rows, keys), jnp.float32)
    square_low = pltpu.VMEM((2, rows, keys), jnp.bfloat16)
    narrow = pltpu.VMEM((2, rows, LANES), jnp.float32)
    table_block = pl.BlockSpec((rows, LANES), lambda pair: (0, pair // 2))
    return attention_call(
        self_backward_kernel,
        "self_backward",
        [
            pair_block(rows),
            pair_block(keys),
            pair_block(keys, 0, width),
            pair_block(keys, 1),
            pair_block(keys, 1, width),
            table_block,
            whole_block((rows, LANES)),
            whole_block((rows, LANES)),
            whole_block((rows, LANES)),
            whole_block((rows, keys)),
            pair_block(rows),
            pair_block(rows),
        ],
        [pair_block(rows), pair_block(2 * keys), pair_block(2 * keys), table_block],
        [
            low_array(rows),
            low_array(2 * keys),
            low_array(2 * keys),
            jax.ShapeDtypeStruct(table.shape, jnp.float32),
        ],
        [square, square, square_low, square_low, narrow, narrow, narrow, narrow],
        (query, pairs, pairs, pairs, pairs, table, spread, edge, turn, mask, log_total, context_grad),
        10 * rows * keys * D,
        rows * keys * HEADS,
    )


def cross_forward(query, pairs, mask):
    rows, keys = mask.shape
    return attention_call(
        cross_forward_kernel,
        "cross_forward",
        [
            pair_block(rows),
            pair_block(keys),
            pair_block(keys, 0, D // LANES),
            whole_block((rows, keys)),
        ],
        [pair_block(rows), pair_block(rows)],
        [low_array(rows), jax.ShapeDtypeStruct((rows, D), jnp.float32)],
        [pltpu.VMEM((2, rows, keys), jnp.float32), pltpu.VMEM((2, rows, keys), jnp.bfloat16)],
        (query, pairs, pairs, mask),
        4 * rows * keys * D,
        rows * keys * HEADS,
    )


def cross_backward(query, pairs, mask, log_total, context_grad):
    rows, keys = mask.shape
    square = pltpu.VMEM((2, rows, keys), jnp.float32)
    square_low = pltpu.VMEM((2, rows, keys), jnp.bfloat16)
    return attention_call(
        cross_backward_kernel,
        "cross_backward",
        [
            pair_block(rows),
            pair_block(keys),
            pair_block(keys, 0, D // LANES),
            whole_block((rows, keys)),
            pair_block(rows),
            pair_block(rows),
        ],
        [pair_block(rows), pair_block(keys), pair_block(keys)],
        [low_array(rows), low_array(keys), low_array(keys)],
        [square, square, square_low, square_low],
        (query, pairs, pairs, mask, log_total, context_grad),
        10 * rows * keys * D,
        rows * keys * HEADS,
    )


def column_sums(left_side, right_side):
    return outer_sum(left_side, right_side).astype(jnp.bfloat16)


def inner_levels(dp_count):
    levels = [("dp", 1, 2), ("stream", 1, 2)]
    if dp_count == 64:
        return levels + [("dp", 2, 2), ("dp", 4, 4)]
    return levels + [("dp", 2, 2)]


def rotation(level, shift, dp_count):
    axis, stride, size = level
    total = 2 if axis == "stream" else dp_count
    pairs = []
    for source in range(total):
        place = (source // stride) % size
        target = source + ((place + shift) % size - place) * stride
        pairs.append((source, target))
    return pairs


def place_on(level):
    axis, stride, size = level
    return (lax.axis_index(axis) // stride) % size


def pick(stacked, index, dim):
    return lax.dynamic_index_in_dim(stacked, index, dim, keepdims=False)


def scatter_level(stacked, dim, level, dp_count, final_type):
    axis, stride, size = level
    mine = place_on(level)
    total = pick(stacked, mine, dim).astype(jnp.float32)
    for shift in range(1, size):
        sent = pick(stacked, (mine + shift) % size, dim)
        came = lax.ppermute(sent, axis, rotation(level, shift, dp_count))
        total = total + came.astype(jnp.float32)
    return total.astype(final_type)


class Scatter:
    def __init__(self, rows, outer_range, dp_count, parts=2):
        self.levels = inner_levels(dp_count)
        self.inner = self.levels[2:]
        self.outer_range = outer_range
        self.dp_count = dp_count
        self.parts = parts
        sizes = [size for axis, stride, size in reversed(self.inner)]
        self.block = rows.shape[0] // (len(outer_range) * math.prod(sizes) * 4)
        self.state = [
            rows.reshape([len(outer_range)] + sizes + [2, 2, self.block, rows.shape[1]])
        ]
        self.done = 0

    def step(self):
        inner_count = len(self.inner)
        if self.done == 0:
            stacked = scatter_level(
                self.state[0], 1 + inner_count, self.levels[0], self.dp_count, jnp.bfloat16
            )
            if self.parts == 1:
                self.state = [stacked]
            else:
                cut = (self.block // 2 + 15) // 16 * 16
                self.state = [stacked[..., :cut, :], stacked[..., cut:, :]]
            order = [self.levels[1]] + self.inner
            other = [self.inner[0], self.levels[1]] + self.inner[1:]
            self.orders = [order, other]
            self.names = [list(reversed(self.inner)) + [self.levels[1]] for part in range(2)]
        elif self.done <= inner_count + 1:
            for part in range(self.parts):
                level = self.orders[part][self.done - 1]
                dim = 1 + self.names[part].index(level)
                self.names[part].remove(level)
                self.state[part] = scatter_level(
                    self.state[part], dim, level, self.dp_count, jnp.bfloat16
                )
        else:
            self.state = [self.outer_step(piece) for piece in self.state]
        self.done += 1

    def outer_step(self, piece):
        level = ("dp", self.dp_count // 4, 4)
        mine = place_on(level)
        first, count = self.outer_range[0], len(self.outer_range)
        total = pick(piece, jnp.clip(mine - first, 0, count - 1), 0).astype(jnp.float32)
        for shift in range(1, 4):
            pairs = [
                pair
                for pair in rotation(level, shift, self.dp_count)
                if pair[1] // level[1] in self.outer_range
            ]
            target = jnp.clip((mine + shift) % 4 - first, 0, count - 1)
            total = total + lax.ppermute(pick(piece, target, 0), "dp", pairs).astype(jnp.float32)
        return total

    def finish(self):
        while self.done < len(self.inner) + 3:
            self.step()
        return jnp.concatenate(self.state)


def after(value, *scatters):
    states = [array for scatter in scatters for array in scatter.state]
    return lax.optimization_barrier((value, *states))[0]


def to_all(part, count):
    shared = jnp.broadcast_to(part[None], (count, *part.shape))
    gathered = lax.all_to_all(shared, ("dp", "stream"), 0, 0, tiled=True)
    return gathered.reshape(-1, *part.shape[1:])


def swap_streams(rows):
    return lax.ppermute(rows, "stream", [(0, 1), (1, 0)])


def both_parts(rows):
    other = swap_streams(rows)
    leading = lax.axis_index("stream") == 0
    return jnp.concatenate(
        [jnp.where(leading, rows, other), jnp.where(leading, other, rows)], axis=0
    )


def pair_sum(rows):
    half = rows.shape[0] // 2
    stream = lax.axis_index("stream")
    sent = lax.dynamic_slice_in_dim(rows, (1 - stream) * half, half).astype(jnp.bfloat16)
    return lax.dynamic_slice_in_dim(rows, stream * half, half) + swap_streams(sent).astype(
        jnp.float32
    )


def adam_step(master, first_moment, second_moment, gradient, step_rate, step_decay):
    first_new = BETA_FIRST * first_moment + (1.0 - BETA_FIRST) * gradient
    second_new = BETA_SECOND * second_moment + (1.0 - BETA_SECOND) * gradient * gradient
    first_hat = first_new / (1.0 - BETA_FIRST**STEP)
    second_hat = second_new / (1.0 - BETA_SECOND**STEP)
    master_new = master - step_rate * (
        first_hat / (jnp.sqrt(second_hat) + ADAM_EPS) + step_decay * master
    )
    return (master_new, first_new, second_new)


def local(
    dp_count,
    main_rows,
    pred_rows,
    enc_rows,
    doc_lengths,
    main_cotangent,
    pred_cotangent,
    proj_master,
    proj_first,
    proj_second,
    bias_master,
    bias_first,
    bias_second,
    down_master,
    down_first,
    down_second,
    small_master,
    small_first,
    small_second,
):
    devices = 2 * dp_count
    rel_width = BUCKETS * HEADS
    cross_start = 4 * D + rel_width
    half_rows = main_rows.shape[0]
    group_rows = pred_rows.shape[0]

    bias_wide = to_all(bias_master.astype(jnp.bfloat16), devices).astype(jnp.float32)
    proj_rows = lax.all_gather(
        proj_master.astype(jnp.bfloat16).T, ("dp", "stream"), axis=0, tiled=True
    )
    down_weight = lax.all_gather(
        down_master.astype(jnp.bfloat16), ("dp", "stream"), axis=0, tiled=True
    )
    query_weight = proj_rows[0:D]
    keys_weight = proj_rows[D : 3 * D]
    out_weight = proj_rows[3 * D : 4 * D]
    table_weight = (
        proj_rows[4 * D : cross_start]
        .reshape(BUCKETS, HEADS, D)
        .transpose(1, 0, 2)
        .reshape(rel_width, D)
    )
    cross_weight = proj_rows[cross_start : cross_start + D]
    pair_weight = proj_rows[cross_start + D : cross_start + 3 * D]
    back_weight = proj_rows[cross_start + 3 * D : cross_start + 4 * D]
    up_weight = proj_rows[cross_start + 4 * D :]
    query_bias = bias_wide[0:D]
    value_bias = bias_wide[D : 2 * D]
    out_bias = bias_wide[2 * D : 3 * D]
    table_bias = bias_wide[3 * D : 3 * D + rel_width].reshape(BUCKETS, HEADS).T.reshape(rel_width)
    cross_bias = bias_wide[3 * D + rel_width : 4 * D + rel_width]
    pair_bias = bias_wide[4 * D + rel_width : 5 * D + rel_width]
    back_bias = bias_wide[5 * D + rel_width : 6 * D + rel_width]
    up_bias = bias_wide[6 * D + rel_width :]
    zero_bias = jnp.zeros((D,), jnp.float32)

    main_start = lax.axis_index("stream") * half_rows
    places = jnp.arange(group_rows, dtype=jnp.int32)
    group_docs = doc_ids(doc_lengths[0], group_rows)
    query_docs = jnp.concatenate(
        [lax.dynamic_slice_in_dim(group_docs, main_start, half_rows), group_docs]
    )
    query_places = jnp.concatenate([main_start + jnp.arange(half_rows, dtype=jnp.int32), places])
    main_flag = jnp.arange(half_rows + group_rows, dtype=jnp.int32) < half_rows
    same_doc = query_docs[:, None] == group_docs[None, :]
    distance = query_places[:, None] - places[None, :]
    allowed = same_doc & ((distance > 0) | (distance == 0) & main_flag[:, None])
    self_mask = jnp.where(allowed, 0.0, MASKED)
    cross_mask = jnp.where(same_doc, 0.0, MASKED)
    lane = jnp.arange(LANES, dtype=jnp.int32)
    turn = jnp.mod(query_places[:, None] - lane[None, :], LANES)
    spread = bucket_of(turn)
    edge = jnp.broadcast_to(query_places[:, None] - LANES, turn.shape)

    main_all = both_parts(main_rows)
    enc_all = both_parts(enc_rows)
    inputs = jnp.concatenate([main_rows, pred_rows], axis=0)
    key_inputs = jnp.concatenate([main_all, pred_rows], axis=0)
    input_values = inputs.astype(jnp.float32)
    query_low = (times_transpose(inputs, query_weight) + query_bias).astype(jnp.bfloat16)
    self_pairs = (
        times_transpose(key_inputs, keys_weight) + jnp.concatenate([zero_bias, value_bias])
    ).astype(jnp.bfloat16)
    table = times_transpose(inputs, table_weight) + table_bias
    cross_pairs = (
        times_transpose(enc_all, pair_weight) + jnp.concatenate([zero_bias, pair_bias])
    ).astype(jnp.bfloat16)
    context_low, self_log = self_forward(query_low, self_pairs, table, spread, edge, self_mask)
    norm_one_in = input_values + times_transpose(context_low, out_weight) + out_bias
    stats_one = norm_stats(norm_one_in)
    hidden_one = (norm_one_in - stats_one[0]) * stats_one[1] * small_master[1] + small_master[4]
    one_low = hidden_one.astype(jnp.bfloat16)

    cross_query = (times_transpose(one_low, cross_weight) + cross_bias).astype(jnp.bfloat16)
    cross_low, cross_log = cross_forward(cross_query, cross_pairs, cross_mask)
    norm_two_in = hidden_one + times_transpose(cross_low, back_weight) + back_bias
    stats_two = norm_stats(norm_two_in)
    hidden_two = (norm_two_in - stats_two[0]) * stats_two[1] * small_master[2] + small_master[5]
    two_low = hidden_two.astype(jnp.bfloat16)

    active, slope = gelu_and_slope(times_transpose(two_low, up_weight) + up_bias)
    active_low = active.astype(jnp.bfloat16)
    slope_low = slope.astype(jnp.bfloat16)
    norm_three_in = hidden_two + matmul(active_low, down_weight) + small_master[0]
    stats_three = norm_stats(norm_three_in)
    final_rows = (
        (norm_three_in - stats_three[0]) * stats_three[1] * small_master[3] + small_master[6]
    ).astype(jnp.bfloat16)

    cotangent = jnp.concatenate([main_cotangent, pred_cotangent], axis=0).astype(jnp.float32)
    sum_three, gain_three, shift_three = norm_back(
        norm_three_in, stats_three, small_master[3], cotangent
    )
    ffn_grad = sum_three.astype(jnp.bfloat16)
    slab = proj_rows.shape[0] // 4
    down_sum = Scatter(column_sums(active_low, ffn_grad), range(4), dp_count)
    down_sum.step()
    pre_grad = (times_transpose(ffn_grad, down_weight) * slope_low.astype(jnp.float32)).astype(
        jnp.bfloat16
    )
    pre_grad = after(pre_grad, down_sum)
    up_cut = 3 * slab - cross_start - 4 * D
    slab_three = Scatter(column_sums(pre_grad[:, up_cut:], two_low), range(3, 4), dp_count)
    up_rows = column_sums(pre_grad[:, :up_cut], two_low)
    down_sum.step()
    slab_three.step()
    two_grad = sum_three + matmul(pre_grad, up_weight)
    two_grad = after(two_grad, slab_three)

    sum_two, gain_two, shift_two = norm_back(norm_two_in, stats_two, small_master[2], two_grad)
    branch_grad = sum_two.astype(jnp.bfloat16)
    cross_low_grad = matmul(branch_grad, back_weight).astype(jnp.bfloat16)
    cross_low_grad = after(cross_low_grad, down_sum)
    down_sum.step()
    slab_three.step()
    back_rows = column_sums(branch_grad, cross_low)
    cquery_grad, ckey_grad, cvalue_grad = cross_backward(
        cross_query, cross_pairs, cross_mask, cross_log, cross_low_grad
    )
    cquery_grad = after(cquery_grad, down_sum, slab_three)
    down_sum.step()
    slab_three.step()
    ckey_rows = column_sums(ckey_grad, enc_all)
    cvalue_rows = column_sums(cvalue_grad, enc_all)
    enc_grad = pair_sum(matmul(ckey_grad, pair_weight[:D]) + matmul(cvalue_grad, pair_weight[D:]))
    one_grad = sum_two + matmul(cquery_grad, cross_weight)

    sum_one, gain_one, shift_one = norm_back(norm_one_in, stats_one, small_master[1], one_grad)
    attn_grad = sum_one.astype(jnp.bfloat16)
    out_rows = column_sums(attn_grad, context_low)
    out_cut = slab - 3 * D
    ckey_cut = 2 * slab - cross_start - D
    slab_middle = Scatter(
        jnp.concatenate(
            [
                out_rows[out_cut:],
                jnp.zeros((rel_width, D), jnp.bfloat16),
                column_sums(cquery_grad, one_low),
                ckey_rows,
                cvalue_rows,
                back_rows,
                up_rows,
            ]
        ),
        range(1, 3),
        dp_count,
    )
    slab_middle.step()
    context_grad = matmul(attn_grad, out_weight).astype(jnp.bfloat16)
    context_grad = after(context_grad, slab_middle, slab_three)
    slab_middle.step()
    slab_three.step()
    query_grad, key_grad, value_grad, table_wide = self_backward(
        query_low, self_pairs, table, spread, edge, turn, self_mask, self_log, context_grad
    )
    table_wide = after(table_wide, slab_middle, slab_three)
    slab_middle.step()
    table_grad = table_wide.astype(jnp.bfloat16)
    table_sum = Scatter(column_sums(table_grad, inputs), range(4), dp_count, 1)
    slab_zero = Scatter(
        jnp.concatenate(
            [
                column_sums(query_grad, inputs),
                column_sums(key_grad, key_inputs),
                column_sums(value_grad, key_inputs),
                out_rows[:out_cut],
            ]
        ),
        range(0, 1),
        dp_count,
    )
    device = lax.axis_index("dp") * 2 + lax.axis_index("stream")
    table_total = (
        to_all(table_sum.finish().astype(jnp.bfloat16), devices)
        .reshape(HEADS, BUCKETS, D)
        .transpose(1, 0, 2)
        .reshape(rel_width, D)
        .astype(jnp.float32)
    )
    shard = proj_rows.shape[0] // devices
    table_part = lax.dynamic_slice_in_dim(
        jnp.pad(table_total, ((shard, shard), (0, 0))),
        jnp.clip((device + 1) * shard - 4 * D, 0, rel_width + shard),
        shard,
    )
    pair_input_grad = matmul(key_grad, keys_weight[:D]) + matmul(value_grad, keys_weight[D:])
    query_input_grad = (
        sum_one + matmul(query_grad, query_weight) + matmul(table_grad, table_weight)
    )
    main_grad = query_input_grad[:half_rows] + pair_sum(pair_input_grad[:group_rows])
    pred_grad = query_input_grad[half_rows:] + pair_input_grad[group_rows:]

    def row_sum(rows):
        return jnp.sum(rows, axis=0, dtype=jnp.float32)

    bias_parts = jnp.concatenate(
        [
            row_sum(query_grad),
            row_sum(value_grad),
            row_sum(attn_grad),
            row_sum(table_grad).reshape(HEADS, BUCKETS).T.reshape(rel_width),
            row_sum(cquery_grad),
            row_sum(cvalue_grad),
            row_sum(branch_grad),
            row_sum(pre_grad),
        ]
    )
    small_parts = jnp.concatenate(
        [row_sum(ffn_grad), gain_one, gain_two, gain_three, shift_one, shift_two, shift_three]
    )
    vector_parts = jnp.concatenate(
        [bias_parts.reshape(devices, -1), small_parts.reshape(devices, -1)], axis=1
    )
    vector_sum = jnp.sum(
        lax.all_to_all(vector_parts, ("dp", "stream"), 0, 0, tiled=True), axis=0
    )
    bias_len = bias_master.shape[0]
    bias_grad = vector_sum[:bias_len]
    small_grad = to_all(vector_sum[bias_len:], devices).reshape(small_master.shape)

    outer = place_on(("dp", dp_count // 4, 4))
    proj_sum = jnp.where(
        outer == 0,
        slab_zero.finish(),
        jnp.where(outer == 3, slab_three.finish(), slab_middle.finish()),
    )
    proj_grad = (proj_sum + table_part).T
    down_grad = down_sum.finish()
    return (
        final_rows[:half_rows],
        final_rows[half_rows:],
        main_grad.astype(jnp.bfloat16),
        pred_grad.astype(jnp.bfloat16),
        enc_grad.astype(jnp.bfloat16),
        *adam_step(proj_master, proj_first, proj_second, proj_grad, RATE_MATRIX, WEIGHT_DECAY),
        *adam_step(bias_master, bias_first, bias_second, bias_grad, RATE_VECTOR, 0.0),
        *adam_step(down_master, down_first, down_second, down_grad, RATE_MATRIX, WEIGHT_DECAY),
        *adam_step(small_master, small_first, small_second, small_grad, RATE_SMALL, 0.0),
    )


def solution(mesh):
    rows = P(("dp", "stream"), None)
    columns = P(None, ("dp", "stream"))
    vector = P(("dp", "stream"))
    masters = (columns,) * 3 + (vector,) * 3 + (rows,) * 3 + (P(),) * 3
    return jax.shard_map(
        partial(local, mesh.shape["dp"]),
        mesh=mesh,
        in_specs=(rows, rows, rows, P("dp", None), rows, rows) + masters,
        out_specs=(rows,) * 5 + masters,
        check_vma=False,
    )
```

time: 3110 us -> 1000 us (0.32)
  waiting for transfers between devices: 1560 us -> 257 us
  matrix products: 866 us -> 232 us
  local copies, waits for them, and re-layouts: 339 us -> 64.4 us
  Pallas kernels: 0 us -> 176 us
  other arithmetic: 273 us -> 119 us
  starting transfers between devices: 1 us -> 126 us
  blocking collectives: 41.5 us -> 0 us
    unnamed x19 -> x2, waiting for transfers between devices: 1130 us -> 0.03 us
    dot_general x60 -> x0, matrix products: 620 us -> none  [the longest x8 411 us: self_scores(): jnp.einsum('hqd,hkd->hqk', query_heads, key_heads, preferred_element_type...]
    reduce_scatter x1 -> x0, waiting for transfers between devices: 307 us -> none  [local(): lax.psum_scatter(down_grad, ('dp', 'stream'), scatter_dimension=0, tiled=...]
    pallas_call x0 -> x4, Pallas kernels: none -> 176 us  [attention_call(): pl.pallas_call(kernel, grid=(HEADS // 2,), in_specs=in_specs, out_specs=o...]
    and x8 -> x0, other arithmetic: 146 us -> none  [local(): allowed = same_doc & ((distance > 0) | (distance == 0) & main_flag[:, None])]
    ppermute x0 -> x54, waiting for transfers between devices: none -> 138 us  [the longest x27 74.7 us: outer_step(): lax.ppermute(pick(piece, target, 0), 'dp', pairs).astype(jnp.float32)]
    unnamed x226 -> x205, local copies, waits for them, and re-layouts: 116 us -> 14.9 us
    ppermute x0 -> x54, starting transfers between devices: none -> 66 us  [the longest x27 42.5 us: outer_step(): lax.ppermute(pick(piece, target, 0), 'dp', pairs).astype(jnp.float32)]
  transfers between devices with their start and end apart: 13 -> 60, of which waited for: 6 -> 17; matrix products, arithmetic and copies ran while one was open for 41% -> 29% of each run, Pallas kernels for 0% -> 11%
where the time goes in v2:
time: 1000 us; the launch traced here: 991 us
  waiting for transfers between devices  257 us (26%)
  matrix products  232 us (23%)
  Pallas kernels  176 us (18%)
  starting transfers between devices  126 us (13%)
  other arithmetic  119 us (12%)
  local copies, waits for them, and re-layouts  64.4 us (6%)
  between operations  16.6 us (2%)
    pallas_call x4, Pallas kernels, attention_call(): pl.pallas_call(kernel, grid=(HEADS // 2,), in_specs=in_specs, out_specs=o...  176 us
    dot_general x9, matrix products, times_transpose(): lax.dot_general(left_side, right_side, (((1,), (1,)), ((), ())), preferre...  116 us
    all_gather x1, waiting for transfers between devices, local(): lax.all_gather(proj_master.astype(jnp.bfloat16).T, ('dp', 'stream'), axis...  115 us
    ppermute x27, waiting for transfers between devices, outer_step(): lax.ppermute(pick(piece, target, 0), 'dp', pairs).astype(jnp.float32)  74.7 us
    dot_general x11, matrix products, matmul(): return jnp.dot(left_side, right_side, preferred_element_type=jnp.float32)  65.8 us
    dot_general x12, matrix products, outer_sum(): lax.dot_general(left_side, right_side, (((0,), (0,)), ((), ())), preferre...  50.7 us
    ppermute x27, starting transfers between devices, outer_step(): lax.ppermute(pick(piece, target, 0), 'dp', pairs).astype(jnp.float32)  42.5 us
    ppermute x4, waiting for transfers between devices, swap_streams(): return lax.ppermute(rows, 'stream', [(0, 1), (1, 0)])  40.9 us
  transfers between devices with their start and end apart: 60, of which 17 were waited for; matrix products, arithmetic and copies ran while one was open for 29% of the time, Pallas kernels for 11%

profile of v2, /device:TPU:11, one launch (start us, length us, event | category | flops | bytes accessed | tf_op | source)
XLA Modules:
  0.0 991.0 jit_solution(3717191810276022547)
XLA Ops:
  12.4 6.3 all-to-all-start
  29.2 12.1 %collective-permute-done.1 = bf16[320,1024]{1,0:T(8,128)(2,1)S(1)} collective-permute-done((bf16[320,1024]{1,0:T(8,128)(2,1)}, bf16[320,1024]{1,0:T(8,128)(2,1)S(1)}, u32[]{:S(2)}, u32[]{:S(2)}) %collective-permute-start.1) | collective-permute-done | bytes 655392 | tf_op jit(solution)/shard_map/ppermute | solution.py:688
  42.1 15.8 %collective-permute-done = bf16[320,1024]{1,0:T(8,128)(2,1)} collective-permute-done((bf16[320,1024]{1,0:T(8,128)(2,1)}, bf16[320,1024]{1,0:T(8,128)(2,1)}, u32[]{:S(2)}, u32[]{:S(2)}) %collective-permute-start) | collective-permute-done | bytes 655392 | tf_op jit(solution)/shard_map/ppermute | solution.py:688
  62.6 114.7 %all-gather.3.cloned.1.call-done = bf16[12800,1024]{1,0:T(8,128)(2,1)} async-done(((bf16[400,1024]{1,0:T(8,128)(2,1)}), bf16[12800,1024]{1,0:T(8,128)(2,1)}) %all-gather.3.cloned.1.call-update) | async-done | bytes 26214416 | tf_op jit(solution)/shard_map/all_gather | solution.py:747
  179.2 4.5 convolution_add_fusion.2.table_ref
  183.7 5.8 add_convert_fusion.5.query_ref
  189.5 11.5 %add_convert_fusion.1.key_ref.value_ref.own_key_ref.own_value_ref = bf16[1280,2048]{1,0:T(8,128)(2,1)} fusion(f32[2048]{0:T(1024)S(1)} %concatenate.57, bf16[12800,1024]{1,0:T(8,128)(2,1)} %all-gather.3.cloned.1.call-done, bf16[640,1024]{1,0:T(8,128)(2,1)S(1)} %copy-done.39, bf16[320,1024]{1,0:T(8,128)(2,1)S(1)} %get-tuple-element.140, ...), kind=kOutput, calls=%fused_computation.9 | convolution fusion | flops 5381816320 | bytes 12066816 | tf_op jit(solution)/shard_map/dot_general | solution.py:59
  201.9 35.6 %self_forward.1 = (bf16[960,1024]{1,0:T(8,128)(2,1)}, f32[960,1024]{1,0:T(8,128)}) custom-call(bf16[960,1024]{1,0:T(8,128)(2,1)} %add_convert_fusion.5.query_ref, bf16[1280,2048]{1,0:T(8,128)(2,1)} %add_convert_fusion.1.key_ref.value_ref.own_key_ref.own_value_ref, bf16[1280,2048]{1,0:T(8,128)(2,1)} %add_convert_fusion.1.key_ref.value_ref.own_key_ref.own_value_ref, ...), custom_call_target="tpu_custom_call" | custom-call | flops 2516582400 | bytes 34242560 | tf_op jit(solution)/shard_map/self_forward/pallas_call | solution.py:445
  237.6 5.2 fusion.125
  245.1 7.0 add_convert_fusion.2.key_ref.value_ref
  252.0 5.1 add_convert_fusion.4.query_ref
  257.1 27.9 %cross_forward.1 = (bf16[960,1024]{1,0:T(8,128)(2,1)}, f32[960,1024]{1,0:T(8,128)}) custom-call(bf16[960,1024]{1,0:T(8,128)(2,1)} %add_convert_fusion.4.query_ref, bf16[640,2048]{1,0:T(8,128)(2,1)} %add_convert_fusion.2.key_ref.value_ref, bf16[640,2048]{1,0:T(8,128)(2,1)} %add_convert_fusion.2.key_ref.value_ref, f32[960,640]{1,0:T(8,128)} %get-tuple-element.125.mask_ref), custom_call_target="tpu_custom_call" | custom-call | flops 2516582400 | bytes 15564800 | tf_op jit(solution)/shard_map/cross_forward/pallas_call | solution.py:445
  285.1 4.8 fusion.126
  291.9 40.8 %multiply_convert_fusion.1 = (bf16[960,4096]{1,0:T(8,128)(2,1)}, f32[960,4096]{1,0:T(8,128)}) fusion(f32[4096]{0:T(1024)S(1)} %slice.212, bf16[12800,1024]{1,0:T(8,128)(2,1)} %all-gather.3.cloned.1.call-done, f32[960,1024]{1,0:T(8,128)S(1)} %get-tuple-element.132, f32[1024]{0:T(1024)S(1)} %bitcast.270, f32[1024]{0:T(1024)S(1)} %bitcast.255, ...), kind=kOutput, calls=%fused_computation.6 | convolution fusion | flops 8191672320 | bytes 35945984 | tf_op jit(solution)/shard_map/dot_general | solution.py:59
  332.8 14.2 %fusion.127 = (f32[960]{0:T(1024)S(1)}, f32[960,1024]{1,0:T(8,128)S(1)}) fusion(f32[1024]{0:T(1024)S(1)} %bitcast.277, bf16[960,4096]{1,0:T(8,128)(2,1)} %get-tuple-element.133, bf16[4096,1024]{1,0:T(8,128)(2,1)} %all-gather.5.cloned.1.call-done, f32[1024]{0:T(1024)S(1)} %bitcast.271, f32[1024]{0:T(1024)S(1)} %bitcast.256, f32[960]{0:T(1024)S(1)} %add_rsqrt_fusion.1, ...), kind=kOutput, calls=%fused_computation.321 | convolution fusion | flops 8059943936 | bytes 24141056 | tf_op jit(solution)/shard_map/dot_general | solution.py:49
  352.2 4.3 convert_reduce_fusion.3
  356.5 11.3 %convolution_convert_fusion.1 = bf16[4096,1024]{1,0:T(8,128)(2,1)} fusion(bf16[960,4096]{1,0:T(8,128)(2,1)S(1)} %bitcast.281, f32[960,1024]{1,0:T(8,128)S(1)} %get-tuple-element.77), kind=kOutput, calls=%fused_computation.13 | convolution fusion | flops 8058241024 | bytes 20185088 | tf_op jit(solution)/shard_map/dot_general | solution.py:53
  367.8 4.7 constant_dynamic-slice_fusion.3
  373.5 31.2 %multiply_convert_fusion = bf16[960,4096]{1,0:T(8,128)(2,1)} fusion(bf16[4096,1024]{1,0:T(8,128)(2,1)} %all-gather.5.cloned.1.call-done, f32[960,4096]{1,0:T(8,128)} %get-tuple-element.134, f32[4096]{0:T(1024)S(1)} %slice.212, f32[960,1024]{1,0:T(8,128)S(1)} %get-tuple-element.77), kind=kOutput, calls=%fused_computation.4 | convolution fusion | flops 8207400960 | bytes 35930112 | tf_op jit(solution)/shard_map/dot_general | solution.py:59
  411.4 9.9 %convolution_convert_fusion = bf16[3200,1024]{1,0:T(8,128)(2,1)} fusion(bf16[960,4096]{1,0:T(8,128)(2,1)S(1)} %copy-done.13, f32[960,1024]{1,0:T(8,128)S(1)} %copy-done.1, f32[1024]{0:T(1024)S(1)} %bitcast.272, f32[1024]{0:T(1024)S(1)} %bitcast.257, f32[960]{0:T(1024)S(1)} %copy-done.64, f32[960]{0:T(1024)S(1)} %copy-done.60), kind=kOutput, calls=%fused_computation.12 | convolution fusion | flops 6299648000 | bytes 16646144 | tf_op jit(solution)/shard_map/dot_general | solution.py:53
  425.6 6.4 collective-permute-done.4
  434.8 10.7 %fusion.32 = f32[960,1024]{1,0:T(8,128)S(1)} fusion(f32[960,1024]{1,0:T(8,128)S(1)} %get-tuple-element.77, bf16[960,4096]{1,0:T(8,128)(2,1)S(1)} %copy-done.13, bf16[12800,1024]{1,0:T(8,128)(2,1)} %all-gather.3.cloned.1.call-done), kind=kOutput, calls=%fused_computation.94 | convolution fusion | flops 8054046720 | bytes 24117248 | tf_op jit(solution)/shard_map/dot_general | solution.py:49
  446.8 4.5 fusion.8
  457.4 6.6 fusion.58.context_ref
  465.5 44.7 %cross_backward.1 = (bf16[960,1024]{1,0:T(8,128)(2,1)}, bf16[640,1024]{1,0:T(8,128)(2,1)}, bf16[640,1024]{1,0:T(8,128)(2,1)}) custom-call(bf16[960,1024]{1,0:T(8,128)(2,1)} %add_convert_fusion.4.query_ref, bf16[640,2048]{1,0:T(8,128)(2,1)} %add_convert_fusion.2.key_ref.value_ref, bf16[640,2048]{1,0:T(8,128)(2,1)} %add_convert_fusion.2.key_ref.value_ref, ...), custom_call_target="tpu_custom_call" | custom-call | flops 6291456000 | bytes 20152320 | tf_op jit(solution)/shard_map/cross_backward/pallas_call | solution.py:445
  514.2 6.5 multiply_reduce_fusion.1
  537.4 4.0 convert_dynamic-update-slice_fusion.4
  558.5 4.4 convert_reduce_fusion
  568.2 6.1 collective-permute-done.51
  583.8 13.1 %collective-permute-done.22 = bf16[320,1024]{1,0:T(8,128)(2,1)S(1)} collective-permute-done((bf16[320,1024]{1,0:T(8,128)(2,1)S(1)}, bf16[320,1024]{1,0:T(8,128)(2,1)S(1)}, u32[]{:S(2)}, u32[]{:S(2)}) %collective-permute-start.22) | collective-permute-done | bytes 655392 | tf_op jit(solution)/shard_map/ppermute | solution.py:688
  600.4 5.1 fusion.55.context_ref
  613.7 4.1 collective-permute-start.16
  617.8 15.6 %collective-permute-done.19 = bf16[192,1024]{1,0:T(8,128)(2,1)} collective-permute-done((bf16[192,1024]{1,0:T(8,128)(2,1)S(1)}, bf16[192,1024]{1,0:T(8,128)(2,1)}, u32[]{:S(2)}, u32[]{:S(2)}) %collective-permute-start.19) | collective-permute-done | bytes 393248 | tf_op jit(solution)/shard_map/ppermute | solution.py:667
  636.7 5.8 collective-permute-done.16
  643.8 11.2 %fusion.1 = bf16[2,2,2,400,1024]{4,3,0,2,1:T(8,128)(2,1)} fusion(bf16[2,2,2,400,1024]{4,3,0,2,1:T(8,128)(2,1)} %collective-permute-done.10, bf16[2,2,1,2,400,1024]{5,4,3,2,1,0:T(8,128)(2,1)} %get-tuple-element.83), kind=kLoop, calls=%fused_computation.8 | loop fusion | flops 13107200 | bytes 19660800 | tf_op jit(solution)/shard_map/convert_element_type | solution.py:611
  661.0 67.6 %self_backward.1 = (bf16[960,1024]{1,0:T(8,128)(2,1)}, bf16[1280,1024]{1,0:T(8,128)(2,1)}, bf16[1280,1024]{1,0:T(8,128)(2,1)}, f32[960,512]{1,0:T(8,128)}) custom-call(bf16[960,1024]{1,0:T(8,128)(2,1)} %add_convert_fusion.5.query_ref, bf16[1280,2048]{1,0:T(8,128)(2,1)} %add_convert_fusion.1.key_ref.value_ref.own_key_ref.own_value_ref, ...), custom_call_target="tpu_custom_call" | custom-call | flops 6291456000 | bytes 43909120 | tf_op jit(solution)/shard_map/self_backward/pallas_call | solution.py:445
  728.7 4.7 convolution_convert_fusion.4
  742.4 17.3 %pad_maximum_fusion = bf16[3200,1024]{1,0:T(8,128)(2,1)S(1)} fusion(bf16[128,1024]{1,0:T(8,128)(2,1)S(1)} %slice-done.2, bf16[1024,1024]{1,0:T(8,128)(2,1)S(1)} %convolution_convert_fusion.2, bf16[1024,1024]{1,0:T(8,128)(2,1)S(1)} %convolution_convert_fusion.3, bf16[1024,1024]{1,0:T(8,128)(2,1)S(1)} %convolution_convert_fusion.4), kind=kLoop, calls=%fused_computation.18 | loop fusion | flops 26214400 | bytes 13107200 | tf_op jit(solution)/shard_map/concatenate | solution.py:900
  763.0 6.3 fusion.40
  773.3 4.7 convolution_add_fusion
  791.8 24.9 %all-to-all-start.2 = ((f32[32,1,560]{2,1,0:T(1,128)}), f32[32,1,560]{2,1,0:T(1,128)S(1)}, u32[]{:S(2)}, u32[]{:S(2)}) async-start(f32[32,1,560]{2,1,0:T(1,128)} %all_to_all.19), calls=%async_computation.2 | async-start | bytes 163840 | tf_op jit(solution)/shard_map/all_to_all | solution.py:954
  825.1 17.1 %all-to-all-start.3 = ((f32[32,1,224]{2,1,0:T(1,128)}), f32[32,1,224]{2,1,0:T(1,128)S(1)}, u32[]{:S(2)}, u32[]{:S(2)}) async-start(f32[32,1,224]{2,1,0:T(1,128)} %broadcast_in_dim.26), calls=%async_computation.3 | async-start | bytes 65536 | tf_op jit(solution)/shard_map/all_to_all | solution.py:683
  873.9 11.3 %all-to-all-start.1 = ((bf16[32,16,1024]{2,1,0:T(8,128)(2,1)}), bf16[32,16,1024]{2,1,0:T(8,128)(2,1)}, u32[]{:S(2)}, u32[]{:S(2)}) async-start(bf16[32,16,1024]{2,1,0:T(8,128)(2,1)} %broadcast_in_dim.25), calls=%async_computation.1 | async-start | bytes 2097152 | tf_op jit(solution)/shard_map/all_to_all | solution.py:683
  895.3 13.3 %collective-permute-done.30 = bf16[1,192,1024]{2,1,0:T(8,128)(2,1)S(1)} collective-permute-done((bf16[1,192,1024]{2,1,0:T(8,128)(2,1)S(1)}, bf16[1,192,1024]{2,1,0:T(8,128)(2,1)S(1)}, u32[]{:S(2)}, u32[]{:S(2)}) %collective-permute-start.30) | collective-permute-done | bytes 393248 | tf_op jit(solution)/shard_map/ppermute | solution.py:609
  915.7 5.1 collective-permute-done.39
  924.2 16.4 %collective-permute-done.37 = bf16[208,1024]{1,0:T(8,128)(2,1)S(1)} collective-permute-done((bf16[208,1024]{1,0:T(8,128)(2,1)S(1)}, bf16[208,1024]{1,0:T(8,128)(2,1)S(1)}, u32[]{:S(2)}, u32[]{:S(2)}) %collective-permute-start.37) | collective-permute-done | bytes 426016 | tf_op jit(solution)/shard_map/ppermute | solution.py:667
  953.3 24.2 %collective-permute-done.28 = bf16[208,1024]{1,0:T(8,128)(2,1)} collective-permute-done((bf16[208,1024]{1,0:T(8,128)(2,1)}, bf16[208,1024]{1,0:T(8,128)(2,1)}, u32[]{:S(2)}, u32[]{:S(2)}) %collective-permute-start.28) | collective-permute-done | bytes 426016 | tf_op jit(solution)/shard_map/ppermute | solution.py:667
  979.2 4.5 multiply_subtract_fusion
  (474 shorter events, 235.2 us)
Async XLA Ops:
  7.2 170.1 %all-gather.3.cloned.1.call-start = ((), (), s32[]{:S(2)}) async-start(), calls=%async_computation.4 | async-start | bytes 27033600 | tf_op jit(solution)/shard_map/all_gather | solution.py:747
  12.4 15.9 %all-to-all-start = ((bf16[32,2,168]{2,1,0:T(2,128)(2,1)}), bf16[32,2,168]{2,1,0:T(2,128)(2,1)S(1)}, u32[]{:S(2)}, u32[]{:S(2)}) async-start(bf16[32,2,168]{2,1,0:T(2,128)(2,1)} %reshape.431), calls=%async_computation | async-start | bytes 65536 | tf_op jit(solution)/shard_map/all_to_all | solution.py:683
  18.8 314.0 %all-gather.5.cloned.1.call-start = ((), (), s32[]{:S(2)}) async-start(), calls=%async_computation.5 | async-start | bytes 8650752 | tf_op jit(solution)/shard_map/all_gather | solution.py:750
  18.9 22.4 %collective-permute-start.1 = (bf16[320,1024]{1,0:T(8,128)(2,1)}, bf16[320,1024]{1,0:T(8,128)(2,1)S(1)}, u32[]{:S(2)}, u32[]{:S(2)}) collective-permute-start(bf16[320,1024]{1,0:T(8,128)(2,1)} %param.20), channel_id=1, source_target_pairs={{0,1},{1,0},{2,3},{3,2},{4,5},{5,4},{6,7},{7,6},{8,9},{9,8},{10,11... | collective-permute-start | bytes 1966088 | tf_op jit(solution)/shard_map/ppermute | solution.py:688
  19.2 38.7 %collective-permute-start = (bf16[320,1024]{1,0:T(8,128)(2,1)}, bf16[320,1024]{1,0:T(8,128)(2,1)}, u32[]{:S(2)}, u32[]{:S(2)}) collective-permute-start(bf16[320,1024]{1,0:T(8,128)(2,1)} %param.18), channel_id=1, source_target_pairs={{0,1},{1,0},{2,3},{3,2},{4,5},{5,4},{6,7},{7,6},{8,9},{9,8},{10,11... | collective-permute-start | bytes 1966088 | tf_op jit(solution)/shard_map/ppermute | solution.py:688
  373.3 31.4 %collective-permute-start.2 = (bf16[4,2,2,128,1024]{4,3,0,2,1:T(8,128)(2,1)S(1)}, bf16[4,2,2,128,1024]{4,3,0,2,1:T(8,128)(2,1)S(1)}, u32[]{:S(2)}, u32[]{:S(2)}) collective-permute-start(bf16[4,2,2,128,1024]{4,3,0,2,1:T(8,128)(2,1)S(1)} %bitcast.245), channel_id=1, source_target_pairs={{0,2},{2,0},{4,6},{6,4},{8,10},{10,8},{12,14},{14,12},{16,18},{18,... | collective-permute-start | bytes 12582920 | tf_op jit(solution)/shard_map/ppermute | solution.py:609
  407.6 24.4 %collective-permute-start.4 = (bf16[4,2,64,1024]{3,2,0,1:T(8,128)(2,1)S(1)}, bf16[4,2,64,1024]{3,2,0,1:T(8,128)(2,1)S(1)}, u32[]{:S(2)}, u32[]{:S(2)}) collective-permute-start(bf16[4,2,64,1024]{3,2,0,1:T(8,128)(2,1)S(1)} %dynamic-slice_bitcast_fusion.5), channel_id=1, source_target_pairs={{0,1},{1,0},{2,3},{3,2},{4,5},{5,4},{6,7},{7,6},{8,9},{9,8},{10,11... | collective-permute-start | bytes 3145736 | tf_op jit(solution)/shard_map/ppermute | solution.py:609
  408.2 24.8 %collective-permute-start.5 = (bf16[4,2,64,1024]{3,2,0,1:T(8,128)(2,1)S(1)}, bf16[4,2,64,1024]{3,2,0,1:T(8,128)(2,1)S(1)}, u32[]{:S(2)}, u32[]{:S(2)}) collective-permute-start(bf16[4,2,64,1024]{3,2,0,1:T(8,128)(2,1)S(1)} %dynamic-slice_bitcast_fusion.4), channel_id=1, source_target_pairs={{0,4},{2,6},{4,0},{6,2},{8,12},{10,14},{12,8},{14,10},{16,20},{18,... | collective-permute-start | bytes 3145736 | tf_op jit(solution)/shard_map/ppermute | solution.py:609
  425.2 21.6 %collective-permute-start.3 = (bf16[1,2,2,400,1024]{4,3,2,1,0:T(8,128)(2,1)}, bf16[1,2,2,400,1024]{4,3,2,1,0:T(8,128)(2,1)}, u32[]{:S(2)}, u32[]{:S(2)}) collective-permute-start(bf16[1,2,2,400,1024]{4,3,2,1,0:T(8,128)(2,1)} %dynamic-slice_bitcast_fusion.1), channel_id=1, source_target_pairs={{0,2},{2,0},{4,6},{6,4},{8,10},{10,8},{12,14},{14,12},{16,18},{18,... | collective-permute-start | bytes 9830408 | tf_op jit(solution)/shard_map/ppermute | solution.py:609
  432.5 13.1 %collective-permute-start.6 = (bf16[4,64,1024]{2,1,0:T(8,128)(2,1)S(1)}, bf16[4,64,1024]{2,1,0:T(8,128)(2,1)S(1)}, u32[]{:S(2)}, u32[]{:S(2)}) collective-permute-start(bf16[4,64,1024]{2,1,0:T(8,128)(2,1)S(1)} %dynamic-slice_bitcast_fusion.14), channel_id=1, source_target_pairs={{0,4},{2,6},{4,0},{6,2},{8,12},{10,14},{12,8},{14,10},{16,20},{18,... | collective-permute-start | bytes 1572872 | tf_op jit(solution)/shard_map/ppermute | solution.py:609
  433.5 12.3 %collective-permute-start.7 = (bf16[4,64,1024]{2,1,0:T(8,128)(2,1)S(1)}, bf16[4,64,1024]{2,1,0:T(8,128)(2,1)S(1)}, u32[]{:S(2)}, u32[]{:S(2)}) collective-permute-start(bf16[4,64,1024]{2,1,0:T(8,128)(2,1)S(1)} %dynamic-slice_bitcast_fusion.13), channel_id=1, source_target_pairs={{0,1},{1,0},{2,3},{3,2},{4,5},{5,4},{6,7},{7,6},{8,9},{9,8},{10,11... | collective-permute-start | bytes 1572872 | tf_op jit(solution)/shard_map/ppermute | solution.py:609
  454.6 55.6 %collective-permute-start.9 = (bf16[1,2,192,1024]{3,2,1,0:T(8,128)(2,1)}, bf16[1,2,192,1024]{3,2,1,0:T(8,128)(2,1)}, u32[]{:S(2)}, u32[]{:S(2)}) collective-permute-start(bf16[1,2,192,1024]{3,2,1,0:T(8,128)(2,1)} %dynamic-slice_bitcast_fusion.11), channel_id=1, source_target_pairs={{0,4},{2,6},{4,0},{6,2},{8,12},{10,14},{12,8},{14,10},{16,20},{18,... | collective-permute-start | bytes 2359304 | tf_op jit(solution)/shard_map/ppermute | solution.py:609
  464.9 47.8 %collective-permute-start.8 = (bf16[1,2,208,1024]{3,2,1,0:T(8,128)(2,1)}, bf16[1,2,208,1024]{3,2,1,0:T(8,128)(2,1)}, u32[]{:S(2)}, u32[]{:S(2)}) collective-permute-start(bf16[1,2,208,1024]{3,2,1,0:T(8,128)(2,1)} %dynamic-slice_bitcast_fusion.8), channel_id=1, source_target_pairs={{0,1},{1,0},{2,3},{3,2},{4,5},{5,4},{6,7},{7,6},{8,9},{9,8},{10,11... | collective-permute-start | bytes 2555912 | tf_op jit(solution)/shard_map/ppermute | solution.py:609
  548.8 95.0 %collective-permute-start.10 = (bf16[2,2,2,400,1024]{4,3,0,2,1:T(8,128)(2,1)}, bf16[2,2,2,400,1024]{4,3,0,2,1:T(8,128)(2,1)}, u32[]{:S(2)}, u32[]{:S(2)}) collective-permute-start(bf16[2,2,2,400,1024]{4,3,0,2,1:T(8,128)(2,1)} %bitcast.232), channel_id=1, source_target_pairs={{0,2},{2,0},{4,6},{6,4},{8,10},{10,8},{12,14},{14,12},{16,18},{18,... | collective-permute-start | bytes 19660808 | tf_op jit(solution)/shard_map/ppermute | solution.py:609
  557.8 16.5 %collective-permute-start.51 = (bf16[64,1024]{1,0:T(8,128)(2,1)S(1)}, bf16[64,1024]{1,0:T(8,128)(2,1)S(1)}, u32[]{:S(2)}, u32[]{:S(2)}) collective-permute-start(bf16[64,1024]{1,0:T(8,128)(2,1)S(1)} %get-tuple-element.106), channel_id=1, source_target_pairs={{0,8},{2,10},{4,12},{6,14},{8,16},{10,18},{12,20},{14,22},{16,24},... | collective-permute-start | bytes 393224 | tf_op jit(solution)/shard_map/ppermute | solution.py:667
  563.0 19.1 %collective-permute-start.50 = (bf16[64,1024]{1,0:T(8,128)(2,1)S(1)}, bf16[64,1024]{1,0:T(8,128)(2,1)S(1)}, u32[]{:S(2)}, u32[]{:S(2)}) collective-permute-start(bf16[64,1024]{1,0:T(8,128)(2,1)S(1)} %get-tuple-element.104), channel_id=1, source_target_pairs={{0,24},{2,26},{4,28},{6,30},{8,0},{10,2},{12,4},{14,6},{16,8},{18,... | collective-permute-start | bytes 393224 | tf_op jit(solution)/shard_map/ppermute | solution.py:667
  563.8 18.2 %collective-permute-start.49 = (bf16[64,1024]{1,0:T(8,128)(2,1)S(1)}, bf16[64,1024]{1,0:T(8,128)(2,1)S(1)}, u32[]{:S(2)}, u32[]{:S(2)}) collective-permute-start(bf16[64,1024]{1,0:T(8,128)(2,1)S(1)} %get-tuple-element.105), channel_id=1, source_target_pairs={{0,16},{2,18},{4,20},{6,22},{8,24},{10,26},{12,28},{14,30},{16,0},... | collective-permute-start | bytes 393224 | tf_op jit(solution)/shard_map/ppermute | solution.py:667
  565.9 16.1 %collective-permute-start.48 = (bf16[64,1024]{1,0:T(8,128)(2,1)S(1)}, bf16[64,1024]{1,0:T(8,128)(2,1)S(1)}, u32[]{:S(2)}, u32[]{:S(2)}) collective-permute-start(bf16[64,1024]{1,0:T(8,128)(2,1)S(1)} %get-tuple-element.103), channel_id=1, source_target_pairs={{0,8},{2,10},{4,12},{6,14},{8,16},{10,18},{12,20},{14,22},{16,24},... | collective-permute-start | bytes 393224 | tf_op jit(solution)/shard_map/ppermute | solution.py:667
  581.1 15.8 %collective-permute-start.22 = (bf16[320,1024]{1,0:T(8,128)(2,1)S(1)}, bf16[320,1024]{1,0:T(8,128)(2,1)S(1)}, u32[]{:S(2)}, u32[]{:S(2)}) collective-permute-start(bf16[320,1024]{1,0:T(8,128)(2,1)S(1)} %dynamic-slice_convert_fusion), channel_id=1, source_target_pairs={{0,1},{1,0},{2,3},{3,2},{4,5},{5,4},{6,7},{7,6},{8,9},{9,8},{10,11... | collective-permute-start | bytes 1966088 | tf_op jit(solution)/shard_map/ppermute | solution.py:688
  599.7 12.1 %collective-permute-start.11 = (bf16[1,208,1024]{2,1,0:T(8,128)(2,1)}, bf16[1,208,1024]{2,1,0:T(8,128)(2,1)}, u32[]{:S(2)}, u32[]{:S(2)}) collective-permute-start(bf16[1,208,1024]{2,1,0:T(8,128)(2,1)} %dynamic-slice_bitcast_fusion.19), channel_id=1, source_target_pairs={{0,4},{2,6},{4,0},{6,2},{8,12},{10,14},{12,8},{14,10},{16,20},{18,... | collective-permute-start | bytes 1277960 | tf_op jit(solution)/shard_map/ppermute | solution.py:609
  609.0 24.5 %collective-permute-start.19 = (bf16[192,1024]{1,0:T(8,128)(2,1)S(1)}, bf16[192,1024]{1,0:T(8,128)(2,1)}, u32[]{:S(2)}, u32[]{:S(2)}) collective-permute-start(bf16[192,1024]{1,0:T(8,128)(2,1)S(1)} %bitcast.251), channel_id=1, source_target_pairs={{8,24},{10,26},{12,28},{14,30},{9,25},{11,27},{13,29},{15,31}} | collective-permute-start | bytes 1179656 | tf_op jit(solution)/shard_map/ppermute | solution.py:667
  611.1 23.4 %collective-permute-start.18 = (bf16[192,1024]{1,0:T(8,128)(2,1)S(1)}, bf16[192,1024]{1,0:T(8,128)(2,1)S(1)}, u32[]{:S(2)}, u32[]{:S(2)}) collective-permute-start(bf16[192,1024]{1,0:T(8,128)(2,1)S(1)} %bitcast.252), channel_id=1, source_target_pairs={{16,24},{18,26},{20,28},{22,30},{17,25},{19,27},{21,29},{23,31}} | collective-permute-start | bytes 1179656 | tf_op jit(solution)/shard_map/ppermute | solution.py:667
  613.0 23.8 %collective-permute-start.17 = (bf16[208,1024]{1,0:T(8,128)(2,1)S(1)}, bf16[208,1024]{1,0:T(8,128)(2,1)S(1)}, u32[]{:S(2)}, u32[]{:S(2)}) collective-permute-start(bf16[208,1024]{1,0:T(8,128)(2,1)S(1)} %bitcast.247), channel_id=1, source_target_pairs={{0,24},{2,26},{4,28},{6,30},{1,25},{3,27},{5,29},{7,31}} | collective-permute-start | bytes 1277960 | tf_op jit(solution)/shard_map/ppermute | solution.py:667
  613.7 28.9 %collective-permute-start.16 = (bf16[208,1024]{1,0:T(8,128)(2,1)S(1)}, bf16[208,1024]{1,0:T(8,128)(2,1)S(1)}, u32[]{:S(2)}, u32[]{:S(2)}) collective-permute-start(bf16[208,1024]{1,0:T(8,128)(2,1)S(1)} %bitcast.248), channel_id=1, source_target_pairs={{8,24},{10,26},{12,28},{14,30},{9,25},{11,27},{13,29},{15,31}} | collective-permute-start | bytes 1277960 | tf_op jit(solution)/shard_map/ppermute | solution.py:667
  737.4 44.3 %collective-permute-start.13 = (bf16[2,2,208,1024]{3,2,0,1:T(8,128)(2,1)}, bf16[2,2,208,1024]{3,2,0,1:T(8,128)(2,1)S(1)}, u32[]{:S(2)}, u32[]{:S(2)}) collective-permute-start(bf16[2,2,208,1024]{3,2,0,1:T(8,128)(2,1)} %dynamic-slice_bitcast_fusion.2), channel_id=1, source_target_pairs={{0,1},{1,0},{2,3},{3,2},{4,5},{5,4},{6,7},{7,6},{8,9},{9,8},{10,11... | collective-permute-start | bytes 5111816 | tf_op jit(solution)/shard_map/ppermute | solution.py:609
  738.3 39.6 %collective-permute-start.14 = (bf16[2,2,192,1024]{3,2,0,1:T(8,128)(2,1)S(1)}, bf16[2,2,192,1024]{3,2,0,1:T(8,128)(2,1)S(1)}, u32[]{:S(2)}, u32[]{:S(2)}) collective-permute-start(bf16[2,2,192,1024]{3,2,0,1:T(8,128)(2,1)S(1)} %dynamic-slice_bitcast_fusion.3), channel_id=1, source_target_pairs={{0,4},{2,6},{4,0},{6,2},{8,12},{10,14},{12,8},{14,10},{16,20},{18,... | collective-permute-start | bytes 4718600 | tf_op jit(solution)/shard_map/ppermute | solution.py:609
  761.9 96.3 %collective-permute-start.23 = (bf16[1,2,2,400,1024]{4,3,2,1,0:T(8,128)(2,1)}, bf16[1,2,2,400,1024]{4,3,2,1,0:T(8,128)(2,1)}, u32[]{:S(2)}, u32[]{:S(2)}) collective-permute-start(bf16[1,2,2,400,1024]{4,3,2,1,0:T(8,128)(2,1)} %dynamic-slice_bitcast_fusion), channel_id=1, source_target_pairs={{0,2},{2,0},{4,6},{6,4},{8,10},{10,8},{12,14},{14,12},{16,18},{18,... | collective-permute-start | bytes 9830408 | tf_op jit(solution)/shard_map/ppermute | solution.py:609
  780.7 70.6 %collective-permute-start.38 = (bf16[2,192,1024]{2,1,0:T(8,128)(2,1)}, bf16[2,192,1024]{2,1,0:T(8,128)(2,1)}, u32[]{:S(2)}, u32[]{:S(2)}) collective-permute-start(bf16[2,192,1024]{2,1,0:T(8,128)(2,1)} %dynamic-slice_bitcast_fusion.9), channel_id=1, source_target_pairs={{0,1},{1,0},{2,3},{3,2},{4,5},{5,4},{6,7},{7,6},{8,9},{9,8},{10,11... | collective-permute-start | bytes 2359304 | tf_op jit(solution)/shard_map/ppermute | solution.py:609
  790.0 64.1 %collective-permute-start.21 = (bf16[320,1024]{1,0:T(8,128)(2,1)}, bf16[320,1024]{1,0:T(8,128)(2,1)}, u32[]{:S(2)}, u32[]{:S(2)}) collective-permute-start(bf16[320,1024]{1,0:T(8,128)(2,1)} %dynamic-slice_convert_fusion.1), channel_id=1, source_target_pairs={{0,1},{1,0},{2,3},{3,2},{4,5},{5,4},{6,7},{7,6},{8,9},{9,8},{10,11... | collective-permute-start | bytes 1966088 | tf_op jit(solution)/shard_map/ppermute | solution.py:688
  791.8 31.2 %all-to-all-start.2 = ((f32[32,1,560]{2,1,0:T(1,128)}), f32[32,1,560]{2,1,0:T(1,128)S(1)}, u32[]{:S(2)}, u32[]{:S(2)}) async-start(f32[32,1,560]{2,1,0:T(1,128)} %all_to_all.19), calls=%async_computation.2 | async-start | bytes 163840 | tf_op jit(solution)/shard_map/all_to_all | solution.py:954
  820.5 28.3 %collective-permute-start.42 = (bf16[4,2,2,16,1024]{4,3,2,1,0:T(8,128)(2,1)}, bf16[4,2,2,16,1024]{4,3,2,1,0:T(8,128)(2,1)}, u32[]{:S(2)}, u32[]{:S(2)}) collective-permute-start(bf16[4,2,2,16,1024]{4,3,2,1,0:T(8,128)(2,1)} %dynamic-slice_bitcast_fusion.12), channel_id=1, source_target_pairs={{0,2},{2,0},{4,6},{6,4},{8,10},{10,8},{12,14},{14,12},{16,18},{18,... | collective-permute-start | bytes 1572872 | tf_op jit(solution)/shard_map/ppermute | solution.py:609
  821.9 63.3 %collective-permute-start.34 = (bf16[2,208,1024]{2,1,0:T(8,128)(2,1)}, bf16[2,208,1024]{2,1,0:T(8,128)(2,1)}, u32[]{:S(2)}, u32[]{:S(2)}) collective-permute-start(bf16[2,208,1024]{2,1,0:T(8,128)(2,1)} %dynamic-slice_bitcast_fusion.6), channel_id=1, source_target_pairs={{0,4},{2,6},{4,0},{6,2},{8,12},{10,14},{12,8},{14,10},{16,20},{18,... | collective-permute-start | bytes 2555912 | tf_op jit(solution)/shard_map/ppermute | solution.py:609
  825.1 22.0 %all-to-all-start.3 = ((f32[32,1,224]{2,1,0:T(1,128)}), f32[32,1,224]{2,1,0:T(1,128)S(1)}, u32[]{:S(2)}, u32[]{:S(2)}) async-start(f32[32,1,224]{2,1,0:T(1,128)} %broadcast_in_dim.26), calls=%async_computation.3 | async-start | bytes 65536 | tf_op jit(solution)/shard_map/all_to_all | solution.py:683
  863.0 27.0 %collective-permute-start.29 = (bf16[1,2,192,1024]{3,2,1,0:T(8,128)(2,1)}, bf16[1,2,192,1024]{3,2,1,0:T(8,128)(2,1)}, u32[]{:S(2)}, u32[]{:S(2)}) collective-permute-start(bf16[1,2,192,1024]{3,2,1,0:T(8,128)(2,1)} %dynamic-slice_bitcast_fusion.10), channel_id=1, source_target_pairs={{0,4},{2,6},{4,0},{6,2},{8,12},{10,14},{12,8},{14,10},{16,20},{18,... | collective-permute-start | bytes 2359304 | tf_op jit(solution)/shard_map/ppermute | solution.py:609
  869.2 41.3 %collective-permute-start.41 = (bf16[192,1024]{1,0:T(8,128)(2,1)}, bf16[192,1024]{1,0:T(8,128)(2,1)S(1)}, u32[]{:S(2)}, u32[]{:S(2)}) collective-permute-start(bf16[192,1024]{1,0:T(8,128)(2,1)} %get-tuple-element.100), channel_id=1, source_target_pairs={{16,8},{18,10},{20,12},{22,14},{24,16},{26,18},{28,20},{30,22},{17... | collective-permute-start | bytes 1179656 | tf_op jit(solution)/shard_map/ppermute | solution.py:667
  870.5 41.2 %collective-permute-start.40 = (bf16[192,1024]{1,0:T(8,128)(2,1)}, bf16[192,1024]{1,0:T(8,128)(2,1)}, u32[]{:S(2)}, u32[]{:S(2)}) collective-permute-start(bf16[192,1024]{1,0:T(8,128)(2,1)} %get-tuple-element.101), channel_id=1, source_target_pairs={{0,16},{2,18},{4,20},{6,22},{24,8},{26,10},{28,12},{30,14},{1,17},... | collective-permute-start | bytes 1179656 | tf_op jit(solution)/shard_map/ppermute | solution.py:667
  871.9 20.6 %collective-permute-start.24 = (bf16[1,2,208,1024]{3,2,1,0:T(8,128)(2,1)}, bf16[1,2,208,1024]{3,2,1,0:T(8,128)(2,1)}, u32[]{:S(2)}, u32[]{:S(2)}) collective-permute-start(bf16[1,2,208,1024]{3,2,1,0:T(8,128)(2,1)} %dynamic-slice_bitcast_fusion.7), channel_id=1, source_target_pairs={{0,1},{1,0},{2,3},{3,2},{4,5},{5,4},{6,7},{7,6},{8,9},{9,8},{10,11... | collective-permute-start | bytes 2555912 | tf_op jit(solution)/shard_map/ppermute | solution.py:609
  873.9 75.7 %all-to-all-start.1 = ((bf16[32,16,1024]{2,1,0:T(8,128)(2,1)}), bf16[32,16,1024]{2,1,0:T(8,128)(2,1)}, u32[]{:S(2)}, u32[]{:S(2)}) async-start(bf16[32,16,1024]{2,1,0:T(8,128)(2,1)} %broadcast_in_dim.25), calls=%async_computation.1 | async-start | bytes 2097152 | tf_op jit(solution)/shard_map/all_to_all | solution.py:683
  885.2 35.6 %collective-permute-start.39 = (bf16[192,1024]{1,0:T(8,128)(2,1)S(1)}, bf16[192,1024]{1,0:T(8,128)(2,1)S(1)}, u32[]{:S(2)}, u32[]{:S(2)}) collective-permute-start(bf16[192,1024]{1,0:T(8,128)(2,1)S(1)} %get-tuple-element.99), channel_id=1, source_target_pairs={{0,8},{2,10},{4,12},{6,14},{8,16},{10,18},{12,20},{14,22},{1,9},{3... | collective-permute-start | bytes 1179656 | tf_op jit(solution)/shard_map/ppermute | solution.py:667
  891.8 16.8 %collective-permute-start.30 = (bf16[1,192,1024]{2,1,0:T(8,128)(2,1)S(1)}, bf16[1,192,1024]{2,1,0:T(8,128)(2,1)S(1)}, u32[]{:S(2)}, u32[]{:S(2)}) collective-permute-start(bf16[1,192,1024]{2,1,0:T(8,128)(2,1)S(1)} %dynamic-slice_bitcast_fusion.23), channel_id=1, source_target_pairs={{0,1},{1,0},{2,3},{3,2},{4,5},{5,4},{6,7},{7,6},{8,9},{9,8},{10,11... | collective-permute-start | bytes 1179656 | tf_op jit(solution)/shard_map/ppermute | solution.py:609
  892.4 48.2 %collective-permute-start.37 = (bf16[208,1024]{1,0:T(8,128)(2,1)S(1)}, bf16[208,1024]{1,0:T(8,128)(2,1)S(1)}, u32[]{:S(2)}, u32[]{:S(2)}) collective-permute-start(bf16[208,1024]{1,0:T(8,128)(2,1)S(1)} %get-tuple-element.97), channel_id=1, source_target_pairs={{16,8},{18,10},{20,12},{22,14},{24,16},{26,18},{28,20},{30,22},{17... | collective-permute-start | bytes 1277960 | tf_op jit(solution)/shard_map/ppermute | solution.py:667
  908.6 33.5 %collective-permute-start.25 = (bf16[1,208,1024]{2,1,0:T(8,128)(2,1)S(1)}, bf16[1,208,1024]{2,1,0:T(8,128)(2,1)S(1)}, u32[]{:S(2)}, u32[]{:S(2)}) collective-permute-start(bf16[1,208,1024]{2,1,0:T(8,128)(2,1)S(1)} %dynamic-slice_bitcast_fusion.18), channel_id=1, source_target_pairs={{0,4},{2,6},{4,0},{6,2},{8,12},{10,14},{12,8},{14,10},{16,20},{18,... | collective-permute-start | bytes 1277960 | tf_op jit(solution)/shard_map/ppermute | solution.py:609
  910.5 33.9 %collective-permute-start.36 = (bf16[208,1024]{1,0:T(8,128)(2,1)S(1)}, bf16[208,1024]{1,0:T(8,128)(2,1)S(1)}, u32[]{:S(2)}, u32[]{:S(2)}) collective-permute-start(bf16[208,1024]{1,0:T(8,128)(2,1)S(1)} %get-tuple-element.98), channel_id=1, source_target_pairs={{0,16},{2,18},{4,20},{6,22},{24,8},{26,10},{28,12},{30,14},{1,17},... | collective-permute-start | bytes 1277960 | tf_op jit(solution)/shard_map/ppermute | solution.py:667
  911.8 34.7 %collective-permute-start.35 = (bf16[208,1024]{1,0:T(8,128)(2,1)S(1)}, bf16[208,1024]{1,0:T(8,128)(2,1)S(1)}, u32[]{:S(2)}, u32[]{:S(2)}) collective-permute-start(bf16[208,1024]{1,0:T(8,128)(2,1)S(1)} %get-tuple-element.96), channel_id=1, source_target_pairs={{0,8},{2,10},{4,12},{6,14},{8,16},{10,18},{12,20},{14,22},{1,9},{3... | collective-permute-start | bytes 1277960 | tf_op jit(solution)/shard_map/ppermute | solution.py:667
  920.8 27.1 %collective-permute-start.33 = (bf16[192,1024]{1,0:T(8,128)(2,1)}, bf16[192,1024]{1,0:T(8,128)(2,1)S(1)}, u32[]{:S(2)}, u32[]{:S(2)}) collective-permute-start(bf16[192,1024]{1,0:T(8,128)(2,1)} %fusion.93), channel_id=1, source_target_pairs={{8,0},{10,2},{12,4},{14,6},{9,1},{11,3},{13,5},{15,7}} | collective-permute-start | bytes 1179656 | tf_op jit(solution)/shard_map/ppermute | solution.py:667
  944.4 33.1 %collective-permute-start.28 = (bf16[208,1024]{1,0:T(8,128)(2,1)}, bf16[208,1024]{1,0:T(8,128)(2,1)}, u32[]{:S(2)}, u32[]{:S(2)}) collective-permute-start(bf16[208,1024]{1,0:T(8,128)(2,1)} %fusion.92), channel_id=1, source_target_pairs={{8,0},{10,2},{12,4},{14,6},{9,1},{11,3},{13,5},{15,7}} | collective-permute-start | bytes 1277960 | tf_op jit(solution)/shard_map/ppermute | solution.py:667
  946.5 31.0 %collective-permute-start.27 = (bf16[208,1024]{1,0:T(8,128)(2,1)}, bf16[208,1024]{1,0:T(8,128)(2,1)}, u32[]{:S(2)}, u32[]{:S(2)}) collective-permute-start(bf16[208,1024]{1,0:T(8,128)(2,1)} %fusion.92), channel_id=1, source_target_pairs={{16,0},{18,2},{20,4},{22,6},{17,1},{19,3},{21,5},{23,7}} | collective-permute-start | bytes 1277960 | tf_op jit(solution)/shard_map/ppermute | solution.py:667
  947.9 29.6 %collective-permute-start.26 = (bf16[208,1024]{1,0:T(8,128)(2,1)}, bf16[208,1024]{1,0:T(8,128)(2,1)}, u32[]{:S(2)}, u32[]{:S(2)}) collective-permute-start(bf16[208,1024]{1,0:T(8,128)(2,1)} %fusion.92), channel_id=1, source_target_pairs={{24,0},{26,2},{28,4},{30,6},{25,1},{27,3},{29,5},{31,7}} | collective-permute-start | bytes 1277960 | tf_op jit(solution)/shard_map/ppermute | solution.py:667
  (107 other events, 2367.2 us)
Sparse Core Ops, SparseCore 0:
  11.5 165.7 all-gather.2
  180.8 77.6 all-gather.4

commit v3 on v2

--- a/solution.py
+++ b/solution.py
@@ -26,6 +26,7 @@
 RATE_SMALL = 0.5
 WEIGHT_DECAY = 0.01
 MASKED = -1e30
+MESH = pl.DeviceIdType.MESH
 
 
 def bucket_edges():
@@ -678,6 +679,29 @@
     return lax.optimization_barrier((value, *states))[0]
 
 
+def sum_shares(rows):
+    part = lax.psum_scatter(rows, "dp", scatter_dimension=0, tiled=True)
+    return lax.psum_scatter(part, "stream", scatter_dimension=0, tiled=True)
+
+
+def to_last_quarter(share, devices, skipped):
+    owners = devices // 4
+    size = share.shape[0]
+    block = (devices * size - skipped) // owners
+    starts = [skipped + owner * block for owner in range(owners)]
+    blocks = []
+    for part in range((size - 1 + block + size - 1) // size):
+        pairs = [
+            (start // size + part, 3 * owners + owner)
+            for owner, start in enumerate(starts)
+            if start // size + part < devices
+        ]
+        blocks.append(lax.ppermute(share, ("dp", "stream"), pairs))
+    mine = lax.axis_index("dp") * 2 + lax.axis_index("stream") - 3 * owners
+    offset = jnp.mod(skipped + jnp.maximum(mine, 0) * block, size)
+    return lax.dynamic_slice_in_dim(jnp.concatenate(blocks, axis=0), offset, block)
+
+
 def to_all(part, count):
     shared = jnp.broadcast_to(part[None], (count, *part.shape))
     gathered = lax.all_to_all(shared, ("dp", "stream"), 0, 0, tiled=True)
@@ -714,6 +738,435 @@
         first_hat / (jnp.sqrt(second_hat) + ADAM_EPS) + step_decay * master
     )
     return (master_new, first_new, second_new)
+
+
+def chunk_rows(block):
+    tiles = block // 16
+    counts = [(tiles + 3 - part) // 4 * 16 for part in range(4)]
+    return [(sum(counts[:part]), counts[part]) for part in range(4)]
+
+
+def add_rows(target_ref, source_ref, start, count):
+    @pl.loop(0, count // 16)
+    def tile_step(tile):
+        rows = pl.ds(pl.multiple_of(start + tile * 16, 16), 16)
+        target_ref[rows, :] = (
+            target_ref[rows, :].astype(jnp.float32) + source_ref[rows, :].astype(jnp.float32)
+        ).astype(jnp.bfloat16)
+
+
+def sum_kernel(
+    grad_ref,
+    out_ref,
+    held,
+    core_in,
+    first_in,
+    second_in,
+    along_in,
+    load_sem,
+    core_send,
+    core_recv,
+    first_send,
+    first_recv,
+    second_send,
+    second_recv,
+    along_send,
+    along_recv,
+):
+    slabs, block = grad_ref.shape[0], grad_ref.shape[4]
+    place, x = lax.axis_index("dp"), lax.axis_index("stream")
+    c, y, z = place % 2, (place // 2) % 2, place // 4
+    sibling, across, beside = (place + 1 - 2 * c, x), (place, 1 - x), (place + 2 - 4 * y, x)
+    above, below = (place + 4, x), (place - 4, x)
+    chunks = chunk_rows(block)
+
+    barrier = pltpu.get_barrier_semaphore()
+    for neighbour in (sibling, across, beside):
+        pl.semaphore_signal(barrier, inc=1, device_id=neighbour, device_id_type=MESH)
+
+    @pl.when(z < 3)
+    def greet_above():
+        pl.semaphore_signal(barrier, inc=1, device_id=above, device_id_type=MESH)
+
+    @pl.when(z > 0)
+    def greet_below():
+        pl.semaphore_signal(barrier, inc=1, device_id=below, device_id_type=MESH)
+
+    pl.semaphore_wait(barrier, 4 + z * (3 - z) // 2)
+
+    def remote(source, target, send_sem, recv_sem, device):
+        return pltpu.make_async_remote_copy(
+            src_ref=source,
+            dst_ref=target,
+            send_sem=send_sem,
+            recv_sem=recv_sem,
+            device_id=device,
+            device_id_type=MESH,
+        )
+
+    def core_copy(s, yy, xx):
+        at = s * 4 + yy * 2 + xx
+        return remote(
+            grad_ref.at[s, yy, 1 - c, xx],
+            core_in.at[s, yy, xx],
+            core_send.at[at],
+            core_recv.at[at],
+            sibling,
+        )
+
+    def load(s, yy, xx):
+        return pltpu.make_async_copy(
+            grad_ref.at[s, yy, c, xx], held.at[s, yy, xx], load_sem.at[s * 4 + yy * 2 + xx]
+        )
+
+    def first_copy(s, chunk, other):
+        rows = pl.ds(*chunks[chunk])
+        at = (s * 4 + chunk) * 2 + other
+        source = held.at[s, other, 1 - x, rows] if chunk < 2 else held.at[s, 1 - y, other, rows]
+        return remote(
+            source,
+            first_in.at[s, other, rows],
+            first_send.at[at],
+            first_recv.at[at],
+            across if chunk < 2 else beside,
+        )
+
+    def second_copy(s, chunk):
+        rows = pl.ds(*chunks[chunk])
+        source = held.at[s, 1 - y, x, rows] if chunk < 2 else held.at[s, y, 1 - x, rows]
+        return remote(
+            source,
+            second_in.at[s, rows],
+            second_send.at[s * 4 + chunk],
+            second_recv.at[s * 4 + chunk],
+            beside if chunk < 2 else across,
+        )
+
+    def along_copy(s, chunk, down):
+        rows = pl.ds(*chunks[chunk])
+        way = 0 if down else 1
+        return remote(
+            held.at[s, y, x, rows],
+            along_in.at[way, s, rows],
+            along_send.at[s * 4 + chunk],
+            along_recv.at[way * slabs * 4 + s * 4 + chunk],
+            below if down else above,
+        )
+
+    def core_stage(s, half):
+        if half == 0:
+            for yy in range(2):
+                for xx in range(2):
+                    load(s, yy, xx).wait()
+                    core_copy(s, yy, xx).wait_recv()
+        for chunk in (half, half + 2):
+            for yy in range(2):
+                for xx in range(2):
+                    add_rows(held.at[s, yy, xx], core_in.at[s, yy, xx], *chunks[chunk])
+            for other in range(2):
+                first_copy(s, chunk, other).start()
+
+    def first_stage(s, half):
+        for chunk in (half, half + 2):
+            for other in range(2):
+                first_copy(s, chunk, other).wait_recv()
+                kept = held.at[s, other, x] if chunk < 2 else held.at[s, y, other]
+                add_rows(kept, first_in.at[s, other], *chunks[chunk])
+            second_copy(s, chunk).start()
+
+    def second_stage(s, half):
+        for chunk in (half, half + 2):
+            second_copy(s, chunk).wait_recv()
+            add_rows(held.at[s, y, x], second_in.at[s], *chunks[chunk])
+        along_stage(s, half, 0)
+
+    def along_stage(s, half, hop):
+        for down in (True, False):
+            source = 3 - hop if down else hop
+            if (source > s) if down else (source < s):
+
+                @pl.when(z == source)
+                def pass_on():
+                    for chunk in (half, half + 2):
+                        if hop > 0:
+                            along_copy(s, chunk, down).wait_recv()
+                            add_rows(
+                                held.at[s, y, x], along_in.at[0 if down else 1, s], *chunks[chunk]
+                            )
+                        along_copy(s, chunk, down).start()
+
+    def last_stage(s, half):
+        @pl.when(z == s)
+        def finish():
+            for chunk in (half, half + 2):
+                start, count = chunks[chunk]
+                if s < 3:
+                    along_copy(s, chunk, True).wait_recv()
+                if s > 0:
+                    along_copy(s, chunk, False).wait_recv()
+
+                @pl.loop(0, count // 16)
+                def tile_step(tile):
+                    rows = pl.ds(pl.multiple_of(start + tile * 16, 16), 16)
+                    total = held[s, y, x, rows, :].astype(jnp.float32)
+                    if s < 3:
+                        total = total + along_in[0, s, rows, :].astype(jnp.float32)
+                    if s > 0:
+                        total = total + along_in[1, s, rows, :].astype(jnp.float32)
+                    out_ref[rows, :] = total
+
+    for s in range(slabs):
+        for yy in range(2):
+            for xx in range(2):
+                core_copy(s, yy, xx).start()
+                load(s, yy, xx).start()
+    out_ref[...] = jnp.zeros_like(out_ref)
+    waves = [(s, half) for s in range(slabs) for half in range(2)]
+    stages = [
+        core_stage,
+        first_stage,
+        second_stage,
+        partial(along_stage, hop=1),
+        partial(along_stage, hop=2),
+        last_stage,
+    ]
+    for step in range(len(waves) + len(stages) - 1):
+        for late, stage in enumerate(stages):
+            if 0 <= step - late < len(waves):
+                stage(*waves[step - late])
+    for s in range(slabs):
+        for yy in range(2):
+            for xx in range(2):
+                core_copy(s, yy, xx).wait_send()
+        for chunk in range(4):
+            for other in range(2):
+                first_copy(s, chunk, other).wait_send()
+            second_copy(s, chunk).wait_send()
+
+            @pl.when(z != s)
+            def sent_along():
+                along_copy(s, chunk, True).wait_send()
+
+
+def sum_slabs(rows, slabs):
+    block, width = rows.shape[0] // (slabs * 8), rows.shape[1]
+    low = jnp.bfloat16
+    dma = pltpu.SemaphoreType.DMA
+    return pl.pallas_call(
+        sum_kernel,
+        out_shape=jax.ShapeDtypeStruct((block, width), jnp.float32),
+        in_specs=[pl.BlockSpec(memory_space=pl.ANY)],
+        out_specs=pl.BlockSpec(memory_space=pltpu.VMEM),
+        scratch_shapes=[
+            pltpu.VMEM((slabs, 2, 2, block, width), low),
+            pltpu.VMEM((slabs, 2, 2, block, width), low),
+            pltpu.VMEM((slabs, 2, block, width), low),
+            pltpu.VMEM((slabs, block, width), low),
+            pltpu.VMEM((2, slabs, block, width), low),
+            dma((slabs * 4,)),
+            dma((slabs * 4,)),
+            dma((slabs * 4,)),
+            dma((slabs * 8,)),
+            dma((slabs * 8,)),
+            dma((slabs * 4,)),
+            dma((slabs * 4,)),
+            dma((slabs * 4,)),
+            dma((slabs * 8,)),
+        ],
+        compiler_params=pltpu.CompilerParams(
+            collective_id=0, has_side_effects=True, vmem_limit_bytes=56 * 2**20
+        ),
+        cost_estimate=pl.CostEstimate(
+            flops=rows.size, bytes_accessed=4 * rows.size, transcendentals=0
+        ),
+        name="sum_slabs",
+    )(rows.reshape(slabs, 2, 2, 2, block, width))
+
+
+def part_rows(block):
+    tiles = block // 16
+    one = (tiles * 2 + 4) // 5
+    two = (tiles - one) * 3 // 5
+    return [(0, one * 16), (one * 16, two * 16), ((one + two) * 16, (tiles - one - two) * 16)]
+
+
+def digit(code, place):
+    power = 1 + 9 * place + 81 * (place * (place - 1) // 2)
+    power = power + 729 * (place * (place - 1) * (place - 2) // 6)
+    return code // power % 10
+
+
+def gather_kernel(shard_ref, out_ref, own_sem, send_sem, link_recv, core_recv):
+    block = shard_ref.shape[0]
+    place, x = lax.axis_index("dp"), lax.axis_index("stream")
+    c, y, z = place % 2, (place // 2) % 2, place // 4
+    up, down, across, beside, sibling = range(5)
+    devices = [(place + 4, x), (place - 4, x), (place, 1 - x), (place + 2 - 4 * y, x)]
+    devices.append((place + 1 - 2 * c, x))
+    parts = part_rows(block)
+    order = [z] + [digit(code, z) for code in (2101, 1322, 33)]
+
+    barrier = pltpu.get_barrier_semaphore()
+    for way in (across, beside, sibling):
+        pl.semaphore_signal(barrier, inc=1, device_id=devices[way], device_id_type=MESH)
+
+    @pl.when(z < 3)
+    def greet_above():
+        pl.semaphore_signal(barrier, inc=1, device_id=devices[up], device_id_type=MESH)
+
+    @pl.when(z > 0)
+    def greet_below():
+        pl.semaphore_signal(barrier, inc=1, device_id=devices[down], device_id_type=MESH)
+
+    own = pltpu.make_async_copy(shard_ref, out_ref.at[z, y, c, x], own_sem)
+    own.start()
+    pl.semaphore_wait(barrier, 4 + z * (3 - z) // 2)
+    own.wait()
+
+    def copy(way, zz, yy, xx, part, core=None):
+        region = out_ref.at[zz, yy, c if core is None else core, xx, pl.ds(*parts[part])]
+        at = ((zz * 2 + yy) * 2 + xx) * 3 + part
+        return pltpu.make_async_remote_copy(
+            src_ref=region,
+            dst_ref=region,
+            send_sem=send_sem.at[way * 48 + at],
+            recv_sem=core_recv.at[at] if way == sibling else link_recv.at[at],
+            device_id=devices[way],
+            device_id_type=MESH,
+        )
+
+    def came(zz, yy, xx, part):
+        copy(across, zz, yy, xx, part).wait_recv()
+
+    def along(zz, yy, xx, part):
+        @pl.when((z < 3) & (zz <= z))
+        def send_up():
+            copy(up, zz, yy, xx, part).start()
+
+        @pl.when((z > 0) & (zz >= z))
+        def send_down():
+            copy(down, zz, yy, xx, part).start()
+
+    def early(k):
+        zz = order[k]
+        for part in range(2):
+            if k > 0:
+                came(zz, y, x, part)
+            along(zz, y, x, part)
+            for way in (beside, across) if part == 0 else (across, beside):
+                copy(way, zz, y, x, part).start()
+            copy(sibling, zz, y, x, part).start()
+
+    def middle(k):
+        zz = order[k]
+        came(zz, 1 - y, x, 0)
+        copy(across, zz, 1 - y, x, 0).start()
+        came(zz, y, 1 - x, 1)
+        copy(beside, zz, y, 1 - x, 1).start()
+        copy(sibling, zz, 1 - y, x, 0).start()
+        copy(sibling, zz, y, 1 - x, 1).start()
+
+    def late(k):
+        zz = order[k]
+        for yy, xx, part in ((y, 1 - x, 0), (1 - y, x, 1), (1 - y, 1 - x, 0), (1 - y, 1 - x, 1)):
+            came(zz, yy, xx, part)
+            copy(sibling, zz, yy, xx, part).start()
+
+    def last_own(k):
+        if k == 0:
+            copy(across, z, y, x, 2).start()
+            copy(beside, z, y, x, 2).start()
+            regions = [(y, x)]
+        elif k == 1:
+            came(z, y, 1 - x, 2)
+            copy(beside, z, y, 1 - x, 2).start()
+            regions = [(y, 1 - x)]
+        else:
+            regions = [(1 - y, x), (1 - y, 1 - x)]
+        for yy, xx in regions:
+            if k == 2:
+                came(z, yy, xx, 2)
+            along(z, yy, xx, 2)
+            copy(sibling, z, yy, xx, 2).start()
+
+    def last(k):
+        zz = order[k]
+        for yy, xx in ((y, x), (y, 1 - x), (1 - y, x), (1 - y, 1 - x)):
+            came(zz, yy, xx, 2)
+            along(zz, yy, xx, 2)
+            copy(sibling, zz, yy, xx, 2).start()
+
+    for stage, k in (
+        (early, 0),
+        (last_own, 0),
+        (last_own, 1),
+        (early, 1),
+        (middle, 0),
+        (last_own, 2),
+        (early, 2),
+        (middle, 1),
+        (early, 3),
+        (last, 1),
+        (late, 0),
+        (middle, 2),
+        (last, 2),
+        (late, 1),
+        (middle, 3),
+        (last, 3),
+        (late, 2),
+        (late, 3),
+    ):
+        stage(k)
+
+    for zz in range(4):
+        for yy in range(2):
+            for xx in range(2):
+                for part in range(3):
+                    copy(sibling, zz, yy, xx, part, 1 - c).wait_recv()
+                    copy(sibling, zz, yy, xx, part).wait_send()
+
+    def sent_along(zz, yy, xx, part):
+        @pl.when((z < 3) & (zz <= z))
+        def sent_up():
+            copy(up, zz, yy, xx, part).wait_send()
+
+        @pl.when((z > 0) & (zz >= z))
+        def sent_down():
+            copy(down, zz, yy, xx, part).wait_send()
+
+    for zz in range(4):
+        for part in range(2):
+            sent_along(zz, y, x, part)
+            copy(beside, zz, y, x, part).wait_send()
+            copy(across, zz, y, x, part).wait_send()
+        copy(across, zz, 1 - y, x, 0).wait_send()
+        copy(beside, zz, y, 1 - x, 1).wait_send()
+        for yy in range(2):
+            for xx in range(2):
+                sent_along(zz, yy, xx, 2)
+    copy(across, z, y, x, 2).wait_send()
+    copy(beside, z, y, x, 2).wait_send()
+    copy(beside, z, y, 1 - x, 2).wait_send()
+
+
+def gather_shards(shard):
+    block, width = shard.shape
+    dma = pltpu.SemaphoreType.DMA
+    gathered = pl.pallas_call(
+        gather_kernel,
+        out_shape=jax.ShapeDtypeStruct((4, 2, 2, 2, block, width), shard.dtype),
+        in_specs=[pl.BlockSpec(memory_space=pl.ANY)],
+        out_specs=pl.BlockSpec(memory_space=pl.ANY),
+        scratch_shapes=[dma, dma((240,)), dma((48,)), dma((48,))],
+        compiler_params=pltpu.CompilerParams(
+            collective_id=1, has_side_effects=True, vmem_limit_bytes=56 * 2**20
+        ),
+        cost_estimate=pl.CostEstimate(
+            flops=0, bytes_accessed=64 * shard.size, transcendentals=0
+        ),
+        name="gather_shards",
+    )(shard)
+    return gathered.reshape(32 * block, width)
 
 
 def local(
@@ -744,12 +1197,13 @@
     group_rows = pred_rows.shape[0]
 
     bias_wide = to_all(bias_master.astype(jnp.bfloat16), devices).astype(jnp.float32)
-    proj_rows = lax.all_gather(
-        proj_master.astype(jnp.bfloat16).T, ("dp", "stream"), axis=0, tiled=True
-    )
-    down_weight = lax.all_gather(
-        down_master.astype(jnp.bfloat16), ("dp", "stream"), axis=0, tiled=True
-    )
+    proj_low = proj_master.astype(jnp.bfloat16).T
+    if dp_count == 16:
+        proj_rows = gather_shards(proj_low)
+    else:
+        proj_rows = lax.all_gather(proj_low, ("dp", "stream"), axis=0, tiled=True)
+    down_low = lax.optimization_barrier((down_master.astype(jnp.bfloat16), proj_rows))[0]
+    down_weight = lax.all_gather(down_low, ("dp", "stream"), axis=0, tiled=True)
     query_weight = proj_rows[0:D]
     keys_weight = proj_rows[D : 3 * D]
     out_weight = proj_rows[3 * D : 4 * D]
@@ -832,95 +1286,50 @@
     )
     ffn_grad = sum_three.astype(jnp.bfloat16)
     slab = proj_rows.shape[0] // 4
-    down_sum = Scatter(column_sums(active_low, ffn_grad), range(4), dp_count)
-    down_sum.step()
+    down_part = sum_shares(column_sums(active_low, ffn_grad))
     pre_grad = (times_transpose(ffn_grad, down_weight) * slope_low.astype(jnp.float32)).astype(
         jnp.bfloat16
     )
-    pre_grad = after(pre_grad, down_sum)
     up_cut = 3 * slab - cross_start - 4 * D
-    slab_three = Scatter(column_sums(pre_grad[:, up_cut:], two_low), range(3, 4), dp_count)
-    up_rows = column_sums(pre_grad[:, :up_cut], two_low)
-    down_sum.step()
-    slab_three.step()
+    up_part = sum_shares(column_sums(pre_grad, two_low))
     two_grad = sum_three + matmul(pre_grad, up_weight)
-    two_grad = after(two_grad, slab_three)
 
     sum_two, gain_two, shift_two = norm_back(norm_two_in, stats_two, small_master[2], two_grad)
     branch_grad = sum_two.astype(jnp.bfloat16)
     cross_low_grad = matmul(branch_grad, back_weight).astype(jnp.bfloat16)
-    cross_low_grad = after(cross_low_grad, down_sum)
-    down_sum.step()
-    slab_three.step()
-    back_rows = column_sums(branch_grad, cross_low)
     cquery_grad, ckey_grad, cvalue_grad = cross_backward(
         cross_query, cross_pairs, cross_mask, cross_log, cross_low_grad
     )
-    cquery_grad = after(cquery_grad, down_sum, slab_three)
-    down_sum.step()
-    slab_three.step()
-    ckey_rows = column_sums(ckey_grad, enc_all)
-    cvalue_rows = column_sums(cvalue_grad, enc_all)
     enc_grad = pair_sum(matmul(ckey_grad, pair_weight[:D]) + matmul(cvalue_grad, pair_weight[D:]))
     one_grad = sum_two + matmul(cquery_grad, cross_weight)
 
     sum_one, gain_one, shift_one = norm_back(norm_one_in, stats_one, small_master[1], one_grad)
     attn_grad = sum_one.astype(jnp.bfloat16)
-    out_rows = column_sums(attn_grad, context_low)
-    out_cut = slab - 3 * D
-    ckey_cut = 2 * slab - cross_start - D
-    slab_middle = Scatter(
-        jnp.concatenate(
-            [
-                out_rows[out_cut:],
-                jnp.zeros((rel_width, D), jnp.bfloat16),
-                column_sums(cquery_grad, one_low),
-                ckey_rows,
-                cvalue_rows,
-                back_rows,
-                up_rows,
-            ]
-        ),
-        range(1, 3),
-        dp_count,
-    )
-    slab_middle.step()
     context_grad = matmul(attn_grad, out_weight).astype(jnp.bfloat16)
-    context_grad = after(context_grad, slab_middle, slab_three)
-    slab_middle.step()
-    slab_three.step()
     query_grad, key_grad, value_grad, table_wide = self_backward(
         query_low, self_pairs, table, spread, edge, turn, self_mask, self_log, context_grad
     )
-    table_wide = after(table_wide, slab_middle, slab_three)
-    slab_middle.step()
+    table_wide = lax.optimization_barrier((table_wide, down_part))[0]
     table_grad = table_wide.astype(jnp.bfloat16)
-    table_sum = Scatter(column_sums(table_grad, inputs), range(4), dp_count, 1)
-    slab_zero = Scatter(
-        jnp.concatenate(
-            [
-                column_sums(query_grad, inputs),
-                column_sums(key_grad, key_inputs),
-                column_sums(value_grad, key_inputs),
-                out_rows[:out_cut],
-            ]
-        ),
-        range(0, 1),
-        dp_count,
-    )
-    device = lax.axis_index("dp") * 2 + lax.axis_index("stream")
-    table_total = (
-        to_all(table_sum.finish().astype(jnp.bfloat16), devices)
+    table_rows = (
+        column_sums(table_grad, inputs)
         .reshape(HEADS, BUCKETS, D)
         .transpose(1, 0, 2)
         .reshape(rel_width, D)
-        .astype(jnp.float32)
-    )
-    shard = proj_rows.shape[0] // devices
-    table_part = lax.dynamic_slice_in_dim(
-        jnp.pad(table_total, ((shard, shard), (0, 0))),
-        jnp.clip((device + 1) * shard - 4 * D, 0, rel_width + shard),
-        shard,
+    )
+    late_rows = jnp.concatenate(
+        [
+            column_sums(query_grad, inputs),
+            column_sums(key_grad, key_inputs),
+            column_sums(value_grad, key_inputs),
+            column_sums(attn_grad, context_low),
+            table_rows,
+            column_sums(cquery_grad, one_low),
+            column_sums(ckey_grad, enc_all),
+            column_sums(cvalue_grad, enc_all),
+            column_sums(branch_grad, cross_low),
+            column_sums(pre_grad[:, :up_cut], two_low),
+        ]
     )
     pair_input_grad = matmul(key_grad, keys_weight[:D]) + matmul(value_grad, keys_weight[D:])
     query_input_grad = (
@@ -957,14 +1366,15 @@
     bias_grad = vector_sum[:bias_len]
     small_grad = to_all(vector_sum[bias_len:], devices).reshape(small_master.shape)
 
+    slab_three = to_last_quarter(up_part, devices, up_cut)
+    late_rows = lax.optimization_barrier((late_rows, vector_sum, slab_three))[0]
+    if dp_count == 16:
+        late_sum = sum_slabs(late_rows, 3)
+    else:
+        late_sum = Scatter(late_rows, range(3), dp_count).finish()
     outer = place_on(("dp", dp_count // 4, 4))
-    proj_sum = jnp.where(
-        outer == 0,
-        slab_zero.finish(),
-        jnp.where(outer == 3, slab_three.finish(), slab_middle.finish()),
-    )
-    proj_grad = (proj_sum + table_part).T
-    down_grad = down_sum.finish()
+    proj_grad = jnp.where(outer == 3, slab_three.astype(jnp.float32), late_sum).T
+    down_grad = down_part.astype(jnp.float32)
     return (
         final_rows[:half_rows],
         final_rows[half_rows:],

time: 1000 us -> 806 us (0.81)
  waiting for transfers between devices: 257 us -> 14.9 us
  Pallas kernels: 176 us -> 407 us
  starting transfers between devices: 126 us -> 39.4 us
  other arithmetic: 119 us -> 47 us
  local copies, waits for them, and re-layouts: 64.4 us -> 29.1 us
  matrix products: 232 us -> 246 us
    pallas_call x0 -> x2, Pallas kernels: none -> 230 us  [the longest x1 122 us: gather_shards(): pl.pallas_call(gather_kernel, out_shape=jax.ShapeDtypeStruct((4, 2, 2, 2,...]
    all_gather x2 -> x1, waiting for transfers between devices: 115 us -> 0.02 us  [local(): down_weight = lax.all_gather(down_low, ('dp', 'stream'), axis=0, tiled=True)]
    ppermute x50 -> x5, waiting for transfers between devices: 97.4 us -> 0.01 us  [to_last_quarter(): blocks.append(lax.ppermute(share, ('dp', 'stream'), pairs))]
    ppermute x50 -> x5, starting transfers between devices: 62.8 us -> 19 us  [to_last_quarter(): blocks.append(lax.ppermute(share, ('dp', 'stream'), pairs))]
    ppermute x4, waiting for transfers between devices: 40.9 us -> 0.01 us  [swap_streams(): return lax.ppermute(rows, 'stream', [(0, 1), (1, 0)])]
    convert_element_type x22 -> x0, other arithmetic: 39.1 us -> none  [the longest x21 39.1 us: scatter_level(): return total.astype(final_type)]
    all_to_all x3 -> x2, starting transfers between devices: 34.7 us -> 10.8 us  [to_all(): gathered = lax.all_to_all(shared, ('dp', 'stream'), 0, 0, tiled=True)]
    all_to_all x1, starting transfers between devices: 24.9 us -> 6.33 us  [local(): lax.all_to_all(vector_parts, ('dp', 'stream'), 0, 0, tiled=True)]
  transfers between devices with their start and end apart: 60 -> 17, of which waited for: 17 -> 2; matrix products, arithmetic and copies ran while one was open for 29% -> 34% of each run, Pallas kernels for 11% -> 51%
where the time goes in v3:
time: 806 us; the launch traced here: 799 us
  Pallas kernels  407 us (50%)
  matrix products  246 us (31%)
  other arithmetic  47 us (6%)
  starting transfers between devices  39.4 us (5%)
  local copies, waits for them, and re-layouts  29.1 us (4%)
  between operations  15.5 us (2%)
  waiting for transfers between devices  14.9 us (2%)
    pallas_call x4, Pallas kernels, attention_call(): pl.pallas_call(kernel, grid=(HEADS // 2,), in_specs=in_specs, out_specs=o...  177 us
    pallas_call x1, Pallas kernels, gather_shards(): pl.pallas_call(gather_kernel, out_shape=jax.ShapeDtypeStruct((4, 2, 2, 2,...  122 us
    pallas_call x1, Pallas kernels, sum_slabs(): pl.pallas_call(sum_kernel, out_shape=jax.ShapeDtypeStruct((block, width),...  108 us
    dot_general x9, matrix products, times_transpose(): lax.dot_general(left_side, right_side, (((1,), (1,)), ((), ())), preferre...  105 us
    dot_general x11, matrix products, matmul(): return jnp.dot(left_side, right_side, preferred_element_type=jnp.float32)  73.8 us
    dot_general x12, matrix products, outer_sum(): lax.dot_general(left_side, right_side, (((0,), (0,)), ((), ())), preferre...  67.7 us
    ppermute x5, starting transfers between devices, to_last_quarter(): blocks.append(lax.ppermute(share, ('dp', 'stream'), pairs))  19 us
    unnamed x168, local copies, waits for them, and re-layouts  16.6 us
  transfers between devices with their start and end apart: 17, of which 2 were waited for; matrix products, arithmetic and copies ran while one was open for 34% of the time, Pallas kernels for 51%

profile of v3, /device:TPU:11, one launch (start us, length us, event | category | flops | bytes accessed | tf_op | source)
XLA Modules:
  0.0 798.8 jit_solution(4366986694564842408)
XLA Ops:
  11.4 6.9 all-to-all-start
  20.8 122.1 %gather_shards.1 = bf16[4,2,2,2,400,1024]{5,4,3,2,1,0:T(8,128)(2,1)} custom-call(bf16[400,1024]{1,0:T(8,128)(2,1)} %convert_bitcast_fusion.shard_ref), custom_call_target="tpu_custom_call" | custom-call | bytes 26214400 | tf_op jit(solution)/shard_map/gather_shards/pallas_call | solution.py:1155
  152.8 3.0 broadcast_select_fusion.1
  158.5 5.2 add_convert_fusion.5.query_ref
  163.7 11.4 %add_convert_fusion.1.key_ref.value_ref.own_key_ref.own_value_ref = bf16[1280,2048]{1,0:T(8,128)(2,1)} fusion(f32[2048]{0:T(1024)S(1)} %concatenate.45, bf16[12800,1024]{1,0:T(8,128)(2,1)} %bitcast.61, bf16[640,1024]{1,0:T(8,128)(2,1)S(1)} %copy-done.29, bf16[320,1024]{1,0:T(8,128)(2,1)S(1)} %get-tuple-element.115, bf16[320,1024]{1,0:T(8,128)(2,1)S(1)} %get-tuple-element.116), kind=kOutput, calls=%fused_computation.7 | convolution fusion | flops 5381816320 | bytes 12066816 | tf_op jit(solution)/shard_map/dot_general | solution.py:60
  176.1 36.2 %self_forward.1 = (bf16[960,1024]{1,0:T(8,128)(2,1)}, f32[960,1024]{1,0:T(8,128)}) custom-call(bf16[960,1024]{1,0:T(8,128)(2,1)} %add_convert_fusion.5.query_ref, bf16[1280,2048]{1,0:T(8,128)(2,1)} %add_convert_fusion.1.key_ref.value_ref.own_key_ref.own_value_ref, bf16[1280,2048]{1,0:T(8,128)(2,1)} %add_convert_fusion.1.key_ref.value_ref.own_key_ref.own_value_ref, ...), custom_call_target="tpu_custom_call" | custom-call | flops 2516582400 | bytes 34242560 | tf_op jit(solution)/shard_map/self_forward/pallas_call | solution.py:446
  212.3 4.6 fusion.89
  218.4 6.9 add_convert_fusion.2.key_ref.value_ref
  225.3 5.1 add_convert_fusion.4.query_ref
  230.4 27.9 %cross_forward.1 = (bf16[960,1024]{1,0:T(8,128)(2,1)}, f32[960,1024]{1,0:T(8,128)}) custom-call(bf16[960,1024]{1,0:T(8,128)(2,1)} %add_convert_fusion.4.query_ref, bf16[640,2048]{1,0:T(8,128)(2,1)} %add_convert_fusion.2.key_ref.value_ref, bf16[640,2048]{1,0:T(8,128)(2,1)} %add_convert_fusion.2.key_ref.value_ref, f32[960,640]{1,0:T(8,128)} %get-tuple-element.98.mask_ref), custom_call_target="tpu_custom_call" | custom-call | flops 2516582400 | bytes 15564800 | tf_op jit(solution)/shard_map/cross_forward/pallas_call | solution.py:446
  258.3 4.8 fusion.90
  265.0 32.3 %multiply_convert_fusion.1 = (bf16[960,4096]{1,0:T(8,128)(2,1)}, f32[960,4096]{1,0:T(8,128)}) fusion(f32[4096]{0:T(1024)S(1)} %slice.168, bf16[12800,1024]{1,0:T(8,128)(2,1)} %bitcast.66, f32[960,1024]{1,0:T(8,128)S(1)} %get-tuple-element.105, f32[1024]{0:T(1024)S(1)} %bitcast.98, f32[1024]{0:T(1024)S(1)} %bitcast.86, f32[960]{0:T(1024)S(1)} %add_rsqrt_fusion.1, ...), kind=kOutput, calls=%fused_computation.6 | convolution fusion | flops 8191672320 | bytes 35945984 | tf_op jit(solution)/shard_map/dot_general | solution.py:60
  297.4 14.1 %fusion.91 = (f32[960]{0:T(1024)S(1)}, f32[960,1024]{1,0:T(8,128)S(1)}) fusion(f32[1024]{0:T(1024)S(1)} %bitcast.105, bf16[960,4096]{1,0:T(8,128)(2,1)} %get-tuple-element.106, bf16[4096,1024]{1,0:T(8,128)(2,1)} %all-gather.2.cloned.1.call-done, f32[1024]{0:T(1024)S(1)} %bitcast.99, f32[1024]{0:T(1024)S(1)} %bitcast.87, f32[960]{0:T(1024)S(1)} %add_rsqrt_fusion.1, ...), kind=kOutput, calls=%fused_computation.208 | convolution fusion | flops 8059943936 | bytes 24141056 | tf_op jit(solution)/shard_map/dot_general | solution.py:50
  313.0 3.7 fusion.14
  316.8 4.4 convert_reduce_fusion.3
  323.0 11.4 %convolution_convert_fusion.1 = bf16[4096,1024]{1,0:T(8,128)(2,1)} fusion(bf16[960,4096]{1,0:T(8,128)(2,1)S(1)} %bitcast.109, f32[960,1024]{1,0:T(8,128)S(1)} %get-tuple-element.74), kind=kOutput, calls=%fused_computation.9 | convolution fusion | flops 8058241024 | bytes 20185088 | tf_op jit(solution)/shard_map/dot_general | solution.py:54
  334.6 31.9 %convert_reduce_fusion = (f32[4096]{0:T(1024)S(1)}, bf16[960,4096]{1,0:T(8,128)(2,1)S(1)}) fusion(f32[960,4096]{1,0:T(8,128)} %get-tuple-element.107, f32[4096]{0:T(1024)S(1)} %slice.168, bf16[4096,1024]{1,0:T(8,128)(2,1)} %all-gather.2.cloned.1.call-done, f32[960,1024]{1,0:T(8,128)} %copy-done.19), kind=kOutput, calls=%fused_computation.3 | convolution fusion | flops 8215261184 | bytes 35946496 | tf_op jit(solution)/shard_map/dot_general | solution.py:60
  366.5 3.2 copy-done.68
  369.7 12.4 %convolution_convert_fusion = bf16[4096,1024]{1,0:T(8,128)(2,1)} fusion(bf16[960,4096]{1,0:T(8,128)(2,1)S(1)} %get-tuple-element.113, f32[960,1024]{1,0:T(8,128)S(1)} %copy-done.4, f32[1024]{0:T(1024)S(1)} %bitcast.100, f32[1024]{0:T(1024)S(1)} %bitcast.88, f32[960]{0:T(1024)S(1)} %add_rsqrt_fusion.1, f32[960]{0:T(1024)S(1)} %broadcast_multiply_fusion.7), kind=kOutput, calls=%fused_computation.8 | convolution fusion | flops 8062173184 | bytes 20200960 | tf_op jit(solution)/shard_map/dot_general | solution.py:54
  382.1 16.3 %multiply_reduce_fusion = (f32[1024]{0:T(1024)S(1)}, f32[960]{0:T(1024)S(1)}, f32[960]{0:T(1024)S(1)}, f32[1024]{0:T(1024)S(1)}, f32[960,1024]{1,0:T(8,128)S(1)}) fusion(f32[960,1024]{1,0:T(8,128)} %copy-done.3, f32[960]{0:T(1024)S(1)} %add_rsqrt_fusion.1, f32[960]{0:T(1024)S(1)} %broadcast_multiply_fusion.7, f32[1024]{0:T(1024)S(1)} %bitcast.89, ...), kind=kOutput, calls=%fused_computation.30 | convolution fusion | flops 8062889984 | bytes 28077056 | tf_op jit(solution)/shard_map/dot_general | solution.py:50
  399.9 6.5 fusion.49.context_ref
  406.5 44.9 %cross_backward.1 = (bf16[960,1024]{1,0:T(8,128)(2,1)}, bf16[640,1024]{1,0:T(8,128)(2,1)}, bf16[640,1024]{1,0:T(8,128)(2,1)}) custom-call(bf16[960,1024]{1,0:T(8,128)(2,1)} %add_convert_fusion.4.query_ref, bf16[640,2048]{1,0:T(8,128)(2,1)} %add_convert_fusion.2.key_ref.value_ref, bf16[640,2048]{1,0:T(8,128)(2,1)} %add_convert_fusion.2.key_ref.value_ref, ...), custom_call_target="tpu_custom_call" | custom-call | flops 6291456000 | bytes 20152320 | tf_op jit(solution)/shard_map/cross_backward/pallas_call | solution.py:446
  451.4 3.6 fusion.28
  455.1 3.5 fusion.55
  460.6 5.0 multiply_reduce_fusion.1
  467.1 6.7 fusion.46.context_ref
  473.9 67.7 %self_backward.1 = (bf16[960,1024]{1,0:T(8,128)(2,1)}, bf16[1280,1024]{1,0:T(8,128)(2,1)}, bf16[1280,1024]{1,0:T(8,128)(2,1)}, f32[960,512]{1,0:T(8,128)}) custom-call(bf16[960,1024]{1,0:T(8,128)(2,1)} %add_convert_fusion.5.query_ref, bf16[1280,2048]{1,0:T(8,128)(2,1)} %add_convert_fusion.1.key_ref.value_ref.own_key_ref.own_value_ref, ...), custom_call_target="tpu_custom_call" | custom-call | flops 6291456000 | bytes 43909120 | tf_op jit(solution)/shard_map/self_backward/pallas_call | solution.py:446
  546.6 5.9 fusion.43
  552.5 3.8 convert_dynamic-update-slice_fusion.7
  556.3 4.6 fusion.33
  561.0 4.2 convert_dynamic-update-slice_fusion.6
  565.2 4.2 convert_dynamic-update-slice_fusion.5
  569.3 6.3 convolution_add_fusion
  577.9 6.6 convert_dynamic-update-slice_fusion.4
  586.8 10.4 %reduce-scatter.7.cloned.1.call-done = bf16[128,1024]{1,0:T(8,128)(2,1)} async-done(((bf16[256,1024]{1,0:T(8,128)(2,1)}), bf16[128,1024]{1,0:T(8,128)(2,1)}) %reduce-scatter.7.cloned.1.call-update) | async-done | bytes 262160 | tf_op jit(solution)/shard_map/reduce_scatter | solution.py:684
  597.4 3.8 convolution_convert_fusion.2
  602.4 6.3 all-to-all-start.1
  611.8 5.8 convert_dynamic-update-slice_fusion.3
  617.6 3.2 convert_dynamic-update-slice_fusion.2
  620.8 3.2 convert_dynamic-update-slice_fusion.1
  630.5 3.8 convert_dynamic-update-slice_fusion
  634.4 5.4 convert_dynamic-update-slice_fusion.8
  641.1 6.8 collective-permute-start.5
  654.1 3.9 all-to-all-start.2
  658.6 4.4 all-to-all-done.2
  663.9 8.2 %collective-permute-start.8 = (bf16[128,1024]{1,0:T(8,128)(2,1)}, bf16[128,1024]{1,0:T(8,128)(2,1)S(1)}, u32[]{:S(2)}, u32[]{:S(2)}) collective-permute-start(bf16[128,1024]{1,0:T(8,128)(2,1)} %reduce-scatter.11.cloned.1.call-done), channel_id=1, source_target_pairs={{11,24},{14,25},{17,26},{20,27},{23,28},{26,29},{29,30}} | collective-permute-start | bytes 786440 | tf_op jit(solution)/shard_map/ppermute | solution.py:699
  676.0 107.8 %sum_slabs.1 = f32[400,1024]{1,0:T(8,128)} custom-call(bf16[3,2,2,2,400,1024]{5,4,3,2,1,0:T(8,128)(2,1)} %bitcast.19.grad_ref), custom_call_target="tpu_custom_call" | custom-call | flops 9830400 | bytes 39321600 | tf_op jit(solution)/shard_map/sum_slabs/pallas_call | solution.py:955
  783.8 5.3 multiply_subtract_fusion
  (282 shorter events, 67.7 us)
Async XLA Ops:
  7.2 145.6 %collective-permute-start = (bf16[320,1024]{1,0:T(8,128)(2,1)}, bf16[320,1024]{1,0:T(8,128)(2,1)}, u32[]{:S(2)}, u32[]{:S(2)}) collective-permute-start(bf16[320,1024]{1,0:T(8,128)(2,1)} %param.18), channel_id=1, source_target_pairs={{0,1},{1,0},{2,3},{3,2},{4,5},{5,4},{6,7},{7,6},{8,9},{9,8},{10,11... | collective-permute-start | bytes 1966088 | tf_op jit(solution)/shard_map/ppermute | solution.py:712
  7.5 145.3 %collective-permute-start.1 = (bf16[320,1024]{1,0:T(8,128)(2,1)}, bf16[320,1024]{1,0:T(8,128)(2,1)}, u32[]{:S(2)}, u32[]{:S(2)}) collective-permute-start(bf16[320,1024]{1,0:T(8,128)(2,1)} %param.20), channel_id=1, source_target_pairs={{0,1},{1,0},{2,3},{3,2},{4,5},{5,4},{6,7},{7,6},{8,9},{9,8},{10,11... | collective-permute-start | bytes 1966088 | tf_op jit(solution)/shard_map/ppermute | solution.py:712
  11.4 140.5 %all-to-all-start = ((bf16[32,2,168]{2,1,0:T(2,128)(2,1)}), bf16[32,2,168]{2,1,0:T(2,128)(2,1)S(1)}, u32[]{:S(2)}, u32[]{:S(2)}) async-start(bf16[32,2,168]{2,1,0:T(2,128)(2,1)} %reshape.217), calls=%async_computation | async-start | bytes 65536 | tf_op jit(solution)/shard_map/all_to_all | solution.py:707
  18.3 279.0 %all-gather.2.cloned.1.call-start = ((), (), s32[]{:S(2)}) async-start(), calls=%async_computation.7 | async-start | bytes 8650752 | tf_op jit(solution)/shard_map/all_gather | solution.py:1206
  20.8 122.2 %copy-start.22 = (f32[128,1024]{1,0:T(8,128)S(1)}, f32[128,1024]{1,0:T(8,128)}, u32[]{:S(2)}) copy-start(f32[128,1024]{1,0:T(8,128)} %param.30) | copy-start | bytes 1572868
  20.8 123.2 %copy-start.65 = (s32[1,8]{1,0:T(1,128)S(1)}, s32[1,8]{1,0:T(1,128)}, u32[]{:S(2)}) copy-start(s32[1,8]{1,0:T(1,128)} %param.21) | copy-start | bytes 100
  143.8 431.9 %reduce-scatter.5.cloned.1.call-start = ((), (), s32[]{:S(2)}) async-start(), calls=%async_computation.8 | async-start | bytes 8912896 | tf_op jit(solution)/shard_map/reduce_scatter | solution.py:683
  150.0 108.3 %copy-start.51 = (f32[1,1024]{1,0:T(1,128)}, f32[1,1024]{1,0:T(1,128)S(1)}, u32[]{:S(2)}) copy-start(f32[1,1024]{1,0:T(1,128)S(1)} %get-tuple-element.96) | copy-start | bytes 12292
  150.0 108.3 %copy-start.60 = (f32[1,1024]{1,0:T(1,128)}, f32[1,1024]{1,0:T(1,128)S(1)}, u32[]{:S(2)}) copy-start(f32[1,1024]{1,0:T(1,128)S(1)} %get-tuple-element.95) | copy-start | bytes 12292
  155.8 7.9 copy-start.37
  155.8 7.9 copy-start.39
  155.8 61.7 %copy-start.33 = (bf16[320,1024]{1,0:T(8,128)(2,1)}, bf16[320,1024]{1,0:T(8,128)(2,1)S(1)}, u32[]{:S(2)}) copy-start(bf16[320,1024]{1,0:T(8,128)(2,1)S(1)} %get-tuple-element.80) | copy-start | bytes 1966084
  176.1 36.2 %copy-start.42 = (bf16[960,1024]{1,0:T(8,128)(2,1)S(1)}, bf16[960,1024]{1,0:T(8,128)(2,1)}, u32[]{:S(2)}) copy-start(bf16[960,1024]{1,0:T(8,128)(2,1)} %copy-done.41) | copy-start | bytes 5898244
  216.9 41.5 %copy-start.7 = (f32[960,1024]{1,0:T(8,128)}, f32[960,1024]{1,0:T(8,128)S(1)}, u32[]{:S(2)}) copy-start(f32[960,1024]{1,0:T(8,128)S(1)} %get-tuple-element.103) | copy-start | bytes 11796484
  216.9 41.4 %copy-start.46 = (f32[960]{0:T(1024)}, f32[960]{0:T(1024)S(1)}, u32[]{:S(2)}) copy-start(f32[960]{0:T(1024)S(1)} %broadcast_multiply_fusion.8) | copy-start | bytes 11524
  217.5 40.9 %copy-start.53 = (f32[960]{0:T(1024)}, f32[960]{0:T(1024)S(1)}, u32[]{:S(2)}) copy-start(f32[960]{0:T(1024)S(1)} %add_rsqrt_fusion.2) | copy-start | bytes 11524
  313.0 10.0 %slice-start.2 = ((s8[7864320]{0:T(1024)(128)(4,1)}), s8[4194304]{0:T(1024)(128)(4,1)S(1)}, s32[]{:S(2)}) async-start(s8[7864320]{0:T(1024)(128)(4,1)} %bitcast.108), calls=%async_computation.14 | async-start | bytes 8388608
  334.5 252.3 %reduce-scatter.9.cloned.1.call-start = ((), (), s32[]{:S(2)}) async-start(), calls=%async_computation.10 | async-start | bytes 8912896 | tf_op jit(solution)/shard_map/reduce_scatter | solution.py:683
  334.6 35.1 %copy-start.4 = (f32[960,1024]{1,0:T(8,128)S(1)}, f32[960,1024]{1,0:T(8,128)}, u32[]{:S(2)}) copy-start(f32[960,1024]{1,0:T(8,128)} %copy-done.3) | copy-start | bytes 11796484
  382.1 215.2 %reduce-scatter.7.cloned.1.call-start = ((), (), s32[]{:S(2)}) async-start(), calls=%async_computation.9 | async-start | bytes 786432 | tf_op jit(solution)/shard_map/reduce_scatter | solution.py:684
  382.1 16.3 %copy-start.5 = (f32[960,1024]{1,0:T(8,128)S(1)}, f32[960,1024]{1,0:T(8,128)}, u32[]{:S(2)}) copy-start(f32[960,1024]{1,0:T(8,128)} %copy-done.3) | copy-start | bytes 11796484
  399.9 60.7 %copy-start.17 = (f32[960,1024]{1,0:T(8,128)}, f32[960,1024]{1,0:T(8,128)S(1)}, u32[]{:S(2)}) copy-start(f32[960,1024]{1,0:T(8,128)S(1)} %get-tuple-element.70) | copy-start | bytes 11796484
  459.6 124.9 %collective-permute-start.3 = (bf16[320,1024]{1,0:T(8,128)(2,1)}, bf16[320,1024]{1,0:T(8,128)(2,1)}, u32[]{:S(2)}, u32[]{:S(2)}) collective-permute-start(bf16[320,1024]{1,0:T(8,128)(2,1)} %dynamic-slice_convert_fusion), channel_id=1, source_target_pairs={{0,1},{1,0},{2,3},{3,2},{4,5},{5,4},{6,7},{7,6},{8,9},{9,8},{10,11... | collective-permute-start | bytes 1966088 | tf_op jit(solution)/shard_map/ppermute | solution.py:712
  467.1 6.7 copy-start
  473.9 69.8 %copy-start.58 = (f32[1024]{0:T(1024)S(1)}, f32[1024]{0:T(1024)}, u32[]{:S(2)}) copy-start(f32[1024]{0:T(1024)} %get-tuple-element.73) | copy-start | bytes 12292
  569.3 6.4 copy-start.56
  569.3 6.4 copy-start.10
  575.7 64.1 %reduce-scatter.11.cloned.1.call-start = ((), (), s32[]{:S(2)}) async-start(), calls=%async_computation.11 | async-start | bytes 786432 | tf_op jit(solution)/shard_map/reduce_scatter | solution.py:684
  577.9 6.6 copy-start.28
  584.5 12.8 %copy-start.11 = (f32[960,512]{1,0:T(8,128)S(1)}, f32[960,512]{1,0:T(8,128)}, u32[]{:S(2)}) copy-start(f32[960,512]{1,0:T(8,128)} %get-tuple-element.39) | copy-start | bytes 5898244
  601.2 10.5 %copy-start.61 = (f32[1,1024]{1,0:T(1,128)S(1)}, f32[1,1024]{1,0:T(1,128)}, u32[]{:S(2)}) copy-start(f32[1,1024]{1,0:T(1,128)} %copy-done.60) | copy-start | bytes 12292
  602.4 50.9 %all-to-all-start.1 = ((f32[32,1,560]{2,1,0:T(1,128)}), f32[32,1,560]{2,1,0:T(1,128)S(1)}, u32[]{:S(2)}, u32[]{:S(2)}) async-start(f32[32,1,560]{2,1,0:T(1,128)} %all_to_all.15), calls=%async_computation.5 | async-start | bytes 163840 | tf_op jit(solution)/shard_map/all_to_all | solution.py:1363
  629.3 159.9 %collective-permute-start.2 = (bf16[320,1024]{1,0:T(8,128)(2,1)}, bf16[320,1024]{1,0:T(8,128)(2,1)}, u32[]{:S(2)}, u32[]{:S(2)}) collective-permute-start(bf16[320,1024]{1,0:T(8,128)(2,1)} %dynamic-slice_convert_fusion.1), channel_id=1, source_target_pairs={{0,1},{1,0},{2,3},{3,2},{4,5},{5,4},{6,7},{7,6},{8,9},{9,8},{10,11... | collective-permute-start | bytes 1966088 | tf_op jit(solution)/shard_map/ppermute | solution.py:712
  634.3 16.3 %copy-start.23 = (f32[128,1024]{1,0:T(8,128)S(1)}, f32[128,1024]{1,0:T(8,128)}, u32[]{:S(2)}) copy-start(f32[128,1024]{1,0:T(8,128)} %param.30) | copy-start | bytes 1572868
  634.3 23.7 %copy-start.59 = (f32[336]{0:T(512)S(1)}, f32[336]{0:T(512)}, u32[]{:S(2)}) copy-start(f32[336]{0:T(512)} %param.27) | copy-start | bytes 4036
  634.3 23.7 %copy-start.62 = (f32[336]{0:T(512)S(1)}, f32[336]{0:T(512)}, u32[]{:S(2)}) copy-start(f32[336]{0:T(512)} %param.28) | copy-start | bytes 4036
  634.3 23.7 %copy-start.63 = (f32[336]{0:T(512)S(1)}, f32[336]{0:T(512)}, u32[]{:S(2)}) copy-start(f32[336]{0:T(512)} %param.29) | copy-start | bytes 4036
  634.3 28.9 %copy-start.45 = (f32[7,1024]{1,0:T(8,128)S(1)}, f32[7,1024]{1,0:T(8,128)}, u32[]{:S(2)}) copy-start(f32[7,1024]{1,0:T(8,128)} %param.33) | copy-start | bytes 86020
  634.4 28.9 %copy-start.49 = (f32[7,1024]{1,0:T(8,128)S(1)}, f32[7,1024]{1,0:T(8,128)}, u32[]{:S(2)}) copy-start(f32[7,1024]{1,0:T(8,128)} %param.34) | copy-start | bytes 86020
  634.4 28.8 %copy-start.50 = (f32[7,1024]{1,0:T(8,128)S(1)}, f32[7,1024]{1,0:T(8,128)}, u32[]{:S(2)}) copy-start(f32[7,1024]{1,0:T(8,128)} %param.35) | copy-start | bytes 86020
  639.8 24.1 %collective-permute-start.4 = (bf16[128,1024]{1,0:T(8,128)(2,1)}, bf16[128,1024]{1,0:T(8,128)(2,1)}, u32[]{:S(2)}, u32[]{:S(2)}) collective-permute-start(bf16[128,1024]{1,0:T(8,128)(2,1)} %reduce-scatter.11.cloned.1.call-done), channel_id=1, source_target_pairs={{7,24},{10,25},{13,26},{16,27},{19,28},{22,29},{25,30},{28,31}} | collective-permute-start | bytes 786440 | tf_op jit(solution)/shard_map/ppermute | solution.py:699
  641.1 31.9 %collective-permute-start.5 = (bf16[128,1024]{1,0:T(8,128)(2,1)}, bf16[128,1024]{1,0:T(8,128)(2,1)}, u32[]{:S(2)}, u32[]{:S(2)}) collective-permute-start(bf16[128,1024]{1,0:T(8,128)(2,1)} %reduce-scatter.11.cloned.1.call-done), channel_id=1, source_target_pairs={{8,24},{11,25},{14,26},{17,27},{20,28},{23,29},{26,30},{29,31}} | collective-permute-start | bytes 786440 | tf_op jit(solution)/shard_map/ppermute | solution.py:699
  647.9 26.1 %collective-permute-start.6 = (bf16[128,1024]{1,0:T(8,128)(2,1)}, bf16[128,1024]{1,0:T(8,128)(2,1)}, u32[]{:S(2)}, u32[]{:S(2)}) collective-permute-start(bf16[128,1024]{1,0:T(8,128)(2,1)} %reduce-scatter.11.cloned.1.call-done), channel_id=1, source_target_pairs={{9,24},{12,25},{15,26},{18,27},{21,28},{24,29},{27,30},{30,31}} | collective-permute-start | bytes 786440 | tf_op jit(solution)/shard_map/ppermute | solution.py:699
  649.3 25.7 %collective-permute-start.7 = (bf16[128,1024]{1,0:T(8,128)(2,1)}, bf16[128,1024]{1,0:T(8,128)(2,1)}, u32[]{:S(2)}, u32[]{:S(2)}) collective-permute-start(bf16[128,1024]{1,0:T(8,128)(2,1)} %reduce-scatter.11.cloned.1.call-done), channel_id=1, source_target_pairs={{10,24},{13,25},{16,26},{19,27},{22,28},{25,29},{28,30},{31,31}} | collective-permute-start | bytes 786440 | tf_op jit(solution)/shard_map/ppermute | solution.py:699
  654.1 8.9 %all-to-all-start.2 = ((f32[32,1,224]{2,1,0:T(1,128)}), f32[32,1,224]{2,1,0:T(1,128)S(1)}, u32[]{:S(2)}, u32[]{:S(2)}) async-start(f32[32,1,224]{2,1,0:T(1,128)} %broadcast_in_dim.20), calls=%async_computation.6 | async-start | bytes 65536 | tf_op jit(solution)/shard_map/all_to_all | solution.py:707
  663.9 12.1 %collective-permute-start.8 = (bf16[128,1024]{1,0:T(8,128)(2,1)}, bf16[128,1024]{1,0:T(8,128)(2,1)S(1)}, u32[]{:S(2)}, u32[]{:S(2)}) collective-permute-start(bf16[128,1024]{1,0:T(8,128)(2,1)} %reduce-scatter.11.cloned.1.call-done), channel_id=1, source_target_pairs={{11,24},{14,25},{17,26},{20,27},{23,28},{26,29},{29,30}} | collective-permute-start | bytes 786440 | tf_op jit(solution)/shard_map/ppermute | solution.py:699
  676.0 107.8 %copy-start.12 = (f32[1024,400]{0,1:T(8,128)S(1)}, f32[1024,400]{0,1:T(8,128)}, u32[]{:S(2)}) copy-start(f32[1024,400]{0,1:T(8,128)} %param.24) | copy-start | bytes 4915204
  676.0 107.8 %copy-start.26 = (f32[1024,400]{0,1:T(8,128)S(1)}, f32[1024,400]{0,1:T(8,128)}, u32[]{:S(2)}) copy-start(f32[1024,400]{0,1:T(8,128)} %param.25) | copy-start | bytes 4915204
  (43 other events, 178.8 us)
Sparse Core Ops, SparseCore 0:
  143.9 84.3 all-gather.1
  334.6 111.2 reduce-scatter.4
  450.0 104.4 reduce-scatter.8
  575.8 21.4 reduce-scatter.6
  599.4 15.4 reduce-scatter.10

commit v4 on v3

--- a/solution.py
+++ b/solution.py
@@ -26,6 +26,8 @@
 RATE_SMALL = 0.5
 WEIGHT_DECAY = 0.01
 MASKED = -1e30
+FFN_TILE = 1024
+FFN_PART = 256
 MESH = pl.DeviceIdType.MESH
 
 
@@ -81,22 +83,12 @@
 
 def gelu_and_slope(values):
     size = jnp.abs(values) * (0.5**0.5)
-    place = 1.0 / (1.0 + 0.5 * size)
-    fit = 0.17087277
-    for coefficient in (
-        -0.82215223,
-        1.48851587,
-        -1.13520398,
-        0.27886807,
-        -0.18628806,
-        0.09678418,
-        0.37409196,
-        1.00002368,
-        -1.26551223,
-    ):
+    place = 1.0 / (1.0 + 0.3275911 * size)
+    fit = 1.061405429
+    for coefficient in (-1.453152027, 1.421413741, -0.284496736, 0.254829592):
         fit = fit * place + coefficient
     bell = jnp.exp(-size * size)
-    tail = 0.5 * place * bell * jnp.exp(fit)
+    tail = (0.5 * place) * (fit * bell)
     below = jnp.where(values >= 0.0, 1.0 - tail, tail)
     return values * below, below + values * bell * (1.0 / math.sqrt(2.0 * math.pi))
 
@@ -1169,6 +1161,45 @@
     return gathered.reshape(32 * block, width)
 
 
+def pre_kernel(grad_ref, weight_ref, slope_ref, pre_ref, sum_ref):
+    for at in range(0, weight_ref.shape[0], FFN_PART):
+        part = slice(at, at + FFN_PART)
+        pre = (
+            dot_rows(grad_ref[...], weight_ref[part, :]) * slope_ref[:, part].astype(jnp.float32)
+        ).astype(jnp.bfloat16)
+        pre_ref[:, part] = pre
+        sum_ref[:, part] = jnp.sum(pre.astype(jnp.float32), axis=0, keepdims=True)
+
+
+def pre_and_sum(grad, weight, slope):
+    count, depth = grad.shape
+    width = weight.shape[0]
+    columns = pl.BlockSpec((count, FFN_TILE), lambda tile: (0, tile))
+    vector = pl.BlockSpec((1, FFN_TILE), lambda tile: (0, tile))
+    pre, total = pl.pallas_call(
+        pre_kernel,
+        grid=(width // FFN_TILE,),
+        in_specs=[
+            pl.BlockSpec((count, depth), lambda tile: (0, 0)),
+            pl.BlockSpec((FFN_TILE, depth), lambda tile: (tile, 0)),
+            columns,
+        ],
+        out_specs=[columns, vector],
+        out_shape=[
+            jax.ShapeDtypeStruct((count, width), jnp.bfloat16),
+            jax.ShapeDtypeStruct((1, width), jnp.float32),
+        ],
+        compiler_params=pltpu.CompilerParams(vmem_limit_bytes=56 * 2**20),
+        cost_estimate=pl.CostEstimate(
+            flops=2 * count * depth * width,
+            bytes_accessed=2 * (count * depth + depth * width + 2 * count * width),
+            transcendentals=0,
+        ),
+        name="pre_and_sum",
+    )(grad, weight, slope)
+    return pre, total[0]
+
+
 def local(
     dp_count,
     main_rows,
@@ -1287,9 +1318,7 @@
     ffn_grad = sum_three.astype(jnp.bfloat16)
     slab = proj_rows.shape[0] // 4
     down_part = sum_shares(column_sums(active_low, ffn_grad))
-    pre_grad = (times_transpose(ffn_grad, down_weight) * slope_low.astype(jnp.float32)).astype(
-        jnp.bfloat16
-    )
+    pre_grad, pre_sum = pre_and_sum(ffn_grad, down_weight, slope_low)
     up_cut = 3 * slab - cross_start - 4 * D
     up_part = sum_shares(column_sums(pre_grad, two_low))
     two_grad = sum_three + matmul(pre_grad, up_weight)
@@ -1350,7 +1379,7 @@
             row_sum(cquery_grad),
             row_sum(cvalue_grad),
             row_sum(branch_grad),
-            row_sum(pre_grad),
+            pre_sum,
         ]
     )
     small_parts = jnp.concatenate(
@@ -1364,7 +1393,7 @@
     )
     bias_len = bias_master.shape[0]
     bias_grad = vector_sum[:bias_len]
-    small_grad = to_all(vector_sum[bias_len:], devices).reshape(small_master.shape)
+    small_sums = to_all(vector_sum[bias_len:], devices)
 
     slab_three = to_last_quarter(up_part, devices, up_cut)
     late_rows = lax.optimization_barrier((late_rows, vector_sum, slab_three))[0]
@@ -1372,6 +1401,7 @@
         late_sum = sum_slabs(late_rows, 3)
     else:
         late_sum = Scatter(late_rows, range(3), dp_count).finish()
+    small_grad = lax.optimization_barrier((small_sums, late_sum))[0].reshape(small_master.shape)
     outer = place_on(("dp", dp_count // 4, 4))
     proj_grad = jnp.where(outer == 3, slab_three.astype(jnp.float32), late_sum).T
     down_grad = down_part.astype(jnp.float32)

time: 806 us -> 816 us (1.012)
  matrix products: 246 us -> 217 us
  waiting for transfers between devices: 14.9 us -> 38.6 us
  Pallas kernels: 407 us -> 421 us
    dot_general x9 -> x8, matrix products: 105 us -> 68.7 us  [times_transpose(): lax.dot_general(left_side, right_side, (((1,), (1,)), ((), ())), preferre...]
    ppermute x4, waiting for transfers between devices: 0.01 us -> 29.9 us  [swap_streams(): return lax.ppermute(rows, 'stream', [(0, 1), (1, 0)])]
    pallas_call x0 -> x1, Pallas kernels: none -> 15.8 us  [pre_and_sum(): pl.pallas_call(pre_kernel, grid=(width // FFN_TILE,), in_specs=[pl.BlockS...]
    unnamed x168 -> x162, local copies, waits for them, and re-layouts: 16.6 us -> 16.2 us
  transfers between devices with their start and end apart: 17 -> 17, of which waited for: 2 -> 4; matrix products, arithmetic and copies ran while one was open for 34% -> 30% of each run, Pallas kernels for 51% -> 37%
where the time goes in v4:
time: 816 us; the launch traced here: 807 us
  Pallas kernels  421 us (52%)
  matrix products  217 us (27%)
  starting transfers between devices  44.9 us (6%)
  other arithmetic  43.8 us (5%)
  waiting for transfers between devices  38.6 us (5%)
  local copies, waits for them, and re-layouts  27.2 us (3%)
  between operations  15.1 us (2%)
    pallas_call x4, Pallas kernels, attention_call(): pl.pallas_call(kernel, grid=(HEADS // 2,), in_specs=in_specs, out_specs=o...  177 us
    pallas_call x1, Pallas kernels, gather_shards(): pl.pallas_call(gather_kernel, out_shape=jax.ShapeDtypeStruct((4, 2, 2, 2,...  122 us
    pallas_call x1, Pallas kernels, sum_slabs(): pl.pallas_call(sum_kernel, out_shape=jax.ShapeDtypeStruct((block, width),...  106 us
    dot_general x11, matrix products, matmul(): return jnp.dot(left_side, right_side, preferred_element_type=jnp.float32)  77.1 us
    dot_general x12, matrix products, outer_sum(): lax.dot_general(left_side, right_side, (((0,), (0,)), ((), ())), preferre...  70.7 us
    dot_general x8, matrix products, times_transpose(): lax.dot_general(left_side, right_side, (((1,), (1,)), ((), ())), preferre...  68.7 us
    ppermute x4, waiting for transfers between devices, swap_streams(): return lax.ppermute(rows, 'stream', [(0, 1), (1, 0)])  29.9 us
    ppermute x5, starting transfers between devices, to_last_quarter(): blocks.append(lax.ppermute(share, ('dp', 'stream'), pairs))  19 us
  transfers between devices with their start and end apart: 17, of which 4 were waited for; matrix products, arithmetic and copies ran while one was open for 30% of the time, Pallas kernels for 37%

profile of v4, /device:TPU:11, one launch (start us, length us, event | category | flops | bytes accessed | tf_op | source)
XLA Modules:
  0.0 806.9 jit_solution(4024147262058084296)
XLA Ops:
  9.7 121.9 %gather_shards.1 = bf16[4,2,2,2,400,1024]{5,4,3,2,1,0:T(8,128)(2,1)} custom-call(bf16[400,1024]{1,0:T(8,128)(2,1)} %convert_bitcast_fusion.shard_ref), custom_call_target="tpu_custom_call" | custom-call | bytes 26214400 | tf_op jit(solution)/shard_map/gather_shards/pallas_call | solution.py:1147
  134.5 11.9 %all-to-all-start = ((bf16[32,2,168]{2,1,0:T(2,128)(2,1)}), bf16[32,2,168]{2,1,0:T(2,128)(2,1)S(1)}, u32[]{:S(2)}, u32[]{:S(2)}) async-start(bf16[32,2,168]{2,1,0:T(2,128)(2,1)} %reshape.225), calls=%async_computation | async-start | bytes 65536 | tf_op jit(solution)/shard_map/all_to_all | solution.py:699
  156.8 8.4 %collective-permute-done.1 = bf16[320,1024]{1,0:T(8,128)(2,1)} collective-permute-done((bf16[320,1024]{1,0:T(8,128)(2,1)S(1)}, bf16[320,1024]{1,0:T(8,128)(2,1)}, u32[]{:S(2)}, u32[]{:S(2)}) %collective-permute-start.1) | collective-permute-done | bytes 655392 | tf_op jit(solution)/shard_map/ppermute | solution.py:704
  165.2 21.5 %collective-permute-done = bf16[320,1024]{1,0:T(8,128)(2,1)} collective-permute-done((bf16[320,1024]{1,0:T(8,128)(2,1)}, bf16[320,1024]{1,0:T(8,128)(2,1)}, u32[]{:S(2)}, u32[]{:S(2)}) %collective-permute-start) | collective-permute-done | bytes 655392 | tf_op jit(solution)/shard_map/ppermute | solution.py:704
  191.8 5.1 add_convert_fusion.5.query_ref
  196.9 11.9 %add_convert_fusion.1.key_ref.value_ref.own_key_ref.own_value_ref = bf16[1280,2048]{1,0:T(8,128)(2,1)} fusion(f32[2048]{0:T(1024)S(1)} %concatenate.45, bf16[12800,1024]{1,0:T(8,128)(2,1)} %bitcast.62, bf16[640,1024]{1,0:T(8,128)(2,1)S(1)} %copy-done.28, bf16[320,1024]{1,0:T(8,128)(2,1)S(1)} %get-tuple-element.119, bf16[320,1024]{1,0:T(8,128)(2,1)S(1)} %get-tuple-element.120), kind=kOutput, calls=%fused_computation.5 | convolution fusion | flops 5381816320 | bytes 12066816 | tf_op jit(solution)/shard_map/dot_general | solution.py:62
  209.8 35.8 %self_forward.1 = (bf16[960,1024]{1,0:T(8,128)(2,1)}, f32[960,1024]{1,0:T(8,128)}) custom-call(bf16[960,1024]{1,0:T(8,128)(2,1)} %add_convert_fusion.5.query_ref, bf16[1280,2048]{1,0:T(8,128)(2,1)} %add_convert_fusion.1.key_ref.value_ref.own_key_ref.own_value_ref, bf16[1280,2048]{1,0:T(8,128)(2,1)} %add_convert_fusion.1.key_ref.value_ref.own_key_ref.own_value_ref, ...), custom_call_target="tpu_custom_call" | custom-call | flops 2516582400 | bytes 34242560 | tf_op jit(solution)/shard_map/self_forward/pallas_call | solution.py:438
  245.6 4.6 fusion.88
  250.8 7.6 add_convert_fusion.2.key_ref.value_ref
  258.4 5.2 add_convert_fusion.4.query_ref
  263.6 28.3 %cross_forward.1 = (bf16[960,1024]{1,0:T(8,128)(2,1)}, f32[960,1024]{1,0:T(8,128)}) custom-call(bf16[960,1024]{1,0:T(8,128)(2,1)} %add_convert_fusion.4.query_ref, bf16[640,2048]{1,0:T(8,128)(2,1)} %add_convert_fusion.2.key_ref.value_ref, bf16[640,2048]{1,0:T(8,128)(2,1)} %add_convert_fusion.2.key_ref.value_ref, f32[960,640]{1,0:T(8,128)} %get-tuple-element.106.mask_ref), custom_call_target="tpu_custom_call" | custom-call | flops 2516582400 | bytes 15564800 | tf_op jit(solution)/shard_map/cross_forward/pallas_call | solution.py:438
  291.9 4.9 fusion.89
  298.7 26.8 %add_convert_fusion = (bf16[960,4096]{1,0:T(8,128)(2,1)}, bf16[960,4096]{1,0:T(8,128)(2,1)}) fusion(f32[4096]{0:T(1024)S(1)} %slice.168, bf16[12800,1024]{1,0:T(8,128)(2,1)} %bitcast.67, f32[960,1024]{1,0:T(8,128)S(1)} %get-tuple-element.113, f32[1024]{0:T(1024)S(1)} %bitcast.101, f32[1024]{0:T(1024)S(1)} %bitcast.88, f32[960]{0:T(1024)S(1)} %add_rsqrt_fusion.1, ...), kind=kOutput, calls=%fused_computation.3 | convolution fusion | flops 8168079360 | bytes 28081664 | tf_op jit(solution)/shard_map/dot_general | solution.py:62
  325.5 14.3 %fusion.90 = (f32[960]{0:T(1024)S(1)}, f32[960,1024]{1,0:T(8,128)S(1)}) fusion(f32[1024]{0:T(1024)S(1)} %bitcast.108, bf16[960,4096]{1,0:T(8,128)(2,1)} %get-tuple-element.84, bf16[4096,1024]{1,0:T(8,128)(2,1)} %all-gather.2.cloned.1.call-done.weight_ref, f32[1024]{0:T(1024)S(1)} %bitcast.102, f32[1024]{0:T(1024)S(1)} %bitcast.89, ...), kind=kOutput, calls=%fused_computation.205 | convolution fusion | flops 8059943936 | bytes 24141056 | tf_op jit(solution)/shard_map/dot_general | solution.py:52
  342.7 3.1 fusion.14
  345.9 3.5 convert_reduce_fusion.2
  350.7 11.3 %convolution_convert_fusion.1 = bf16[4096,1024]{1,0:T(8,128)(2,1)} fusion(bf16[960,4096]{1,0:T(8,128)(2,1)S(1)} %bitcast.112, bf16[960,1024]{1,0:T(8,128)(2,1)S(1)} %get-tuple-element.80.grad_ref), kind=kOutput, calls=%fused_computation.7 | convolution fusion | flops 8057257984 | bytes 18219008 | tf_op jit(solution)/shard_map/dot_general | solution.py:56
  362.1 15.8 %pre_and_sum.1 = (bf16[960,4096]{1,0:T(8,128)(2,1)}, f32[1,4096]{1,0:T(1,128)}) custom-call(bf16[960,1024]{1,0:T(8,128)(2,1)} %copy-done.24, bf16[4096,1024]{1,0:T(8,128)(2,1)} %all-gather.2.cloned.1.call-done.weight_ref, bf16[960,4096]{1,0:T(8,128)(2,1)} %get-tuple-element.83.slope_ref), custom_call_target="tpu_custom_call" | custom-call | flops 8053063680 | bytes 26083328 | tf_op jit(solution)/shard_map/pre_and_sum/pallas_call | solution.py:1179
  377.9 15.7 %convolution_convert_fusion = bf16[4096,1024]{1,0:T(8,128)(2,1)} fusion(bf16[960,4096]{1,0:T(8,128)(2,1)} %get-tuple-element.37, f32[960,1024]{1,0:T(8,128)S(1)} %copy-done.5, f32[1024]{0:T(1024)S(1)} %bitcast.103, f32[1024]{0:T(1024)S(1)} %bitcast.90, f32[960]{0:T(1024)S(1)} %add_rsqrt_fusion.1, f32[960]{0:T(1024)S(1)} %broadcast_multiply_fusion.7), kind=kOutput, calls=%fused_computation.6 | convolution fusion | flops 8062173184 | bytes 20200960 | tf_op jit(solution)/shard_map/dot_general | solution.py:56
  393.6 19.5 %multiply_reduce_fusion = (f32[1024]{0:T(1024)S(1)}, f32[960]{0:T(1024)S(1)}, f32[960]{0:T(1024)S(1)}, f32[1024]{0:T(1024)S(1)}, f32[960,1024]{1,0:T(8,128)}) fusion(f32[960,1024]{1,0:T(8,128)} %copy-done.4, f32[960]{0:T(1024)S(1)} %add_rsqrt_fusion.1, f32[960]{0:T(1024)S(1)} %broadcast_multiply_fusion.7, f32[1024]{0:T(1024)S(1)} %bitcast.91, ...), kind=kOutput, calls=%fused_computation.28 | convolution fusion | flops 8073703424 | bytes 30062592 | tf_op jit(solution)/shard_map/dot_general | solution.py:52
  413.2 3.0 convert_reduce_fusion.3
  416.2 6.5 fusion.49.context_ref
  422.7 45.2 %cross_backward.1 = (bf16[960,1024]{1,0:T(8,128)(2,1)}, bf16[640,1024]{1,0:T(8,128)(2,1)}, bf16[640,1024]{1,0:T(8,128)(2,1)}) custom-call(bf16[960,1024]{1,0:T(8,128)(2,1)} %add_convert_fusion.4.query_ref, bf16[640,2048]{1,0:T(8,128)(2,1)} %add_convert_fusion.2.key_ref.value_ref, bf16[640,2048]{1,0:T(8,128)(2,1)} %add_convert_fusion.2.key_ref.value_ref, ...), custom_call_target="tpu_custom_call" | custom-call | flops 6291456000 | bytes 20152320 | tf_op jit(solution)/shard_map/cross_backward/pallas_call | solution.py:438
  467.9 3.6 fusion.28
  471.6 3.3 fusion.55
  476.4 5.1 multiply_reduce_fusion.1
  483.1 6.7 fusion.46.context_ref
  489.8 68.1 %self_backward.1 = (bf16[960,1024]{1,0:T(8,128)(2,1)}, bf16[1280,1024]{1,0:T(8,128)(2,1)}, bf16[1280,1024]{1,0:T(8,128)(2,1)}, f32[960,512]{1,0:T(8,128)}) custom-call(bf16[960,1024]{1,0:T(8,128)(2,1)} %add_convert_fusion.5.query_ref, bf16[1280,2048]{1,0:T(8,128)(2,1)} %add_convert_fusion.1.key_ref.value_ref.own_key_ref.own_value_ref, ...), custom_call_target="tpu_custom_call" | custom-call | flops 6291456000 | bytes 43909120 | tf_op jit(solution)/shard_map/self_backward/pallas_call | solution.py:438
  561.1 5.8 fusion.43
  566.9 3.7 convert_dynamic-update-slice_fusion.7
  570.7 4.6 fusion.33
  575.4 4.2 convert_dynamic-update-slice_fusion.6
  579.5 4.2 convert_dynamic-update-slice_fusion.5
  583.7 6.3 convolution_add_fusion
  592.7 6.6 convert_dynamic-update-slice_fusion.4
  600.4 4.2 reduce-scatter.7.cloned.1.call-done
  616.8 4.1 convert_dynamic-update-slice_fusion.3
  621.0 3.2 convert_dynamic-update-slice_fusion.2
  624.2 3.2 convert_dynamic-update-slice_fusion.1
  628.7 6.3 all-to-all-start.1
  635.0 6.6 convert_dynamic-update-slice_fusion
  641.7 5.0 convert_dynamic-update-slice_fusion.8
  648.1 6.8 collective-permute-start.5
  660.4 3.9 all-to-all-start.2
  664.9 4.4 all-to-all-done.2
  669.5 8.8 %collective-permute-start.8 = (bf16[128,1024]{1,0:T(8,128)(2,1)}, bf16[128,1024]{1,0:T(8,128)(2,1)S(1)}, u32[]{:S(2)}, u32[]{:S(2)}) collective-permute-start(bf16[128,1024]{1,0:T(8,128)(2,1)} %reduce-scatter.11.cloned.1.call-done), channel_id=1, source_target_pairs={{11,24},{14,25},{17,26},{20,27},{23,28},{26,29},{29,30}} | collective-permute-start | bytes 786440 | tf_op jit(solution)/shard_map/ppermute | solution.py:691
  684.8 105.7 %sum_slabs.1 = f32[400,1024]{1,0:T(8,128)} custom-call(bf16[3,2,2,2,400,1024]{5,4,3,2,1,0:T(8,128)(2,1)} %bitcast.20.grad_ref), custom_call_target="tpu_custom_call" | custom-call | flops 9830400 | bytes 39321600 | tf_op jit(solution)/shard_map/sum_slabs/pallas_call | solution.py:947
  791.2 6.4 multiply_subtract_fusion
  (277 shorter events, 69.2 us)
Async XLA Ops:
  7.2 318.3 %all-gather.2.cloned.1.call-start = ((), (), s32[]{:S(2)}) async-start(), calls=%async_computation.7 | async-start | bytes 8650752 | tf_op jit(solution)/shard_map/all_gather | solution.py:1237
  9.7 122.0 %copy-start.20 = (f32[128,1024]{1,0:T(8,128)S(1)}, f32[128,1024]{1,0:T(8,128)}, u32[]{:S(2)}) copy-start(f32[128,1024]{1,0:T(8,128)} %param.30) | copy-start | bytes 1572868
  9.7 122.8 %copy-start.57 = (f32[336]{0:T(512)S(1)}, f32[336]{0:T(512)}, u32[]{:S(2)}) copy-start(f32[336]{0:T(512)} %param.27) | copy-start | bytes 4036
  9.7 136.9 %copy-start.32 = (bf16[320,1024]{1,0:T(8,128)(2,1)S(1)}, bf16[320,1024]{1,0:T(8,128)(2,1)}, u32[]{:S(2)}) copy-start(bf16[320,1024]{1,0:T(8,128)(2,1)} %param.20) | copy-start | bytes 1966084
  9.7 138.4 %copy-start.64 = (s32[1,8]{1,0:T(1,128)S(1)}, s32[1,8]{1,0:T(1,128)}, u32[]{:S(2)}) copy-start(s32[1,8]{1,0:T(1,128)} %param.21) | copy-start | bytes 100
  131.7 21.8 %copy-start.44 = (f32[7,1024]{1,0:T(8,128)S(1)}, f32[7,1024]{1,0:T(8,128)}, u32[]{:S(2)}) copy-start(f32[7,1024]{1,0:T(8,128)} %param.33) | copy-start | bytes 86020
  134.5 21.5 %all-to-all-start = ((bf16[32,2,168]{2,1,0:T(2,128)(2,1)}), bf16[32,2,168]{2,1,0:T(2,128)(2,1)S(1)}, u32[]{:S(2)}, u32[]{:S(2)}) async-start(bf16[32,2,168]{2,1,0:T(2,128)(2,1)} %reshape.225), calls=%async_computation | async-start | bytes 65536 | tf_op jit(solution)/shard_map/all_to_all | solution.py:699
  146.4 443.7 %reduce-scatter.5.cloned.1.call-start = ((), (), s32[]{:S(2)}) async-start(), calls=%async_computation.8 | async-start | bytes 8912896 | tf_op jit(solution)/shard_map/reduce_scatter | solution.py:675
  146.6 18.6 %collective-permute-start.1 = (bf16[320,1024]{1,0:T(8,128)(2,1)S(1)}, bf16[320,1024]{1,0:T(8,128)(2,1)}, u32[]{:S(2)}, u32[]{:S(2)}) collective-permute-start(bf16[320,1024]{1,0:T(8,128)(2,1)S(1)} %copy-done.32), channel_id=1, source_target_pairs={{0,1},{1,0},{2,3},{3,2},{4,5},{5,4},{6,7},{7,6},{8,9},{9,8},{10,11... | collective-permute-start | bytes 1966088 | tf_op jit(solution)/shard_map/ppermute | solution.py:704
  146.9 39.7 %collective-permute-start = (bf16[320,1024]{1,0:T(8,128)(2,1)}, bf16[320,1024]{1,0:T(8,128)(2,1)}, u32[]{:S(2)}, u32[]{:S(2)}) collective-permute-start(bf16[320,1024]{1,0:T(8,128)(2,1)} %param.18), channel_id=1, source_target_pairs={{0,1},{1,0},{2,3},{3,2},{4,5},{5,4},{6,7},{7,6},{8,9},{9,8},{10,11... | collective-permute-start | bytes 1966088 | tf_op jit(solution)/shard_map/ppermute | solution.py:704
  154.0 137.8 %copy-start.51 = (f32[1,1024]{1,0:T(1,128)}, f32[1,1024]{1,0:T(1,128)S(1)}, u32[]{:S(2)}) copy-start(f32[1,1024]{1,0:T(1,128)S(1)} %get-tuple-element.104) | copy-start | bytes 12292
  154.0 137.8 %copy-start.59 = (f32[1,1024]{1,0:T(1,128)}, f32[1,1024]{1,0:T(1,128)S(1)}, u32[]{:S(2)}) copy-start(f32[1,1024]{1,0:T(1,128)S(1)} %get-tuple-element.103) | copy-start | bytes 12292
  155.3 33.7 %copy-start.28 = (bf16[640,1024]{1,0:T(8,128)(2,1)S(1)}, bf16[640,1024]{1,0:T(8,128)(2,1)}, u32[]{:S(2)}) copy-start(bf16[640,1024]{1,0:T(8,128)(2,1)} %param.19) | copy-start | bytes 3932164
  155.9 33.2 %copy-start.14 = (bf16[16,32,1024]{2,1,0:T(8,128)(2,1)}, bf16[16,32,1024]{2,1,0:T(8,128)(2,1)S(1)}, u32[]{:S(2)}) copy-start(bf16[16,32,1024]{2,1,0:T(8,128)(2,1)S(1)} %copy.46) | copy-start | bytes 3145732
  189.0 7.9 copy-start.37
  189.0 7.9 copy-start.39
  189.0 61.8 %copy-start.33 = (bf16[320,1024]{1,0:T(8,128)(2,1)}, bf16[320,1024]{1,0:T(8,128)(2,1)S(1)}, u32[]{:S(2)}) copy-start(bf16[320,1024]{1,0:T(8,128)(2,1)S(1)} %get-tuple-element.88) | copy-start | bytes 1966084
  189.0 61.8 %copy-start.35 = (bf16[320,1024]{1,0:T(8,128)(2,1)}, bf16[320,1024]{1,0:T(8,128)(2,1)S(1)}, u32[]{:S(2)}) copy-start(bf16[320,1024]{1,0:T(8,128)(2,1)S(1)} %get-tuple-element.89) | copy-start | bytes 1966084
  209.8 35.8 %copy-start.42 = (bf16[960,1024]{1,0:T(8,128)(2,1)S(1)}, bf16[960,1024]{1,0:T(8,128)(2,1)}, u32[]{:S(2)}) copy-start(bf16[960,1024]{1,0:T(8,128)(2,1)} %copy-done.41) | copy-start | bytes 5898244
  250.2 41.7 %copy-start.8 = (f32[960,1024]{1,0:T(8,128)}, f32[960,1024]{1,0:T(8,128)S(1)}, u32[]{:S(2)}) copy-start(f32[960,1024]{1,0:T(8,128)S(1)} %get-tuple-element.111) | copy-start | bytes 11796484
  250.2 41.7 %copy-start.46 = (f32[960]{0:T(1024)}, f32[960]{0:T(1024)S(1)}, u32[]{:S(2)}) copy-start(f32[960]{0:T(1024)S(1)} %broadcast_multiply_fusion.8) | copy-start | bytes 11524
  250.8 41.1 %copy-start.53 = (f32[960]{0:T(1024)}, f32[960]{0:T(1024)S(1)}, u32[]{:S(2)}) copy-start(f32[960]{0:T(1024)S(1)} %add_rsqrt_fusion.2) | copy-start | bytes 11524
  342.7 7.9 slice-start.2
  362.0 238.4 %reduce-scatter.9.cloned.1.call-start = ((), (), s32[]{:S(2)}) async-start(), calls=%async_computation.10 | async-start | bytes 8912896 | tf_op jit(solution)/shard_map/reduce_scatter | solution.py:675
  362.1 15.8 %copy-start.5 = (f32[960,1024]{1,0:T(8,128)S(1)}, f32[960,1024]{1,0:T(8,128)}, u32[]{:S(2)}) copy-start(f32[960,1024]{1,0:T(8,128)} %copy-done.4) | copy-start | bytes 11796484
  393.6 211.0 %reduce-scatter.7.cloned.1.call-start = ((), (), s32[]{:S(2)}) async-start(), calls=%async_computation.9 | async-start | bytes 786432 | tf_op jit(solution)/shard_map/reduce_scatter | solution.py:676
  393.6 19.5 %copy-start.6 = (f32[960,1024]{1,0:T(8,128)S(1)}, f32[960,1024]{1,0:T(8,128)}, u32[]{:S(2)}) copy-start(f32[960,1024]{1,0:T(8,128)} %copy-done.4) | copy-start | bytes 11796484
  416.2 60.1 %copy-start.17 = (f32[960,1024]{1,0:T(8,128)}, f32[960,1024]{1,0:T(8,128)S(1)}, u32[]{:S(2)}) copy-start(f32[960,1024]{1,0:T(8,128)S(1)} %get-tuple-element.76) | copy-start | bytes 11796484
  475.0 124.3 %collective-permute-start.3 = (bf16[320,1024]{1,0:T(8,128)(2,1)S(1)}, bf16[320,1024]{1,0:T(8,128)(2,1)S(1)}, u32[]{:S(2)}, u32[]{:S(2)}) collective-permute-start(bf16[320,1024]{1,0:T(8,128)(2,1)S(1)} %dynamic-slice_convert_fusion), channel_id=1, source_target_pairs={{0,1},{1,0},{2,3},{3,2},{4,5},{5,4},{6,7},{7,6},{8,9},{9,8},{10,11... | collective-permute-start | bytes 1966088 | tf_op jit(solution)/shard_map/ppermute | solution.py:704
  489.8 70.3 %copy-start.30 = (bf16[640,1024]{1,0:T(8,128)(2,1)S(1)}, bf16[640,1024]{1,0:T(8,128)(2,1)}, u32[]{:S(2)}) copy-start(bf16[640,1024]{1,0:T(8,128)(2,1)} %get-tuple-element.47) | copy-start | bytes 3932164
  583.7 6.8 copy-start.12
  590.1 56.6 %reduce-scatter.11.cloned.1.call-start = ((), (), s32[]{:S(2)}) async-start(), calls=%async_computation.11 | async-start | bytes 786432 | tf_op jit(solution)/shard_map/reduce_scatter | solution.py:676
  592.7 11.9 %copy-start.11 = (f32[960,512]{1,0:T(8,128)S(1)}, f32[960,512]{1,0:T(8,128)}, u32[]{:S(2)}) copy-start(f32[960,512]{1,0:T(8,128)} %get-tuple-element.43) | copy-start | bytes 5898244
  613.8 183.8 %collective-permute-start.2 = (bf16[320,1024]{1,0:T(8,128)(2,1)}, bf16[320,1024]{1,0:T(8,128)(2,1)}, u32[]{:S(2)}, u32[]{:S(2)}) collective-permute-start(bf16[320,1024]{1,0:T(8,128)(2,1)} %dynamic-slice_convert_fusion.1), channel_id=1, source_target_pairs={{0,1},{1,0},{2,3},{3,2},{4,5},{5,4},{6,7},{7,6},{8,9},{9,8},{10,11... | collective-permute-start | bytes 1966088 | tf_op jit(solution)/shard_map/ppermute | solution.py:704
  628.7 30.9 %all-to-all-start.1 = ((f32[32,1,560]{2,1,0:T(1,128)}), f32[32,1,560]{2,1,0:T(1,128)S(1)}, u32[]{:S(2)}, u32[]{:S(2)}) async-start(f32[32,1,560]{2,1,0:T(1,128)} %all_to_all.15), calls=%async_computation.5 | async-start | bytes 163840 | tf_op jit(solution)/shard_map/all_to_all | solution.py:1392
  641.6 15.2 %copy-start.21 = (f32[128,1024]{1,0:T(8,128)S(1)}, f32[128,1024]{1,0:T(8,128)}, u32[]{:S(2)}) copy-start(f32[128,1024]{1,0:T(8,128)} %param.30) | copy-start | bytes 1572868
  641.6 22.7 %copy-start.58 = (f32[336]{0:T(512)S(1)}, f32[336]{0:T(512)}, u32[]{:S(2)}) copy-start(f32[336]{0:T(512)} %param.27) | copy-start | bytes 4036
  641.6 22.7 %copy-start.61 = (f32[336]{0:T(512)S(1)}, f32[336]{0:T(512)}, u32[]{:S(2)}) copy-start(f32[336]{0:T(512)} %param.28) | copy-start | bytes 4036
  641.6 22.7 %copy-start.62 = (f32[336]{0:T(512)S(1)}, f32[336]{0:T(512)}, u32[]{:S(2)}) copy-start(f32[336]{0:T(512)} %param.29) | copy-start | bytes 4036
  646.7 22.8 %collective-permute-start.4 = (bf16[128,1024]{1,0:T(8,128)(2,1)}, bf16[128,1024]{1,0:T(8,128)(2,1)}, u32[]{:S(2)}, u32[]{:S(2)}) collective-permute-start(bf16[128,1024]{1,0:T(8,128)(2,1)} %reduce-scatter.11.cloned.1.call-done), channel_id=1, source_target_pairs={{7,24},{10,25},{13,26},{16,27},{19,28},{22,29},{25,30},{28,31}} | collective-permute-start | bytes 786440 | tf_op jit(solution)/shard_map/ppermute | solution.py:691
  648.1 31.9 %collective-permute-start.5 = (bf16[128,1024]{1,0:T(8,128)(2,1)}, bf16[128,1024]{1,0:T(8,128)(2,1)}, u32[]{:S(2)}, u32[]{:S(2)}) collective-permute-start(bf16[128,1024]{1,0:T(8,128)(2,1)} %reduce-scatter.11.cloned.1.call-done), channel_id=1, source_target_pairs={{8,24},{11,25},{14,26},{17,27},{20,28},{23,29},{26,30},{29,31}} | collective-permute-start | bytes 786440 | tf_op jit(solution)/shard_map/ppermute | solution.py:691
  654.8 26.8 %collective-permute-start.6 = (bf16[128,1024]{1,0:T(8,128)(2,1)}, bf16[128,1024]{1,0:T(8,128)(2,1)}, u32[]{:S(2)}, u32[]{:S(2)}) collective-permute-start(bf16[128,1024]{1,0:T(8,128)(2,1)} %reduce-scatter.11.cloned.1.call-done), channel_id=1, source_target_pairs={{9,24},{12,25},{15,26},{18,27},{21,28},{24,29},{27,30},{30,31}} | collective-permute-start | bytes 786440 | tf_op jit(solution)/shard_map/ppermute | solution.py:691
  656.2 27.2 %collective-permute-start.7 = (bf16[128,1024]{1,0:T(8,128)(2,1)}, bf16[128,1024]{1,0:T(8,128)(2,1)S(1)}, u32[]{:S(2)}, u32[]{:S(2)}) collective-permute-start(bf16[128,1024]{1,0:T(8,128)(2,1)} %reduce-scatter.11.cloned.1.call-done), channel_id=1, source_target_pairs={{10,24},{13,25},{16,26},{19,27},{22,28},{25,29},{28,30},{31,31}} | collective-permute-start | bytes 786440 | tf_op jit(solution)/shard_map/ppermute | solution.py:691
  660.4 9.0 %all-to-all-start.2 = ((f32[32,1,224]{2,1,0:T(1,128)}), f32[32,1,224]{2,1,0:T(1,128)S(1)}, u32[]{:S(2)}, u32[]{:S(2)}) async-start(f32[32,1,224]{2,1,0:T(1,128)} %broadcast_in_dim.20), calls=%async_computation.6 | async-start | bytes 65536 | tf_op jit(solution)/shard_map/all_to_all | solution.py:699
  669.5 14.6 %collective-permute-start.8 = (bf16[128,1024]{1,0:T(8,128)(2,1)}, bf16[128,1024]{1,0:T(8,128)(2,1)S(1)}, u32[]{:S(2)}, u32[]{:S(2)}) collective-permute-start(bf16[128,1024]{1,0:T(8,128)(2,1)} %reduce-scatter.11.cloned.1.call-done), channel_id=1, source_target_pairs={{11,24},{14,25},{17,26},{20,27},{23,28},{26,29},{29,30}} | collective-permute-start | bytes 786440 | tf_op jit(solution)/shard_map/ppermute | solution.py:691
  684.8 105.7 %copy-start.45 = (f32[7,1024]{1,0:T(8,128)S(1)}, f32[7,1024]{1,0:T(8,128)}, u32[]{:S(2)}) copy-start(f32[7,1024]{1,0:T(8,128)} %param.33) | copy-start | bytes 86020
  684.8 105.7 %copy-start.49 = (f32[7,1024]{1,0:T(8,128)S(1)}, f32[7,1024]{1,0:T(8,128)}, u32[]{:S(2)}) copy-start(f32[7,1024]{1,0:T(8,128)} %param.34) | copy-start | bytes 86020
  684.8 105.7 %copy-start.50 = (f32[7,1024]{1,0:T(8,128)S(1)}, f32[7,1024]{1,0:T(8,128)}, u32[]{:S(2)}) copy-start(f32[7,1024]{1,0:T(8,128)} %param.35) | copy-start | bytes 86020
  (40 other events, 159.5 us)
Sparse Core Ops, SparseCore 0:
  132.6 93.5 all-gather.1
  362.1 105.3 reduce-scatter.4
  471.6 104.3 reduce-scatter.8
  590.2 14.3 reduce-scatter.6
  606.8 18.0 reduce-scatter.10

commit v5 on v4

--- a/solution.py
+++ b/solution.py
@@ -26,6 +26,8 @@
 RATE_SMALL = 0.5
 WEIGHT_DECAY = 0.01
 MASKED = -1e30
+SUM_WAVES = 4
+SUM_CHUNKS = 2 * SUM_WAVES
 FFN_TILE = 1024
 FFN_PART = 256
 MESH = pl.DeviceIdType.MESH
@@ -704,8 +706,7 @@
     return lax.ppermute(rows, "stream", [(0, 1), (1, 0)])
 
 
-def both_parts(rows):
-    other = swap_streams(rows)
+def both_parts(rows, other):
     leading = lax.axis_index("stream") == 0
     return jnp.concatenate(
         [jnp.where(leading, rows, other), jnp.where(leading, other, rows)], axis=0
@@ -734,8 +735,8 @@
 
 def chunk_rows(block):
     tiles = block // 16
-    counts = [(tiles + 3 - part) // 4 * 16 for part in range(4)]
-    return [(sum(counts[:part]), counts[part]) for part in range(4)]
+    counts = [(tiles + SUM_CHUNKS - 1 - part) // SUM_CHUNKS * 16 for part in range(SUM_CHUNKS)]
+    return [(sum(counts[:part]), counts[part]) for part in range(SUM_CHUNKS)]
 
 
 def add_rows(target_ref, source_ref, start, count):
@@ -813,25 +814,25 @@
 
     def first_copy(s, chunk, other):
         rows = pl.ds(*chunks[chunk])
-        at = (s * 4 + chunk) * 2 + other
-        source = held.at[s, other, 1 - x, rows] if chunk < 2 else held.at[s, 1 - y, other, rows]
+        at = (s * SUM_CHUNKS + chunk) * 2 + other
+        source = held.at[s, other, 1 - x, rows] if chunk < SUM_WAVES else held.at[s, 1 - y, other, rows]
         return remote(
             source,
             first_in.at[s, other, rows],
             first_send.at[at],
             first_recv.at[at],
-            across if chunk < 2 else beside,
+            across if chunk < SUM_WAVES else beside,
         )
 
     def second_copy(s, chunk):
         rows = pl.ds(*chunks[chunk])
-        source = held.at[s, 1 - y, x, rows] if chunk < 2 else held.at[s, y, 1 - x, rows]
+        source = held.at[s, 1 - y, x, rows] if chunk < SUM_WAVES else held.at[s, y, 1 - x, rows]
         return remote(
             source,
             second_in.at[s, rows],
-            second_send.at[s * 4 + chunk],
-            second_recv.at[s * 4 + chunk],
-            beside if chunk < 2 else across,
+            second_send.at[s * SUM_CHUNKS + chunk],
+            second_recv.at[s * SUM_CHUNKS + chunk],
+            beside if chunk < SUM_WAVES else across,
         )
 
     def along_copy(s, chunk, down):
@@ -840,8 +841,8 @@
         return remote(
             held.at[s, y, x, rows],
             along_in.at[way, s, rows],
-            along_send.at[s * 4 + chunk],
-            along_recv.at[way * slabs * 4 + s * 4 + chunk],
+            along_send.at[s * SUM_CHUNKS + chunk],
+            along_recv.at[way * slabs * SUM_CHUNKS + s * SUM_CHUNKS + chunk],
             below if down else above,
         )
 
@@ -851,7 +852,7 @@
                 for xx in range(2):
                     load(s, yy, xx).wait()
                     core_copy(s, yy, xx).wait_recv()
-        for chunk in (half, half + 2):
+        for chunk in (half, half + SUM_WAVES):
             for yy in range(2):
                 for xx in range(2):
                     add_rows(held.at[s, yy, xx], core_in.at[s, yy, xx], *chunks[chunk])
@@ -859,15 +860,15 @@
                 first_copy(s, chunk, other).start()
 
     def first_stage(s, half):
-        for chunk in (half, half + 2):
+        for chunk in (half, half + SUM_WAVES):
             for other in range(2):
                 first_copy(s, chunk, other).wait_recv()
-                kept = held.at[s, other, x] if chunk < 2 else held.at[s, y, other]
+                kept = held.at[s, other, x] if chunk < SUM_WAVES else held.at[s, y, other]
                 add_rows(kept, first_in.at[s, other], *chunks[chunk])
             second_copy(s, chunk).start()
 
     def second_stage(s, half):
-        for chunk in (half, half + 2):
+        for chunk in (half, half + SUM_WAVES):
             second_copy(s, chunk).wait_recv()
             add_rows(held.at[s, y, x], second_in.at[s], *chunks[chunk])
         along_stage(s, half, 0)
@@ -879,7 +880,7 @@
 
                 @pl.when(z == source)
                 def pass_on():
-                    for chunk in (half, half + 2):
+                    for chunk in (half, half + SUM_WAVES):
                         if hop > 0:
                             along_copy(s, chunk, down).wait_recv()
                             add_rows(
@@ -890,7 +891,7 @@
     def last_stage(s, half):
         @pl.when(z == s)
         def finish():
-            for chunk in (half, half + 2):
+            for chunk in (half, half + SUM_WAVES):
                 start, count = chunks[chunk]
                 if s < 3:
                     along_copy(s, chunk, True).wait_recv()
@@ -913,7 +914,7 @@
                 core_copy(s, yy, xx).start()
                 load(s, yy, xx).start()
     out_ref[...] = jnp.zeros_like(out_ref)
-    waves = [(s, half) for s in range(slabs) for half in range(2)]
+    waves = [(s, half) for s in range(slabs) for half in range(SUM_WAVES)]
     stages = [
         core_stage,
         first_stage,
@@ -930,7 +931,7 @@
         for yy in range(2):
             for xx in range(2):
                 core_copy(s, yy, xx).wait_send()
-        for chunk in range(4):
+        for chunk in range(SUM_CHUNKS):
             for other in range(2):
                 first_copy(s, chunk, other).wait_send()
             second_copy(s, chunk).wait_send()
@@ -958,12 +959,12 @@
             dma((slabs * 4,)),
             dma((slabs * 4,)),
             dma((slabs * 4,)),
-            dma((slabs * 8,)),
-            dma((slabs * 8,)),
-            dma((slabs * 4,)),
-            dma((slabs * 4,)),
-            dma((slabs * 4,)),
-            dma((slabs * 8,)),
+            dma((slabs * SUM_CHUNKS * 2,)),
+            dma((slabs * SUM_CHUNKS * 2,)),
+            dma((slabs * SUM_CHUNKS,)),
+            dma((slabs * SUM_CHUNKS,)),
+            dma((slabs * SUM_CHUNKS,)),
+            dma((slabs * SUM_CHUNKS * 2,)),
         ],
         compiler_params=pltpu.CompilerParams(
             collective_id=0, has_side_effects=True, vmem_limit_bytes=56 * 2**20
@@ -977,8 +978,7 @@
 
 def part_rows(block):
     tiles = block // 16
-    one = (tiles * 2 + 4) // 5
-    two = (tiles - one) * 3 // 5
+    one, two = tiles // 4, tiles // 2
     return [(0, one * 16), (one * 16, two * 16), ((one + two) * 16, (tiles - one - two) * 16)]
 
 
@@ -988,7 +988,20 @@
     return code // power % 10
 
 
-def gather_kernel(shard_ref, out_ref, own_sem, send_sem, link_recv, core_recv):
+def gather_kernel(
+    shard_ref,
+    bias_ref,
+    main_ref,
+    out_ref,
+    bias_out_ref,
+    main_out_ref,
+    own_sem,
+    send_sem,
+    link_recv,
+    core_recv,
+    swap_send,
+    swap_recv,
+):
     block = shard_ref.shape[0]
     place, x = lax.axis_index("dp"), lax.axis_index("stream")
     c, y, z = place % 2, (place // 2) % 2, place // 4
@@ -1010,18 +1023,25 @@
     def greet_below():
         pl.semaphore_signal(barrier, inc=1, device_id=devices[down], device_id_type=MESH)
 
-    own = pltpu.make_async_copy(shard_ref, out_ref.at[z, y, c, x], own_sem)
+    own = pltpu.make_async_copy(shard_ref, out_ref.at[z, y, c, x], own_sem.at[0])
     own.start()
+    own_bias = pltpu.make_async_copy(bias_ref, bias_out_ref.at[z, y, c, x], own_sem.at[1])
+    own_bias.start()
     pl.semaphore_wait(barrier, 4 + z * (3 - z) // 2)
     own.wait()
+    own_bias.wait()
 
     def copy(way, zz, yy, xx, part, core=None):
-        region = out_ref.at[zz, yy, c if core is None else core, xx, pl.ds(*parts[part])]
-        at = ((zz * 2 + yy) * 2 + xx) * 3 + part
+        cc = c if core is None else core
+        if part == 3:
+            region = bias_out_ref.at[zz, yy, cc, xx]
+        else:
+            region = out_ref.at[zz, yy, cc, xx, pl.ds(*parts[part])]
+        at = ((zz * 2 + yy) * 2 + xx) * 4 + part
         return pltpu.make_async_remote_copy(
             src_ref=region,
             dst_ref=region,
-            send_sem=send_sem.at[way * 48 + at],
+            send_sem=send_sem.at[way * 64 + at],
             recv_sem=core_recv.at[at] if way == sibling else link_recv.at[at],
             device_id=devices[way],
             device_id_type=MESH,
@@ -1065,33 +1085,48 @@
             copy(sibling, zz, yy, xx, part).start()
 
     def last_own(k):
-        if k == 0:
-            copy(across, z, y, x, 2).start()
-            copy(beside, z, y, x, 2).start()
-            regions = [(y, x)]
-        elif k == 1:
-            came(z, y, 1 - x, 2)
-            copy(beside, z, y, 1 - x, 2).start()
-            regions = [(y, 1 - x)]
-        else:
-            regions = [(1 - y, x), (1 - y, 1 - x)]
-        for yy, xx in regions:
-            if k == 2:
-                came(z, yy, xx, 2)
-            along(z, yy, xx, 2)
-            copy(sibling, z, yy, xx, 2).start()
+        for part in (2, 3):
+            if k == 0:
+                copy(across, z, y, x, part).start()
+                copy(beside, z, y, x, part).start()
+                regions = [(y, x)]
+            elif k == 1:
+                came(z, y, 1 - x, part)
+                copy(beside, z, y, 1 - x, part).start()
+                regions = [(y, 1 - x)]
+            else:
+                regions = [(1 - y, x), (1 - y, 1 - x)]
+            for yy, xx in regions:
+                if k == 2:
+                    came(z, yy, xx, part)
+                along(z, yy, xx, part)
+                copy(sibling, z, yy, xx, part).start()
 
     def last(k):
         zz = order[k]
         for yy, xx in ((y, x), (y, 1 - x), (1 - y, x), (1 - y, 1 - x)):
-            came(zz, yy, xx, 2)
-            along(zz, yy, xx, 2)
-            copy(sibling, zz, yy, xx, 2).start()
+            for part in (2, 3):
+                came(zz, yy, xx, part)
+                along(zz, yy, xx, part)
+                copy(sibling, zz, yy, xx, part).start()
+
+    swap = pltpu.make_async_remote_copy(
+        src_ref=main_ref,
+        dst_ref=main_out_ref,
+        send_sem=swap_send,
+        recv_sem=swap_recv,
+        device_id=devices[across],
+        device_id_type=MESH,
+    )
+
+    def swap_main(k):
+        swap.start()
 
     for stage, k in (
         (early, 0),
         (last_own, 0),
         (last_own, 1),
+        (swap_main, 0),
         (early, 1),
         (middle, 0),
         (last_own, 2),
@@ -1110,10 +1145,11 @@
     ):
         stage(k)
 
+    swap.wait()
     for zz in range(4):
         for yy in range(2):
             for xx in range(2):
-                for part in range(3):
+                for part in range(4):
                     copy(sibling, zz, yy, xx, part, 1 - c).wait_recv()
                     copy(sibling, zz, yy, xx, part).wait_send()
 
@@ -1136,20 +1172,29 @@
         for yy in range(2):
             for xx in range(2):
                 sent_along(zz, yy, xx, 2)
-    copy(across, z, y, x, 2).wait_send()
-    copy(beside, z, y, x, 2).wait_send()
-    copy(beside, z, y, 1 - x, 2).wait_send()
-
-
-def gather_shards(shard):
+                sent_along(zz, yy, xx, 3)
+    for part in (2, 3):
+        copy(across, z, y, x, part).wait_send()
+        copy(beside, z, y, x, part).wait_send()
+        copy(beside, z, y, 1 - x, part).wait_send()
+
+
+def gather_shards(shard, bias, main_rows):
     block, width = shard.shape
+    tile = (16, LANES)
+    bias_tile = jnp.pad(bias, (0, tile[0] * tile[1] - bias.shape[0])).reshape(tile)
     dma = pltpu.SemaphoreType.DMA
-    gathered = pl.pallas_call(
+    place = pl.BlockSpec(memory_space=pl.ANY)
+    gathered, biases, main_other = pl.pallas_call(
         gather_kernel,
-        out_shape=jax.ShapeDtypeStruct((4, 2, 2, 2, block, width), shard.dtype),
-        in_specs=[pl.BlockSpec(memory_space=pl.ANY)],
-        out_specs=pl.BlockSpec(memory_space=pl.ANY),
-        scratch_shapes=[dma, dma((240,)), dma((48,)), dma((48,))],
+        out_shape=[
+            jax.ShapeDtypeStruct((4, 2, 2, 2, block, width), shard.dtype),
+            jax.ShapeDtypeStruct((4, 2, 2, 2, *tile), bias.dtype),
+            jax.ShapeDtypeStruct(main_rows.shape, main_rows.dtype),
+        ],
+        in_specs=[place] * 3,
+        out_specs=[place] * 3,
+        scratch_shapes=[dma((2,)), dma((320,)), dma((64,)), dma((64,)), dma, dma],
         compiler_params=pltpu.CompilerParams(
             collective_id=1, has_side_effects=True, vmem_limit_bytes=56 * 2**20
         ),
@@ -1157,8 +1202,9 @@
             flops=0, bytes_accessed=64 * shard.size, transcendentals=0
         ),
         name="gather_shards",
-    )(shard)
-    return gathered.reshape(32 * block, width)
+    )(shard, bias_tile, main_rows)
+    biases = biases.reshape(32, tile[0] * tile[1])[:, : bias.shape[0]].reshape(-1)
+    return gathered.reshape(32 * block, width), biases, main_other
 
 
 def pre_kernel(grad_ref, weight_ref, slope_ref, pre_ref, sum_ref):
@@ -1227,14 +1273,17 @@
     half_rows = main_rows.shape[0]
     group_rows = pred_rows.shape[0]
 
-    bias_wide = to_all(bias_master.astype(jnp.bfloat16), devices).astype(jnp.float32)
+    bias_low = bias_master.astype(jnp.bfloat16)
     proj_low = proj_master.astype(jnp.bfloat16).T
     if dp_count == 16:
-        proj_rows = gather_shards(proj_low)
+        proj_rows, bias_low, main_other = gather_shards(proj_low, bias_low, main_rows)
     else:
         proj_rows = lax.all_gather(proj_low, ("dp", "stream"), axis=0, tiled=True)
+        bias_low = to_all(bias_low, devices)
+        main_other = swap_streams(main_rows)
     down_low = lax.optimization_barrier((down_master.astype(jnp.bfloat16), proj_rows))[0]
     down_weight = lax.all_gather(down_low, ("dp", "stream"), axis=0, tiled=True)
+    bias_wide = bias_low.astype(jnp.float32)
     query_weight = proj_rows[0:D]
     keys_weight = proj_rows[D : 3 * D]
     out_weight = proj_rows[3 * D : 4 * D]
@@ -1276,8 +1325,7 @@
     spread = bucket_of(turn)
     edge = jnp.broadcast_to(query_places[:, None] - LANES, turn.shape)
 
-    main_all = both_parts(main_rows)
-    enc_all = both_parts(enc_rows)
+    main_all = both_parts(main_rows, main_other)
     inputs = jnp.concatenate([main_rows, pred_rows], axis=0)
     key_inputs = jnp.concatenate([main_all, pred_rows], axis=0)
     input_values = inputs.astype(jnp.float32)
@@ -1286,10 +1334,12 @@
         times_transpose(key_inputs, keys_weight) + jnp.concatenate([zero_bias, value_bias])
     ).astype(jnp.bfloat16)
     table = times_transpose(inputs, table_weight) + table_bias
+    context_low, self_log = self_forward(query_low, self_pairs, table, spread, edge, self_mask)
+    enc_other = swap_streams(enc_rows) + jnp.bfloat16(0.0) * context_low[0:1, 0:1]
+    enc_all = both_parts(enc_rows, enc_other)
     cross_pairs = (
         times_transpose(enc_all, pair_weight) + jnp.concatenate([zero_bias, pair_bias])
     ).astype(jnp.bfloat16)
-    context_low, self_log = self_forward(query_low, self_pairs, table, spread, edge, self_mask)
     norm_one_in = input_values + times_transpose(context_low, out_weight) + out_bias
     stats_one = norm_stats(norm_one_in)
     hidden_one = (norm_one_in - stats_one[0]) * stats_one[1] * small_master[1] + small_master[4]
@@ -1385,23 +1435,18 @@
     small_parts = jnp.concatenate(
         [row_sum(ffn_grad), gain_one, gain_two, gain_three, shift_one, shift_two, shift_three]
     )
-    vector_parts = jnp.concatenate(
-        [bias_parts.reshape(devices, -1), small_parts.reshape(devices, -1)], axis=1
-    )
-    vector_sum = jnp.sum(
-        lax.all_to_all(vector_parts, ("dp", "stream"), 0, 0, tiled=True), axis=0
-    )
-    bias_len = bias_master.shape[0]
-    bias_grad = vector_sum[:bias_len]
-    small_sums = to_all(vector_sum[bias_len:], devices)
-
+    vector_sum = lax.psum(jnp.concatenate([bias_parts, small_parts]), ("dp", "stream"))
     slab_three = to_last_quarter(up_part, devices, up_cut)
-    late_rows = lax.optimization_barrier((late_rows, vector_sum, slab_three))[0]
+    late_rows = lax.optimization_barrier((late_rows, slab_three))[0]
     if dp_count == 16:
         late_sum = sum_slabs(late_rows, 3)
     else:
         late_sum = Scatter(late_rows, range(3), dp_count).finish()
-    small_grad = lax.optimization_barrier((small_sums, late_sum))[0].reshape(small_master.shape)
+    vector_sum = vector_sum + 0.0 * late_sum[0, 0]
+    device = lax.axis_index("dp") * 2 + lax.axis_index("stream")
+    bias_len = bias_master.shape[0]
+    bias_grad = lax.dynamic_slice_in_dim(vector_sum, device * bias_len, bias_len)
+    small_grad = vector_sum[devices * bias_len :].reshape(small_master.shape)
     outer = place_on(("dp", dp_count // 4, 4))
     proj_grad = jnp.where(outer == 3, slab_three.astype(jnp.float32), late_sum).T
     down_grad = down_part.astype(jnp.float32)

time: 816 us -> 778 us (0.953)
  starting transfers between devices: 44.9 us -> 19.6 us
  waiting for transfers between devices: 38.6 us -> 14 us
    ppermute x4 -> x3, waiting for transfers between devices: 29.9 us -> 0.01 us  [swap_streams(): return lax.ppermute(rows, 'stream', [(0, 1), (1, 0)])]
    all_to_all x3 -> x0, starting transfers between devices: 22.1 us -> none  [the longest x2 15.8 us: to_all(): gathered = lax.all_to_all(shared, ('dp', 'stream'), 0, 0, tiled=True)]
    pallas_call x1, Pallas kernels: 122 us -> 131 us  [gather_shards(): pl.pallas_call(gather_kernel, out_shape=[jax.ShapeDtypeStruct((4, 2, 2, 2...]
    reduce_scatter x2, waiting for transfers between devices: 4.2 us -> 13.1 us  [sum_shares(): return lax.psum_scatter(part, 'stream', scatter_dimension=0, tiled=True)]
  transfers between devices with their start and end apart: 17 -> 14, of which waited for: 4 -> 2; matrix products, arithmetic and copies ran while one was open for 30% -> 31% of each run, Pallas kernels for 37% -> 39%
where the time goes in v5:
time: 778 us; the launch traced here: 769 us
  Pallas kernels  429 us (55%)
  matrix products  215 us (28%)
  other arithmetic  47.4 us (6%)
  local copies, waits for them, and re-layouts  26.4 us (3%)
  starting transfers between devices  19.6 us (3%)
  between operations  17 us (2%)
  waiting for transfers between devices  14 us (2%)
    pallas_call x4, Pallas kernels, attention_call(): pl.pallas_call(kernel, grid=(HEADS // 2,), in_specs=in_specs, out_specs=o...  177 us
    pallas_call x1, Pallas kernels, gather_shards(): pl.pallas_call(gather_kernel, out_shape=[jax.ShapeDtypeStruct((4, 2, 2, 2...  131 us
    pallas_call x1, Pallas kernels, sum_slabs(): pl.pallas_call(sum_kernel, out_shape=jax.ShapeDtypeStruct((block, width),...  106 us
    dot_general x11, matrix products, matmul(): return jnp.dot(left_side, right_side, preferred_element_type=jnp.float32)  75.9 us
    dot_general x12, matrix products, outer_sum(): lax.dot_general(left_side, right_side, (((0,), (0,)), ((), ())), preferre...  70.4 us
    dot_general x8, matrix products, times_transpose(): lax.dot_general(left_side, right_side, (((1,), (1,)), ((), ())), preferre...  68.9 us
    ppermute x5, starting transfers between devices, to_last_quarter(): blocks.append(lax.ppermute(share, ('dp', 'stream'), pairs))  16.5 us
  transfers between devices with their start and end apart: 14, of which 2 were waited for; matrix products, arithmetic and copies ran while one was open for 31% of the time, Pallas kernels for 39%

profile of v5, /device:TPU:11, one launch (start us, length us, event | category | flops | bytes accessed | tf_op | source)
XLA Modules:
  0.0 768.6 jit_solution(4725431983297358352)
XLA Ops:
  7.2 2.5 convert_bitcast_fusion.shard_ref
  12.9 131.3 %gather_shards.1 = (bf16[4,2,2,2,400,1024]{5,4,3,2,1,0:T(8,128)(2,1)}, bf16[4,2,2,2,16,128]{5,4,3,2,1,0:T(8,128)(2,1)}, bf16[320,1024]{1,0:T(8,128)(2,1)}) custom-call(bf16[400,1024]{1,0:T(8,128)(2,1)} %convert_bitcast_fusion.shard_ref, bf16[16,128]{1,0:T(8,128)(2,1)} %pad_bitcast_fusion.bias_ref, bf16[320,1024]{1,0:T(8,128)(2,1)} %main_ref.1), custom_call_target="tpu_custom_call" | custom-call | bytes 26214400 | tf_op jit(solution)/shard_map/gather_shards/pallas_call | solution.py:1188
  153.7 3.4 compare_select_fusion
  157.1 2.6 convolution_add_fusion.2.table_ref
  159.6 5.3 add_convert_fusion.5.query_ref
  165.0 11.4 %add_convert_fusion.1.key_ref.value_ref.own_key_ref.own_value_ref = bf16[1280,2048]{1,0:T(8,128)(2,1)} fusion(f32[2048]{0:T(1024)S(1)} %concatenate.39, bf16[12800,1024]{1,0:T(8,128)(2,1)} %bitcast.80, bf16[640,1024]{1,0:T(8,128)(2,1)S(1)} %copy-done.29, bf16[320,1024]{1,0:T(8,128)(2,1)S(1)} %get-tuple-element.95, bf16[320,1024]{1,0:T(8,128)(2,1)S(1)} %get-tuple-element.94), kind=kOutput, calls=%fused_computation.5 | convolution fusion | flops 5381816320 | bytes 12066816 | tf_op jit(solution)/shard_map/dot_general | solution.py:64
  177.3 35.6 %self_forward.1 = (bf16[960,1024]{1,0:T(8,128)(2,1)}, f32[960,1024]{1,0:T(8,128)}) custom-call(bf16[960,1024]{1,0:T(8,128)(2,1)} %add_convert_fusion.5.query_ref, bf16[1280,2048]{1,0:T(8,128)(2,1)} %add_convert_fusion.1.key_ref.value_ref.own_key_ref.own_value_ref, bf16[1280,2048]{1,0:T(8,128)(2,1)} %add_convert_fusion.1.key_ref.value_ref.own_key_ref.own_value_ref, ...), custom_call_target="tpu_custom_call" | custom-call | flops 2516582400 | bytes 34242560 | tf_op jit(solution)/shard_map/self_forward/pallas_call | solution.py:440
  214.8 4.6 fusion.89
  220.3 5.8 add_convert_fusion.4.query_ref
  227.4 7.4 add_convert_fusion.2.key_ref.value_ref
  234.7 27.9 %cross_forward.1 = (bf16[960,1024]{1,0:T(8,128)(2,1)}, f32[960,1024]{1,0:T(8,128)}) custom-call(bf16[960,1024]{1,0:T(8,128)(2,1)} %add_convert_fusion.4.query_ref, bf16[640,2048]{1,0:T(8,128)(2,1)} %add_convert_fusion.2.key_ref.value_ref, bf16[640,2048]{1,0:T(8,128)(2,1)} %add_convert_fusion.2.key_ref.value_ref, f32[960,640]{1,0:T(8,128)} %get-tuple-element.112.mask_ref), custom_call_target="tpu_custom_call" | custom-call | flops 2516582400 | bytes 15564800 | tf_op jit(solution)/shard_map/cross_forward/pallas_call | solution.py:440
  262.6 4.8 fusion.90
  269.3 27.0 %add_convert_fusion = (bf16[960,4096]{1,0:T(8,128)(2,1)}, bf16[960,4096]{1,0:T(8,128)(2,1)}) fusion(f32[4096]{0:T(1024)S(1)} %slice.177, bf16[12800,1024]{1,0:T(8,128)(2,1)} %bitcast.85, f32[960,1024]{1,0:T(8,128)S(1)} %get-tuple-element.119, f32[1024]{0:T(1024)S(1)} %bitcast.112, f32[1024]{0:T(1024)S(1)} %bitcast.99, f32[960]{0:T(1024)S(1)} %add_rsqrt_fusion.1, ...), kind=kOutput, calls=%fused_computation.3 | convolution fusion | flops 8168079360 | bytes 28081664 | tf_op jit(solution)/shard_map/dot_general | solution.py:64
  296.3 14.1 %fusion.91 = (f32[960]{0:T(1024)S(1)}, f32[960,1024]{1,0:T(8,128)S(1)}) fusion(f32[1024]{0:T(1024)S(1)} %bitcast.119, bf16[960,4096]{1,0:T(8,128)(2,1)} %get-tuple-element.88, bf16[4096,1024]{1,0:T(8,128)(2,1)} %all-gather.2.cloned.1.call-done.weight_ref, f32[1024]{0:T(1024)S(1)} %bitcast.113, f32[1024]{0:T(1024)S(1)} %bitcast.100, ...), kind=kOutput, calls=%fused_computation.208 | convolution fusion | flops 8059943936 | bytes 24141056 | tf_op jit(solution)/shard_map/dot_general | solution.py:54
  313.4 3.7 fusion.14
  317.1 4.1 convert_reduce_fusion.2
  322.5 11.7 %convolution_convert_fusion.1 = bf16[4096,1024]{1,0:T(8,128)(2,1)} fusion(bf16[960,4096]{1,0:T(8,128)(2,1)S(1)} %bitcast.123, bf16[960,1024]{1,0:T(8,128)(2,1)S(1)} %get-tuple-element.77.grad_ref), kind=kOutput, calls=%fused_computation.7 | convolution fusion | flops 8057257984 | bytes 18219008 | tf_op jit(solution)/shard_map/dot_general | solution.py:58
  334.3 15.1 %pre_and_sum.1 = (bf16[960,4096]{1,0:T(8,128)(2,1)}, f32[1,4096]{1,0:T(1,128)}) custom-call(bf16[960,1024]{1,0:T(8,128)(2,1)} %copy-done.23, bf16[4096,1024]{1,0:T(8,128)(2,1)} %all-gather.2.cloned.1.call-done.weight_ref, bf16[960,4096]{1,0:T(8,128)(2,1)} %get-tuple-element.87.slope_ref), custom_call_target="tpu_custom_call" | custom-call | flops 8053063680 | bytes 26083328 | tf_op jit(solution)/shard_map/pre_and_sum/pallas_call | solution.py:1225
  349.4 15.7 %convolution_convert_fusion = bf16[4096,1024]{1,0:T(8,128)(2,1)} fusion(bf16[960,4096]{1,0:T(8,128)(2,1)} %get-tuple-element.42, f32[960,1024]{1,0:T(8,128)S(1)} %copy-done.6, f32[1024]{0:T(1024)S(1)} %bitcast.114, f32[1024]{0:T(1024)S(1)} %bitcast.101, f32[960]{0:T(1024)S(1)} %add_rsqrt_fusion.1, f32[960]{0:T(1024)S(1)} %broadcast_multiply_fusion.7), kind=kOutput, calls=%fused_computation.6 | convolution fusion | flops 8062173184 | bytes 20200960 | tf_op jit(solution)/shard_map/dot_general | solution.py:58
  365.2 18.8 %multiply_reduce_fusion = (f32[1024]{0:T(1024)S(1)}, f32[960]{0:T(1024)S(1)}, f32[960]{0:T(1024)S(1)}, f32[1024]{0:T(1024)S(1)}, f32[960,1024]{1,0:T(8,128)}) fusion(f32[960,1024]{1,0:T(8,128)} %copy-done.5, f32[960]{0:T(1024)S(1)} %add_rsqrt_fusion.1, f32[960]{0:T(1024)S(1)} %broadcast_multiply_fusion.7, f32[1024]{0:T(1024)S(1)} %bitcast.102, ...), kind=kOutput, calls=%fused_computation.28 | convolution fusion | flops 8073703424 | bytes 30062592 | tf_op jit(solution)/shard_map/dot_general | solution.py:54
  384.0 3.0 convert_reduce_fusion.3
  387.0 6.5 fusion.49.context_ref
  393.5 45.0 %cross_backward.1 = (bf16[960,1024]{1,0:T(8,128)(2,1)}, bf16[640,1024]{1,0:T(8,128)(2,1)}, bf16[640,1024]{1,0:T(8,128)(2,1)}) custom-call(bf16[960,1024]{1,0:T(8,128)(2,1)} %add_convert_fusion.4.query_ref, bf16[640,2048]{1,0:T(8,128)(2,1)} %add_convert_fusion.2.key_ref.value_ref, bf16[640,2048]{1,0:T(8,128)(2,1)} %add_convert_fusion.2.key_ref.value_ref, ...), custom_call_target="tpu_custom_call" | custom-call | flops 6291456000 | bytes 20152320 | tf_op jit(solution)/shard_map/cross_backward/pallas_call | solution.py:440
  438.5 3.6 fusion.28
  442.2 3.3 fusion.55
  447.1 4.9 multiply_reduce_fusion.1
  453.8 6.5 fusion.46.context_ref
  460.4 68.1 %self_backward.1 = (bf16[960,1024]{1,0:T(8,128)(2,1)}, bf16[1280,1024]{1,0:T(8,128)(2,1)}, bf16[1280,1024]{1,0:T(8,128)(2,1)}, f32[960,512]{1,0:T(8,128)}) custom-call(bf16[960,1024]{1,0:T(8,128)(2,1)} %add_convert_fusion.5.query_ref, bf16[1280,2048]{1,0:T(8,128)(2,1)} %add_convert_fusion.1.key_ref.value_ref.own_key_ref.own_value_ref, ...), custom_call_target="tpu_custom_call" | custom-call | flops 6291456000 | bytes 43909120 | tf_op jit(solution)/shard_map/self_backward/pallas_call | solution.py:440
  531.6 5.8 fusion.43
  537.4 3.8 convert_dynamic-update-slice_fusion.7
  541.2 4.6 fusion.33
  545.9 4.2 convert_dynamic-update-slice_fusion.6
  550.1 4.1 convert_dynamic-update-slice_fusion.5
  554.2 6.3 convolution_add_fusion
  563.4 5.5 convert_dynamic-update-slice_fusion.4
  570.2 13.1 %reduce-scatter.7.cloned.1.call-done = bf16[128,1024]{1,0:T(8,128)(2,1)} async-done(((bf16[256,1024]{1,0:T(8,128)(2,1)}), bf16[128,1024]{1,0:T(8,128)(2,1)}) %reduce-scatter.7.cloned.1.call-update) | async-done | bytes 262160 | tf_op jit(solution)/shard_map/reduce_scatter | solution.py:678
  583.3 3.0 convolution_convert_fusion.2
  595.5 4.1 convert_dynamic-update-slice_fusion.3
  599.6 3.2 convert_dynamic-update-slice_fusion.2
  602.8 3.2 convert_dynamic-update-slice_fusion.1
  606.5 6.6 convert_dynamic-update-slice_fusion
  613.1 5.4 convert_dynamic-update-slice_fusion.8
  619.2 6.6 collective-permute-start.4
  627.2 2.6 multiply_subtract_fusion.1
  629.8 7.9 %collective-permute-start.7 = (bf16[128,1024]{1,0:T(8,128)(2,1)}, bf16[128,1024]{1,0:T(8,128)(2,1)S(1)}, u32[]{:S(2)}, u32[]{:S(2)}) collective-permute-start(bf16[128,1024]{1,0:T(8,128)(2,1)} %reduce-scatter.11.cloned.1.call-done), channel_id=1, source_target_pairs={{11,24},{14,25},{17,26},{20,27},{23,28},{26,29},{29,30}} | collective-permute-start | bytes 786440 | tf_op jit(solution)/shard_map/ppermute | solution.py:693
  642.1 106.0 %sum_slabs.1 = f32[400,1024]{1,0:T(8,128)} custom-call(bf16[3,2,2,2,400,1024]{5,4,3,2,1,0:T(8,128)(2,1)} %bitcast.20.grad_ref), custom_call_target="tpu_custom_call" | custom-call | flops 9830400 | bytes 39321600 | tf_op jit(solution)/shard_map/sum_slabs/pallas_call | solution.py:948
  752.3 6.4 multiply_subtract_fusion
  758.7 2.7 fusion.58
  (270 shorter events, 52.9 us)
Async XLA Ops:
  7.2 137.1 %copy-start.33 = (bf16[320,1024]{1,0:T(8,128)(2,1)S(1)}, bf16[320,1024]{1,0:T(8,128)(2,1)}, u32[]{:S(2)}) copy-start(bf16[320,1024]{1,0:T(8,128)(2,1)} %param.20) | copy-start | bytes 1966084
  7.2 289.1 %all-gather.2.cloned.1.call-start = ((), (), s32[]{:S(2)}) async-start(), calls=%async_computation.4 | async-start | bytes 8650752 | tf_op jit(solution)/shard_map/all_gather | solution.py:1285
  9.7 138.2 %copy-start.67 = (s32[1,8]{1,0:T(1,128)S(1)}, s32[1,8]{1,0:T(1,128)}, u32[]{:S(2)}) copy-start(s32[1,8]{1,0:T(1,128)} %param.21) | copy-start | bytes 100
  9.7 138.6 %copy-start.20 = (bf16[320,1024]{1,0:T(8,128)(2,1)S(1)}, bf16[320,1024]{1,0:T(8,128)(2,1)}, u32[]{:S(2)}) copy-start(bf16[320,1024]{1,0:T(8,128)(2,1)} %main_ref.1) | copy-start | bytes 1966084
  144.3 416.2 %reduce-scatter.5.cloned.1.call-start = ((), (), s32[]{:S(2)}) async-start(), calls=%async_computation.5 | async-start | bytes 8912896 | tf_op jit(solution)/shard_map/reduce_scatter | solution.py:677
  144.3 81.8 %collective-permute-start = (bf16[320,1024]{1,0:T(8,128)(2,1)S(1)}, bf16[320,1024]{1,0:T(8,128)(2,1)}, u32[]{:S(2)}, u32[]{:S(2)}) collective-permute-start(bf16[320,1024]{1,0:T(8,128)(2,1)S(1)} %copy-done.33), channel_id=1, source_target_pairs={{0,1},{1,0},{2,3},{3,2},{4,5},{5,4},{6,7},{7,6},{8,9},{9,8},{10,11... | collective-permute-start | bytes 1966088 | tf_op jit(solution)/shard_map/ppermute | solution.py:706
  147.6 9.5 %copy-start.15 = (bf16[16,32,1024]{2,1,0:T(8,128)(2,1)}, bf16[16,32,1024]{2,1,0:T(8,128)(2,1)S(1)}, u32[]{:S(2)}) copy-start(bf16[16,32,1024]{2,1,0:T(8,128)(2,1)S(1)} %copy.42) | copy-start | bytes 3145732
  149.8 15.1 %copy-start.38 = (bf16[320,1024]{1,0:T(8,128)(2,1)}, bf16[320,1024]{1,0:T(8,128)(2,1)S(1)}, u32[]{:S(2)}) copy-start(bf16[320,1024]{1,0:T(8,128)(2,1)S(1)} %get-tuple-element.94) | copy-start | bytes 1966084
  149.8 15.1 %copy-start.40 = (bf16[320,1024]{1,0:T(8,128)(2,1)}, bf16[320,1024]{1,0:T(8,128)(2,1)S(1)}, u32[]{:S(2)}) copy-start(bf16[320,1024]{1,0:T(8,128)(2,1)S(1)} %get-tuple-element.95) | copy-start | bytes 1966084
  151.7 7.9 %copy-start.43 = (bf16[960,1024]{1,0:T(8,128)(2,1)}, bf16[960,1024]{1,0:T(8,128)(2,1)S(1)}, u32[]{:S(2)}) copy-start(bf16[960,1024]{1,0:T(8,128)(2,1)S(1)} %constant_dynamic-update-slice_fusion) | copy-start | bytes 5898244
  177.3 37.5 %copy-start.44 = (bf16[960,1024]{1,0:T(8,128)(2,1)S(1)}, bf16[960,1024]{1,0:T(8,128)(2,1)}, u32[]{:S(2)}) copy-start(bf16[960,1024]{1,0:T(8,128)(2,1)} %copy-done.43) | copy-start | bytes 5898244
  219.5 43.1 %copy-start.9 = (f32[960,1024]{1,0:T(8,128)}, f32[960,1024]{1,0:T(8,128)S(1)}, u32[]{:S(2)}) copy-start(f32[960,1024]{1,0:T(8,128)S(1)} %get-tuple-element.117) | copy-start | bytes 11796484
  219.5 43.1 %copy-start.49 = (f32[960]{0:T(1024)}, f32[960]{0:T(1024)S(1)}, u32[]{:S(2)}) copy-start(f32[960]{0:T(1024)S(1)} %broadcast_multiply_fusion.8) | copy-start | bytes 11524
  220.3 42.3 %copy-start.55 = (f32[960]{0:T(1024)}, f32[960]{0:T(1024)S(1)}, u32[]{:S(2)}) copy-start(f32[960]{0:T(1024)S(1)} %add_rsqrt_fusion.2) | copy-start | bytes 11524
  220.3 42.3 %copy-start.53 = (f32[1,1024]{1,0:T(1,128)}, f32[1,1024]{1,0:T(1,128)S(1)}, u32[]{:S(2)}) copy-start(f32[1,1024]{1,0:T(1,128)S(1)} %get-tuple-element.110) | copy-start | bytes 12292
  220.3 42.3 %copy-start.62 = (f32[1,1024]{1,0:T(1,128)}, f32[1,1024]{1,0:T(1,128)S(1)}, u32[]{:S(2)}) copy-start(f32[1,1024]{1,0:T(1,128)S(1)} %get-tuple-element.109) | copy-start | bytes 12292
  227.3 7.4 copy-start.34
  227.4 7.4 copy-start.36
  310.5 6.6 copy-start
  313.4 9.1 %slice-start.2 = ((s8[7864320]{0:T(1024)(128)(4,1)}), s8[4194304]{0:T(1024)(128)(4,1)S(1)}, s32[]{:S(2)}) async-start(s8[7864320]{0:T(1024)(128)(4,1)} %bitcast.122), calls=%async_computation.12 | async-start | bytes 8388608
  334.2 235.7 %reduce-scatter.9.cloned.1.call-start = ((), (), s32[]{:S(2)}) async-start(), calls=%async_computation.7 | async-start | bytes 8912896 | tf_op jit(solution)/shard_map/reduce_scatter | solution.py:677
  334.3 15.1 %copy-start.6 = (f32[960,1024]{1,0:T(8,128)S(1)}, f32[960,1024]{1,0:T(8,128)}, u32[]{:S(2)}) copy-start(f32[960,1024]{1,0:T(8,128)} %copy-done.5) | copy-start | bytes 11796484
  365.2 218.1 %reduce-scatter.7.cloned.1.call-start = ((), (), s32[]{:S(2)}) async-start(), calls=%async_computation.6 | async-start | bytes 786432 | tf_op jit(solution)/shard_map/reduce_scatter | solution.py:678
  365.2 18.8 %copy-start.7 = (f32[960,1024]{1,0:T(8,128)S(1)}, f32[960,1024]{1,0:T(8,128)}, u32[]{:S(2)}) copy-start(f32[960,1024]{1,0:T(8,128)} %copy-done.5) | copy-start | bytes 11796484
  387.0 60.0 %copy-start.18 = (f32[960,1024]{1,0:T(8,128)}, f32[960,1024]{1,0:T(8,128)S(1)}, u32[]{:S(2)}) copy-start(f32[960,1024]{1,0:T(8,128)S(1)} %get-tuple-element.79) | copy-start | bytes 11796484
  445.7 123.2 %collective-permute-start.2 = (bf16[320,1024]{1,0:T(8,128)(2,1)S(1)}, bf16[320,1024]{1,0:T(8,128)(2,1)S(1)}, u32[]{:S(2)}, u32[]{:S(2)}) collective-permute-start(bf16[320,1024]{1,0:T(8,128)(2,1)S(1)} %dynamic-slice_convert_fusion), channel_id=1, source_target_pairs={{0,1},{1,0},{2,3},{3,2},{4,5},{5,4},{6,7},{7,6},{8,9},{9,8},{10,11... | collective-permute-start | bytes 1966088 | tf_op jit(solution)/shard_map/ppermute | solution.py:706
  453.8 6.5 copy-start.2
  460.4 70.2 %copy-start.31 = (bf16[640,1024]{1,0:T(8,128)(2,1)S(1)}, bf16[640,1024]{1,0:T(8,128)(2,1)}, u32[]{:S(2)}) copy-start(bf16[640,1024]{1,0:T(8,128)(2,1)} %get-tuple-element.52) | copy-start | bytes 3932164
  554.2 6.4 copy-start.13
  560.5 58.0 %reduce-scatter.11.cloned.1.call-start = ((), (), s32[]{:S(2)}) async-start(), calls=%async_computation.8 | async-start | bytes 786432 | tf_op jit(solution)/shard_map/reduce_scatter | solution.py:678
  563.4 19.9 %copy-start.12 = (f32[960,512]{1,0:T(8,128)S(1)}, f32[960,512]{1,0:T(8,128)}, u32[]{:S(2)}) copy-start(f32[960,512]{1,0:T(8,128)} %get-tuple-element.48) | copy-start | bytes 5898244
  570.0 180.0 %all-reduce.5.cloned.1.call-start = ((), (), s32[]{:S(2)}) async-start(), calls=%async_computation.9 | async-start | bytes 147456 | tf_op jit(solution)/shard_map/psum | solution.py:1438
  592.5 166.2 %collective-permute-start.1 = (bf16[320,1024]{1,0:T(8,128)(2,1)}, bf16[320,1024]{1,0:T(8,128)(2,1)}, u32[]{:S(2)}, u32[]{:S(2)}) collective-permute-start(bf16[320,1024]{1,0:T(8,128)(2,1)} %dynamic-slice_convert_fusion.1), channel_id=1, source_target_pairs={{0,1},{1,0},{2,3},{3,2},{4,5},{5,4},{6,7},{7,6},{8,9},{9,8},{10,11... | collective-permute-start | bytes 1966088 | tf_op jit(solution)/shard_map/ppermute | solution.py:706
  606.4 6.6 copy-start.48
  606.5 6.6 copy-start.8
  613.1 14.1 %copy-start.22 = (f32[128,1024]{1,0:T(8,128)S(1)}, f32[128,1024]{1,0:T(8,128)}, u32[]{:S(2)}) copy-start(f32[128,1024]{1,0:T(8,128)} %param.30) | copy-start | bytes 1572868
  613.1 14.1 %copy-start.42 = (bf16[128,1024]{1,0:T(8,128)(2,1)S(1)}, bf16[128,1024]{1,0:T(8,128)(2,1)}, u32[]{:S(2)}) copy-start(bf16[128,1024]{1,0:T(8,128)(2,1)} %reduce-scatter.7.cloned.1.call-done) | copy-start | bytes 786436
  618.5 11.3 %collective-permute-start.3 = (bf16[128,1024]{1,0:T(8,128)(2,1)}, bf16[128,1024]{1,0:T(8,128)(2,1)S(1)}, u32[]{:S(2)}, u32[]{:S(2)}) collective-permute-start(bf16[128,1024]{1,0:T(8,128)(2,1)} %reduce-scatter.11.cloned.1.call-done), channel_id=1, source_target_pairs={{7,24},{10,25},{13,26},{16,27},{19,28},{22,29},{25,30},{28,31}} | collective-permute-start | bytes 786440 | tf_op jit(solution)/shard_map/ppermute | solution.py:693
  619.2 19.2 %collective-permute-start.4 = (bf16[128,1024]{1,0:T(8,128)(2,1)}, bf16[128,1024]{1,0:T(8,128)(2,1)S(1)}, u32[]{:S(2)}, u32[]{:S(2)}) collective-permute-start(bf16[128,1024]{1,0:T(8,128)(2,1)} %reduce-scatter.11.cloned.1.call-done), channel_id=1, source_target_pairs={{8,24},{11,25},{14,26},{17,27},{20,28},{23,29},{26,30},{29,31}} | collective-permute-start | bytes 786440 | tf_op jit(solution)/shard_map/ppermute | solution.py:693
  625.8 13.3 %collective-permute-start.5 = (bf16[128,1024]{1,0:T(8,128)(2,1)}, bf16[128,1024]{1,0:T(8,128)(2,1)S(1)}, u32[]{:S(2)}, u32[]{:S(2)}) collective-permute-start(bf16[128,1024]{1,0:T(8,128)(2,1)} %reduce-scatter.11.cloned.1.call-done), channel_id=1, source_target_pairs={{9,24},{12,25},{15,26},{18,27},{21,28},{24,29},{27,30},{30,31}} | collective-permute-start | bytes 786440 | tf_op jit(solution)/shard_map/ppermute | solution.py:693
  626.5 13.4 %collective-permute-start.6 = (bf16[128,1024]{1,0:T(8,128)(2,1)}, bf16[128,1024]{1,0:T(8,128)(2,1)S(1)}, u32[]{:S(2)}, u32[]{:S(2)}) collective-permute-start(bf16[128,1024]{1,0:T(8,128)(2,1)} %reduce-scatter.11.cloned.1.call-done), channel_id=1, source_target_pairs={{10,24},{13,25},{16,26},{19,27},{22,28},{25,29},{28,30},{31,31}} | collective-permute-start | bytes 786440 | tf_op jit(solution)/shard_map/ppermute | solution.py:693
  629.8 11.5 %collective-permute-start.7 = (bf16[128,1024]{1,0:T(8,128)(2,1)}, bf16[128,1024]{1,0:T(8,128)(2,1)S(1)}, u32[]{:S(2)}, u32[]{:S(2)}) collective-permute-start(bf16[128,1024]{1,0:T(8,128)(2,1)} %reduce-scatter.11.cloned.1.call-done), channel_id=1, source_target_pairs={{11,24},{14,25},{17,26},{20,27},{23,28},{26,29},{29,30}} | collective-permute-start | bytes 786440 | tf_op jit(solution)/shard_map/ppermute | solution.py:693
  642.1 108.8 %copy-start.47 = (f32[7,1024]{1,0:T(8,128)S(1)}, f32[7,1024]{1,0:T(8,128)}, u32[]{:S(2)}) copy-start(f32[7,1024]{1,0:T(8,128)} %param.33) | copy-start | bytes 86020
  642.1 108.8 %copy-start.51 = (f32[7,1024]{1,0:T(8,128)S(1)}, f32[7,1024]{1,0:T(8,128)}, u32[]{:S(2)}) copy-start(f32[7,1024]{1,0:T(8,128)} %param.34) | copy-start | bytes 86020
  642.1 108.9 %copy-start.52 = (f32[7,1024]{1,0:T(8,128)S(1)}, f32[7,1024]{1,0:T(8,128)}, u32[]{:S(2)}) copy-start(f32[7,1024]{1,0:T(8,128)} %param.35) | copy-start | bytes 86020
  642.1 109.5 %copy-start.61 = (f32[336]{0:T(512)S(1)}, f32[336]{0:T(512)}, u32[]{:S(2)}) copy-start(f32[336]{0:T(512)} %param.27) | copy-start | bytes 4036
  642.1 109.5 %copy-start.64 = (f32[336]{0:T(512)S(1)}, f32[336]{0:T(512)}, u32[]{:S(2)}) copy-start(f32[336]{0:T(512)} %param.28) | copy-start | bytes 4036
  642.1 109.5 %copy-start.65 = (f32[336]{0:T(512)S(1)}, f32[336]{0:T(512)}, u32[]{:S(2)}) copy-start(f32[336]{0:T(512)} %param.29) | copy-start | bytes 4036
  (40 other events, 148.3 us)
Sparse Core Ops, SparseCore 0:
  144.4 87.4 all-gather.1
  334.3 112.6 reduce-scatter.4
  451.1 104.3 reduce-scatter.8
  560.6 22.5 reduce-scatter.6
  585.5 18.0 reduce-scatter.10
  618.6 127.5 all-reduce.4

commit v6 on v5

--- a/solution.py
+++ b/solution.py
@@ -137,6 +137,11 @@
     lane = lax.broadcasted_iota(jnp.int32, block.shape, 1)
     turned = pltpu.roll(block, HEAD_DIM, 1)
     return jnp.where((lane < HEAD_DIM) == (head == 0), block, turned)
+
+
+def in_turns(works):
+    while any([next(work, works) is not works for work in works]):
+        pass
 
 
 def self_forward_kernel(
@@ -366,11 +371,12 @@
     query_ref, key_ref, value_ref, mask_ref, context_ref, log_ref, score_ref, prob_ref
 ):
     rows = mask_ref.shape[0]
-    for head in range(2):
+    def head_steps(head):
         at = head * HEAD_DIM
         head_lanes = slice(at, at + HEAD_DIM)
         query = query_ref[:, head_lanes] * jnp.bfloat16(SCORE_SCALE)
         score_ref[head] = dot_rows(query, key_ref[:, head_lanes])
+        yield
         for row in range(0, rows, CHUNK):
             part = slice(row, min(row + CHUNK, rows))
             scores = score_ref[head, part] + mask_ref[part]
@@ -384,6 +390,9 @@
         context_ref[:, head_lanes] = matmul(prob_ref[head], value_ref[:, head_lanes]).astype(
             jnp.bfloat16
         )
+        yield
+
+    in_turns([head_steps(head) for head in range(2)])
 
 
 def cross_backward_kernel(
@@ -402,7 +411,7 @@
     score_grad_ref,
 ):
     rows = mask_ref.shape[0]
-    for head in range(2):
+    def head_steps(head):
         at = head * HEAD_DIM
         head_lanes = slice(at, at + HEAD_DIM)
         query = query_ref[:, head_lanes] * jnp.bfloat16(SCORE_SCALE)
@@ -410,6 +419,7 @@
         context = context_ref[:, head_lanes]
         score_ref[head] = dot_rows(query, keys)
         prob_grad_ref[head] = dot_rows(context, value_ref[:, head_lanes])
+        yield
         for row in range(0, rows, CHUNK):
             part = slice(row, min(row + CHUNK, rows))
             probs = jnp.exp(
@@ -419,11 +429,15 @@
             row_dot = jnp.sum(probs * prob_grad, axis=1, keepdims=True)
             prob_ref[head, part] = probs.astype(jnp.bfloat16)
             score_grad_ref[head, part] = (probs * (prob_grad - row_dot)).astype(jnp.bfloat16)
+        yield
         query_grad_ref[:, head_lanes] = (matmul(score_grad_ref[head], keys) * SCORE_SCALE).astype(
             jnp.bfloat16
         )
-        key_grad_ref[:, head_lanes] = outer_sum(score_grad_ref[head], query).astype(jnp.bfloat16)
-        value_grad_ref[:, head_lanes] = outer_sum(prob_ref[head], context).astype(jnp.bfloat16)
+        key_grad_ref[:, head_lanes] = outer_sum(query, score_grad_ref[head]).T.astype(jnp.bfloat16)
+        value_grad_ref[:, head_lanes] = outer_sum(context, prob_ref[head]).T.astype(jnp.bfloat16)
+        yield
+
+    in_turns([head_steps(head) for head in range(2)])
 
 
 def pair_block(row_count, row_block=0, first_pair=0):

time: 778 us -> 765 us (0.983)
  Pallas kernels: 429 us -> 416 us
    pallas_call x4, Pallas kernels: 177 us -> 163 us  [attention_call(): pl.pallas_call(kernel, grid=(HEADS // 2,), in_specs=in_specs, out_specs=o...]
  transfers between devices with their start and end apart: 14 -> 14, of which waited for: 2 -> 2; matrix products, arithmetic and copies ran while one was open for 31% -> 31% of each run, Pallas kernels for 39% -> 38%
where the time goes in v6:
time: 765 us; the launch traced here: 755 us
  Pallas kernels  416 us (54%)
  matrix products  215 us (28%)
  other arithmetic  46.8 us (6%)
  local copies, waits for them, and re-layouts  26.3 us (3%)
  starting transfers between devices  19.6 us (3%)
  between operations  16.8 us (2%)
  waiting for transfers between devices  14.9 us (2%)
    pallas_call x4, Pallas kernels, attention_call(): pl.pallas_call(kernel, grid=(HEADS // 2,), in_specs=in_specs, out_specs=o...  163 us
    pallas_call x1, Pallas kernels, gather_shards(): pl.pallas_call(gather_kernel, out_shape=[jax.ShapeDtypeStruct((4, 2, 2, 2...  131 us
    pallas_call x1, Pallas kernels, sum_slabs(): pl.pallas_call(sum_kernel, out_shape=jax.ShapeDtypeStruct((block, width),...  106 us
    dot_general x11, matrix products, matmul(): return jnp.dot(left_side, right_side, preferred_element_type=jnp.float32)  76.2 us
    dot_general x12, matrix products, outer_sum(): lax.dot_general(left_side, right_side, (((0,), (0,)), ((), ())), preferre...  70.2 us
    dot_general x8, matrix products, times_transpose(): lax.dot_general(left_side, right_side, (((1,), (1,)), ((), ())), preferre...  68.8 us
    ppermute x5, starting transfers between devices, to_last_quarter(): blocks.append(lax.ppermute(share, ('dp', 'stream'), pairs))  16.5 us
  transfers between devices with their start and end apart: 14, of which 2 were waited for; matrix products, arithmetic and copies ran while one was open for 31% of the time, Pallas kernels for 38%

profile of v6, /device:TPU:11, one launch (start us, length us, event | category | flops | bytes accessed | tf_op | source)
XLA Modules:
  0.0 755.3 jit_solution(3603715691557496200)
XLA Ops:
  7.2 2.5 convert_bitcast_fusion.shard_ref
  12.9 131.3 %gather_shards.1 = (bf16[4,2,2,2,400,1024]{5,4,3,2,1,0:T(8,128)(2,1)}, bf16[4,2,2,2,16,128]{5,4,3,2,1,0:T(8,128)(2,1)}, bf16[320,1024]{1,0:T(8,128)(2,1)}) custom-call(bf16[400,1024]{1,0:T(8,128)(2,1)} %convert_bitcast_fusion.shard_ref, bf16[16,128]{1,0:T(8,128)(2,1)} %pad_bitcast_fusion.bias_ref, bf16[320,1024]{1,0:T(8,128)(2,1)} %main_ref.1), custom_call_target="tpu_custom_call" | custom-call | bytes 26214400 | tf_op jit(solution)/shard_map/gather_shards/pallas_call | solution.py:1202
  153.7 3.1 compare_select_fusion
  156.8 2.6 convolution_add_fusion.2.table_ref
  159.4 5.3 add_convert_fusion.5.query_ref
  164.7 11.4 %add_convert_fusion.1.key_ref.value_ref.own_key_ref.own_value_ref = bf16[1280,2048]{1,0:T(8,128)(2,1)} fusion(f32[2048]{0:T(1024)S(1)} %concatenate.39, bf16[12800,1024]{1,0:T(8,128)(2,1)} %bitcast.80, bf16[640,1024]{1,0:T(8,128)(2,1)S(1)} %copy-done.29, bf16[320,1024]{1,0:T(8,128)(2,1)S(1)} %get-tuple-element.95, bf16[320,1024]{1,0:T(8,128)(2,1)S(1)} %get-tuple-element.94), kind=kOutput, calls=%fused_computation.5 | convolution fusion | flops 5381816320 | bytes 12066816 | tf_op jit(solution)/shard_map/dot_general | solution.py:64
  177.1 35.9 %self_forward.1 = (bf16[960,1024]{1,0:T(8,128)(2,1)}, f32[960,1024]{1,0:T(8,128)}) custom-call(bf16[960,1024]{1,0:T(8,128)(2,1)} %add_convert_fusion.5.query_ref, bf16[1280,2048]{1,0:T(8,128)(2,1)} %add_convert_fusion.1.key_ref.value_ref.own_key_ref.own_value_ref, bf16[1280,2048]{1,0:T(8,128)(2,1)} %add_convert_fusion.1.key_ref.value_ref.own_key_ref.own_value_ref, ...), custom_call_target="tpu_custom_call" | custom-call | flops 2516582400 | bytes 34242560 | tf_op jit(solution)/shard_map/self_forward/pallas_call | solution.py:454
  214.8 4.6 fusion.89
  220.3 5.8 add_convert_fusion.4.query_ref
  227.3 7.4 add_convert_fusion.2.key_ref.value_ref
  234.7 23.5 %cross_forward.1 = (bf16[960,1024]{1,0:T(8,128)(2,1)}, f32[960,1024]{1,0:T(8,128)}) custom-call(bf16[960,1024]{1,0:T(8,128)(2,1)} %add_convert_fusion.4.query_ref, bf16[640,2048]{1,0:T(8,128)(2,1)} %add_convert_fusion.2.key_ref.value_ref, bf16[640,2048]{1,0:T(8,128)(2,1)} %add_convert_fusion.2.key_ref.value_ref, f32[960,640]{1,0:T(8,128)} %get-tuple-element.112.mask_ref), custom_call_target="tpu_custom_call" | custom-call | flops 2516582400 | bytes 15564800 | tf_op jit(solution)/shard_map/cross_forward/pallas_call | solution.py:454
  258.3 4.8 fusion.90
  264.9 26.9 %add_convert_fusion = (bf16[960,4096]{1,0:T(8,128)(2,1)}, bf16[960,4096]{1,0:T(8,128)(2,1)}) fusion(f32[4096]{0:T(1024)S(1)} %slice.177, bf16[12800,1024]{1,0:T(8,128)(2,1)} %bitcast.85, f32[960,1024]{1,0:T(8,128)S(1)} %get-tuple-element.119, f32[1024]{0:T(1024)S(1)} %bitcast.112, f32[1024]{0:T(1024)S(1)} %bitcast.99, f32[960]{0:T(1024)S(1)} %add_rsqrt_fusion.1, ...), kind=kOutput, calls=%fused_computation.3 | convolution fusion | flops 8168079360 | bytes 28081664 | tf_op jit(solution)/shard_map/dot_general | solution.py:64
  291.9 14.1 %fusion.91 = (f32[960]{0:T(1024)S(1)}, f32[960,1024]{1,0:T(8,128)S(1)}) fusion(f32[1024]{0:T(1024)S(1)} %bitcast.119, bf16[960,4096]{1,0:T(8,128)(2,1)} %get-tuple-element.88, bf16[4096,1024]{1,0:T(8,128)(2,1)} %all-gather.2.cloned.1.call-done.weight_ref, f32[1024]{0:T(1024)S(1)} %bitcast.113, f32[1024]{0:T(1024)S(1)} %bitcast.100, ...), kind=kOutput, calls=%fused_computation.208 | convolution fusion | flops 8059943936 | bytes 24141056 | tf_op jit(solution)/shard_map/dot_general | solution.py:54
  309.0 3.7 fusion.14
  312.7 4.1 convert_reduce_fusion.2
  318.1 11.5 %convolution_convert_fusion.1 = bf16[4096,1024]{1,0:T(8,128)(2,1)} fusion(bf16[960,4096]{1,0:T(8,128)(2,1)S(1)} %bitcast.123, bf16[960,1024]{1,0:T(8,128)(2,1)S(1)} %get-tuple-element.77.grad_ref), kind=kOutput, calls=%fused_computation.7 | convolution fusion | flops 8057257984 | bytes 18219008 | tf_op jit(solution)/shard_map/dot_general | solution.py:58
  329.7 15.1 %pre_and_sum.1 = (bf16[960,4096]{1,0:T(8,128)(2,1)}, f32[1,4096]{1,0:T(1,128)}) custom-call(bf16[960,1024]{1,0:T(8,128)(2,1)} %copy-done.23, bf16[4096,1024]{1,0:T(8,128)(2,1)} %all-gather.2.cloned.1.call-done.weight_ref, bf16[960,4096]{1,0:T(8,128)(2,1)} %get-tuple-element.87.slope_ref), custom_call_target="tpu_custom_call" | custom-call | flops 8053063680 | bytes 26083328 | tf_op jit(solution)/shard_map/pre_and_sum/pallas_call | solution.py:1239
  344.8 15.7 %convolution_convert_fusion = bf16[4096,1024]{1,0:T(8,128)(2,1)} fusion(bf16[960,4096]{1,0:T(8,128)(2,1)} %get-tuple-element.42, f32[960,1024]{1,0:T(8,128)S(1)} %copy-done.6, f32[1024]{0:T(1024)S(1)} %bitcast.114, f32[1024]{0:T(1024)S(1)} %bitcast.101, f32[960]{0:T(1024)S(1)} %add_rsqrt_fusion.1, f32[960]{0:T(1024)S(1)} %broadcast_multiply_fusion.7), kind=kOutput, calls=%fused_computation.6 | convolution fusion | flops 8062173184 | bytes 20200960 | tf_op jit(solution)/shard_map/dot_general | solution.py:58
  360.6 19.1 %multiply_reduce_fusion = (f32[1024]{0:T(1024)S(1)}, f32[960]{0:T(1024)S(1)}, f32[960]{0:T(1024)S(1)}, f32[1024]{0:T(1024)S(1)}, f32[960,1024]{1,0:T(8,128)}) fusion(f32[960,1024]{1,0:T(8,128)} %copy-done.5, f32[960]{0:T(1024)S(1)} %add_rsqrt_fusion.1, f32[960]{0:T(1024)S(1)} %broadcast_multiply_fusion.7, f32[1024]{0:T(1024)S(1)} %bitcast.102, ...), kind=kOutput, calls=%fused_computation.28 | convolution fusion | flops 8073703424 | bytes 30062592 | tf_op jit(solution)/shard_map/dot_general | solution.py:54
  379.8 3.0 convert_reduce_fusion.3
  382.8 6.5 fusion.49.context_ref
  389.3 35.8 %cross_backward.1 = (bf16[960,1024]{1,0:T(8,128)(2,1)}, bf16[640,1024]{1,0:T(8,128)(2,1)}, bf16[640,1024]{1,0:T(8,128)(2,1)}) custom-call(bf16[960,1024]{1,0:T(8,128)(2,1)} %add_convert_fusion.4.query_ref, bf16[640,2048]{1,0:T(8,128)(2,1)} %add_convert_fusion.2.key_ref.value_ref, bf16[640,2048]{1,0:T(8,128)(2,1)} %add_convert_fusion.2.key_ref.value_ref, ...), custom_call_target="tpu_custom_call" | custom-call | flops 6291456000 | bytes 20152320 | tf_op jit(solution)/shard_map/cross_backward/pallas_call | solution.py:454
  425.0 3.6 fusion.28
  428.7 3.3 fusion.55
  433.5 4.9 multiply_reduce_fusion.1
  439.9 6.5 fusion.46.context_ref
  446.5 67.9 %self_backward.1 = (bf16[960,1024]{1,0:T(8,128)(2,1)}, bf16[1280,1024]{1,0:T(8,128)(2,1)}, bf16[1280,1024]{1,0:T(8,128)(2,1)}, f32[960,512]{1,0:T(8,128)}) custom-call(bf16[960,1024]{1,0:T(8,128)(2,1)} %add_convert_fusion.5.query_ref, bf16[1280,2048]{1,0:T(8,128)(2,1)} %add_convert_fusion.1.key_ref.value_ref.own_key_ref.own_value_ref, ...), custom_call_target="tpu_custom_call" | custom-call | flops 6291456000 | bytes 43909120 | tf_op jit(solution)/shard_map/self_backward/pallas_call | solution.py:454
  517.5 5.8 fusion.43
  523.3 3.8 convert_dynamic-update-slice_fusion.7
  527.1 4.6 fusion.33
  531.8 4.2 convert_dynamic-update-slice_fusion.6
  536.0 4.1 convert_dynamic-update-slice_fusion.5
  540.1 6.3 convolution_add_fusion
  549.4 5.5 convert_dynamic-update-slice_fusion.4
  556.1 14.0 %reduce-scatter.7.cloned.1.call-done = bf16[128,1024]{1,0:T(8,128)(2,1)} async-done(((bf16[256,1024]{1,0:T(8,128)(2,1)}), bf16[128,1024]{1,0:T(8,128)(2,1)}) %reduce-scatter.7.cloned.1.call-update) | async-done | bytes 262160 | tf_op jit(solution)/shard_map/reduce_scatter | solution.py:692
  570.2 3.0 convolution_convert_fusion.2
  582.3 4.2 convert_dynamic-update-slice_fusion.3
  586.5 3.2 convert_dynamic-update-slice_fusion.2
  589.7 3.2 convert_dynamic-update-slice_fusion.1
  593.3 6.6 convert_dynamic-update-slice_fusion
  600.0 5.3 convert_dynamic-update-slice_fusion.8
  606.1 6.6 collective-permute-start.4
  614.1 2.6 multiply_subtract_fusion.1
  616.7 7.9 %collective-permute-start.7 = (bf16[128,1024]{1,0:T(8,128)(2,1)}, bf16[128,1024]{1,0:T(8,128)(2,1)S(1)}, u32[]{:S(2)}, u32[]{:S(2)}) collective-permute-start(bf16[128,1024]{1,0:T(8,128)(2,1)} %reduce-scatter.11.cloned.1.call-done), channel_id=1, source_target_pairs={{11,24},{14,25},{17,26},{20,27},{23,28},{26,29},{29,30}} | collective-permute-start | bytes 786440 | tf_op jit(solution)/shard_map/ppermute | solution.py:707
  628.9 106.1 %sum_slabs.1 = f32[400,1024]{1,0:T(8,128)} custom-call(bf16[3,2,2,2,400,1024]{5,4,3,2,1,0:T(8,128)(2,1)} %bitcast.20.grad_ref), custom_call_target="tpu_custom_call" | custom-call | flops 9830400 | bytes 39321600 | tf_op jit(solution)/shard_map/sum_slabs/pallas_call | solution.py:962
  739.2 6.4 multiply_subtract_fusion
  745.5 2.7 fusion.58
  (270 shorter events, 52.4 us)
Async XLA Ops:
  7.2 137.1 %copy-start.33 = (bf16[320,1024]{1,0:T(8,128)(2,1)S(1)}, bf16[320,1024]{1,0:T(8,128)(2,1)}, u32[]{:S(2)}) copy-start(bf16[320,1024]{1,0:T(8,128)(2,1)} %param.20) | copy-start | bytes 1966084
  7.2 284.7 %all-gather.2.cloned.1.call-start = ((), (), s32[]{:S(2)}) async-start(), calls=%async_computation.4 | async-start | bytes 8650752 | tf_op jit(solution)/shard_map/all_gather | solution.py:1299
  9.7 138.2 %copy-start.67 = (s32[1,8]{1,0:T(1,128)S(1)}, s32[1,8]{1,0:T(1,128)}, u32[]{:S(2)}) copy-start(s32[1,8]{1,0:T(1,128)} %param.21) | copy-start | bytes 100
  9.7 138.6 %copy-start.20 = (bf16[320,1024]{1,0:T(8,128)(2,1)S(1)}, bf16[320,1024]{1,0:T(8,128)(2,1)}, u32[]{:S(2)}) copy-start(bf16[320,1024]{1,0:T(8,128)(2,1)} %main_ref.1) | copy-start | bytes 1966084
  144.3 402.2 %reduce-scatter.5.cloned.1.call-start = ((), (), s32[]{:S(2)}) async-start(), calls=%async_computation.5 | async-start | bytes 8912896 | tf_op jit(solution)/shard_map/reduce_scatter | solution.py:691
  144.3 81.8 %collective-permute-start = (bf16[320,1024]{1,0:T(8,128)(2,1)S(1)}, bf16[320,1024]{1,0:T(8,128)(2,1)}, u32[]{:S(2)}, u32[]{:S(2)}) collective-permute-start(bf16[320,1024]{1,0:T(8,128)(2,1)S(1)} %copy-done.33), channel_id=1, source_target_pairs={{0,1},{1,0},{2,3},{3,2},{4,5},{5,4},{6,7},{7,6},{8,9},{9,8},{10,11... | collective-permute-start | bytes 1966088 | tf_op jit(solution)/shard_map/ppermute | solution.py:720
  147.6 9.2 %copy-start.15 = (bf16[16,32,1024]{2,1,0:T(8,128)(2,1)}, bf16[16,32,1024]{2,1,0:T(8,128)(2,1)S(1)}, u32[]{:S(2)}) copy-start(bf16[16,32,1024]{2,1,0:T(8,128)(2,1)S(1)} %copy.42) | copy-start | bytes 3145732
  149.8 14.9 %copy-start.38 = (bf16[320,1024]{1,0:T(8,128)(2,1)}, bf16[320,1024]{1,0:T(8,128)(2,1)S(1)}, u32[]{:S(2)}) copy-start(bf16[320,1024]{1,0:T(8,128)(2,1)S(1)} %get-tuple-element.94) | copy-start | bytes 1966084
  149.8 14.9 %copy-start.40 = (bf16[320,1024]{1,0:T(8,128)(2,1)}, bf16[320,1024]{1,0:T(8,128)(2,1)S(1)}, u32[]{:S(2)}) copy-start(bf16[320,1024]{1,0:T(8,128)(2,1)S(1)} %get-tuple-element.95) | copy-start | bytes 1966084
  151.7 7.7 %copy-start.43 = (bf16[960,1024]{1,0:T(8,128)(2,1)}, bf16[960,1024]{1,0:T(8,128)(2,1)S(1)}, u32[]{:S(2)}) copy-start(bf16[960,1024]{1,0:T(8,128)(2,1)S(1)} %constant_dynamic-update-slice_fusion) | copy-start | bytes 5898244
  177.1 37.7 %copy-start.44 = (bf16[960,1024]{1,0:T(8,128)(2,1)S(1)}, bf16[960,1024]{1,0:T(8,128)(2,1)}, u32[]{:S(2)}) copy-start(bf16[960,1024]{1,0:T(8,128)(2,1)} %copy-done.43) | copy-start | bytes 5898244
  219.4 38.8 %copy-start.9 = (f32[960,1024]{1,0:T(8,128)}, f32[960,1024]{1,0:T(8,128)S(1)}, u32[]{:S(2)}) copy-start(f32[960,1024]{1,0:T(8,128)S(1)} %get-tuple-element.117) | copy-start | bytes 11796484
  219.5 38.8 %copy-start.49 = (f32[960]{0:T(1024)}, f32[960]{0:T(1024)S(1)}, u32[]{:S(2)}) copy-start(f32[960]{0:T(1024)S(1)} %broadcast_multiply_fusion.8) | copy-start | bytes 11524
  220.2 38.0 %copy-start.55 = (f32[960]{0:T(1024)}, f32[960]{0:T(1024)S(1)}, u32[]{:S(2)}) copy-start(f32[960]{0:T(1024)S(1)} %add_rsqrt_fusion.2) | copy-start | bytes 11524
  220.2 38.0 %copy-start.53 = (f32[1,1024]{1,0:T(1,128)}, f32[1,1024]{1,0:T(1,128)S(1)}, u32[]{:S(2)}) copy-start(f32[1,1024]{1,0:T(1,128)S(1)} %get-tuple-element.110) | copy-start | bytes 12292
  220.3 38.0 %copy-start.62 = (f32[1,1024]{1,0:T(1,128)}, f32[1,1024]{1,0:T(1,128)S(1)}, u32[]{:S(2)}) copy-start(f32[1,1024]{1,0:T(1,128)S(1)} %get-tuple-element.109) | copy-start | bytes 12292
  227.3 7.4 copy-start.34
  227.3 7.4 copy-start.36
  306.1 6.6 copy-start
  309.0 9.1 %slice-start.2 = ((s8[7864320]{0:T(1024)(128)(4,1)}), s8[4194304]{0:T(1024)(128)(4,1)S(1)}, s32[]{:S(2)}) async-start(s8[7864320]{0:T(1024)(128)(4,1)} %bitcast.122), calls=%async_computation.12 | async-start | bytes 8388608
  329.6 226.3 %reduce-scatter.9.cloned.1.call-start = ((), (), s32[]{:S(2)}) async-start(), calls=%async_computation.7 | async-start | bytes 8912896 | tf_op jit(solution)/shard_map/reduce_scatter | solution.py:691
  329.7 15.1 %copy-start.6 = (f32[960,1024]{1,0:T(8,128)S(1)}, f32[960,1024]{1,0:T(8,128)}, u32[]{:S(2)}) copy-start(f32[960,1024]{1,0:T(8,128)} %copy-done.5) | copy-start | bytes 11796484
  360.5 209.6 %reduce-scatter.7.cloned.1.call-start = ((), (), s32[]{:S(2)}) async-start(), calls=%async_computation.6 | async-start | bytes 786432 | tf_op jit(solution)/shard_map/reduce_scatter | solution.py:692
  360.6 19.1 %copy-start.7 = (f32[960,1024]{1,0:T(8,128)S(1)}, f32[960,1024]{1,0:T(8,128)}, u32[]{:S(2)}) copy-start(f32[960,1024]{1,0:T(8,128)} %copy-done.5) | copy-start | bytes 11796484
  382.8 50.8 %copy-start.18 = (f32[960,1024]{1,0:T(8,128)}, f32[960,1024]{1,0:T(8,128)S(1)}, u32[]{:S(2)}) copy-start(f32[960,1024]{1,0:T(8,128)S(1)} %get-tuple-element.79) | copy-start | bytes 11796484
  432.2 122.7 %collective-permute-start.2 = (bf16[320,1024]{1,0:T(8,128)(2,1)S(1)}, bf16[320,1024]{1,0:T(8,128)(2,1)S(1)}, u32[]{:S(2)}, u32[]{:S(2)}) collective-permute-start(bf16[320,1024]{1,0:T(8,128)(2,1)S(1)} %dynamic-slice_convert_fusion), channel_id=1, source_target_pairs={{0,1},{1,0},{2,3},{3,2},{4,5},{5,4},{6,7},{7,6},{8,9},{9,8},{10,11... | collective-permute-start | bytes 1966088 | tf_op jit(solution)/shard_map/ppermute | solution.py:720
  439.9 6.5 copy-start.2
  446.5 70.0 %copy-start.31 = (bf16[640,1024]{1,0:T(8,128)(2,1)S(1)}, bf16[640,1024]{1,0:T(8,128)(2,1)}, u32[]{:S(2)}) copy-start(bf16[640,1024]{1,0:T(8,128)(2,1)} %get-tuple-element.52) | copy-start | bytes 3932164
  540.1 6.4 copy-start.13
  546.5 58.9 %reduce-scatter.11.cloned.1.call-start = ((), (), s32[]{:S(2)}) async-start(), calls=%async_computation.8 | async-start | bytes 786432 | tf_op jit(solution)/shard_map/reduce_scatter | solution.py:692
  549.3 20.8 %copy-start.12 = (f32[960,512]{1,0:T(8,128)S(1)}, f32[960,512]{1,0:T(8,128)}, u32[]{:S(2)}) copy-start(f32[960,512]{1,0:T(8,128)} %get-tuple-element.48) | copy-start | bytes 5898244
  555.9 180.9 %all-reduce.5.cloned.1.call-start = ((), (), s32[]{:S(2)}) async-start(), calls=%async_computation.9 | async-start | bytes 147456 | tf_op jit(solution)/shard_map/psum | solution.py:1452
  579.4 166.2 %collective-permute-start.1 = (bf16[320,1024]{1,0:T(8,128)(2,1)}, bf16[320,1024]{1,0:T(8,128)(2,1)}, u32[]{:S(2)}, u32[]{:S(2)}) collective-permute-start(bf16[320,1024]{1,0:T(8,128)(2,1)} %dynamic-slice_convert_fusion.1), channel_id=1, source_target_pairs={{0,1},{1,0},{2,3},{3,2},{4,5},{5,4},{6,7},{7,6},{8,9},{9,8},{10,11... | collective-permute-start | bytes 1966088 | tf_op jit(solution)/shard_map/ppermute | solution.py:720
  593.3 6.6 copy-start.48
  593.3 6.6 copy-start.8
  600.0 14.1 %copy-start.22 = (f32[128,1024]{1,0:T(8,128)S(1)}, f32[128,1024]{1,0:T(8,128)}, u32[]{:S(2)}) copy-start(f32[128,1024]{1,0:T(8,128)} %param.30) | copy-start | bytes 1572868
  600.0 14.1 %copy-start.42 = (bf16[128,1024]{1,0:T(8,128)(2,1)S(1)}, bf16[128,1024]{1,0:T(8,128)(2,1)}, u32[]{:S(2)}) copy-start(bf16[128,1024]{1,0:T(8,128)(2,1)} %reduce-scatter.7.cloned.1.call-done) | copy-start | bytes 786436
  605.4 11.3 %collective-permute-start.3 = (bf16[128,1024]{1,0:T(8,128)(2,1)}, bf16[128,1024]{1,0:T(8,128)(2,1)S(1)}, u32[]{:S(2)}, u32[]{:S(2)}) collective-permute-start(bf16[128,1024]{1,0:T(8,128)(2,1)} %reduce-scatter.11.cloned.1.call-done), channel_id=1, source_target_pairs={{7,24},{10,25},{13,26},{16,27},{19,28},{22,29},{25,30},{28,31}} | collective-permute-start | bytes 786440 | tf_op jit(solution)/shard_map/ppermute | solution.py:707
  606.1 19.2 %collective-permute-start.4 = (bf16[128,1024]{1,0:T(8,128)(2,1)}, bf16[128,1024]{1,0:T(8,128)(2,1)S(1)}, u32[]{:S(2)}, u32[]{:S(2)}) collective-permute-start(bf16[128,1024]{1,0:T(8,128)(2,1)} %reduce-scatter.11.cloned.1.call-done), channel_id=1, source_target_pairs={{8,24},{11,25},{14,26},{17,27},{20,28},{23,29},{26,30},{29,31}} | collective-permute-start | bytes 786440 | tf_op jit(solution)/shard_map/ppermute | solution.py:707
  612.7 13.3 %collective-permute-start.5 = (bf16[128,1024]{1,0:T(8,128)(2,1)}, bf16[128,1024]{1,0:T(8,128)(2,1)S(1)}, u32[]{:S(2)}, u32[]{:S(2)}) collective-permute-start(bf16[128,1024]{1,0:T(8,128)(2,1)} %reduce-scatter.11.cloned.1.call-done), channel_id=1, source_target_pairs={{9,24},{12,25},{15,26},{18,27},{21,28},{24,29},{27,30},{30,31}} | collective-permute-start | bytes 786440 | tf_op jit(solution)/shard_map/ppermute | solution.py:707
  613.3 13.3 %collective-permute-start.6 = (bf16[128,1024]{1,0:T(8,128)(2,1)}, bf16[128,1024]{1,0:T(8,128)(2,1)S(1)}, u32[]{:S(2)}, u32[]{:S(2)}) collective-permute-start(bf16[128,1024]{1,0:T(8,128)(2,1)} %reduce-scatter.11.cloned.1.call-done), channel_id=1, source_target_pairs={{10,24},{13,25},{16,26},{19,27},{22,28},{25,29},{28,30},{31,31}} | collective-permute-start | bytes 786440 | tf_op jit(solution)/shard_map/ppermute | solution.py:707
  616.7 11.5 %collective-permute-start.7 = (bf16[128,1024]{1,0:T(8,128)(2,1)}, bf16[128,1024]{1,0:T(8,128)(2,1)S(1)}, u32[]{:S(2)}, u32[]{:S(2)}) collective-permute-start(bf16[128,1024]{1,0:T(8,128)(2,1)} %reduce-scatter.11.cloned.1.call-done), channel_id=1, source_target_pairs={{11,24},{14,25},{17,26},{20,27},{23,28},{26,29},{29,30}} | collective-permute-start | bytes 786440 | tf_op jit(solution)/shard_map/ppermute | solution.py:707
  628.9 108.9 %copy-start.47 = (f32[7,1024]{1,0:T(8,128)S(1)}, f32[7,1024]{1,0:T(8,128)}, u32[]{:S(2)}) copy-start(f32[7,1024]{1,0:T(8,128)} %param.33) | copy-start | bytes 86020
  628.9 108.9 %copy-start.51 = (f32[7,1024]{1,0:T(8,128)S(1)}, f32[7,1024]{1,0:T(8,128)}, u32[]{:S(2)}) copy-start(f32[7,1024]{1,0:T(8,128)} %param.34) | copy-start | bytes 86020
  628.9 108.9 %copy-start.52 = (f32[7,1024]{1,0:T(8,128)S(1)}, f32[7,1024]{1,0:T(8,128)}, u32[]{:S(2)}) copy-start(f32[7,1024]{1,0:T(8,128)} %param.35) | copy-start | bytes 86020
  628.9 109.6 %copy-start.61 = (f32[336]{0:T(512)S(1)}, f32[336]{0:T(512)}, u32[]{:S(2)}) copy-start(f32[336]{0:T(512)} %param.27) | copy-start | bytes 4036
  628.9 109.6 %copy-start.64 = (f32[336]{0:T(512)S(1)}, f32[336]{0:T(512)}, u32[]{:S(2)}) copy-start(f32[336]{0:T(512)} %param.28) | copy-start | bytes 4036
  628.9 109.6 %copy-start.65 = (f32[336]{0:T(512)S(1)}, f32[336]{0:T(512)}, u32[]{:S(2)}) copy-start(f32[336]{0:T(512)} %param.29) | copy-start | bytes 4036
  (40 other events, 148.2 us)
Sparse Core Ops, SparseCore 0:
  144.4 87.4 all-gather.1
  329.7 112.6 reduce-scatter.4
  446.5 104.4 reduce-scatter.8
  553.0 17.0 reduce-scatter.6
  572.3 17.9 reduce-scatter.10
  605.5 127.5 all-reduce.4
